TPU v7x, 32 devices: a whole 2x2x4 slice. The times are simulated.
32 devices in a mesh: dom: 2 (over y), freq: 4 (over z), win: 2 (over x), rep: 2 (over core).
Axes of the slice: x: 2, y: 2, z: 4, core: 2. Of those that a mesh axis runs over, the one named last changes fastest.
Arguments:
- recorded: float32 [2, 128, 4, 1024], P(None, 'freq', ('dom', 'win'), 'rep'), parts along dimension 2, may hold values from -8 to 8
- geometry: float32 [2, 4, 1024], P(None, ('dom', 'win'), 'rep'), parts along dimension 1, may hold values from -1 to 1
- present: int32 [4, 1024], P(('dom', 'win'), 'rep'), parts along dimension 0, may hold values 0 or 1
- intersection_index: int32 [4, 2, 128], P(('dom', 'win'), 'rep'), parts along dimension 0, may hold values from 0 to 127, each once within a row
- pattern: int32 [128, 8, 8], P('freq', None, 'rep'), may hold values from 0 to 1
- group_scale: float32 [512], replicated, may hold values from 0.05 to 1.5
Outputs:
- coefficients: float32 [2, 128, 4, 512], P(None, 'freq', ('dom', 'win')), parts along dimension 2
- reconstruction: float32 [2, 128, 4, 1024], P(None, 'freq', ('dom', 'win'), 'rep'), parts along dimension 2
There are 2 independent parts, one for each index of `dom`. A program takes and returns all parts, laid end to end along the dimension named above; an argument that names none is the same for every part. Nothing has to cross between parts.
Inputs may be any that keep to these rules, and one draw needn't show every extreme that they name: Each row intersection_index[w, r] is an ordering of 0 to 127: leading trace j of strip r of window w is the same point as trailing trace intersection_index[w, r, j] of strip r of window w - 1.
All inputs are finite; a program needn't handle non-finite values. No bound on the sum of `present` on one device may be relied on, other than what follows from the above.
Results may differ from a plain program's by a relative error of at most 0.0051.
Values may be sent and summed in bfloat16 or wider, within the bound.
No kernel may reach another device: no remote copies, remote signals or barrier semaphores. Data moves between devices by JAX's collectives and lax.ppermute only.
A program may use at most 64 MiB of HBM per device.

v0:
```python
import math

import jax
import jax.numpy as jnp
from jax import lax
from jax.sharding import PartitionSpec as P

PX = 16
PY = 32
SPB = 64
OBS = 128
ITERS = 3


wave_scale = 32.0
step_length = 1.0
epsilon = 1e-06


def extended(x, sides, width):
    for axis, dim in sides:
        size, length = (lax.axis_size(axis), x.shape[dim])
        up = [(i, (i + 1) % size) for i in range(size - 1)]
        down = [(j, i) for i, j in up]
        last = lax.slice_in_dim(x, length - width, length, axis=dim)
        leading = lax.slice_in_dim(x, 0, width, axis=dim)
        before = lax.ppermute(last, axis, up)
        after = lax.ppermute(leading, axis, down)
        x = jnp.concatenate([before, x, after], axis=dim)
    return x


def build_tables(angular_block, pattern_block, geometry, amplitude):
    inline_offset = geometry[0, 0]
    cross_offset = geometry[1, 0]
    inline_slow = (jnp.arange(PX, dtype=jnp.float32) + 0.5) * (2.0 / PX) - 1.0
    cross_slow = (jnp.arange(PY, dtype=jnp.float32) + 0.5) * (2.0 / PY) - 1.0
    phase_inline = (
        angular_block[:, None, None] * inline_offset[None, :, None] * inline_slow[None, None, :]
    )
    phase_cross = (
        angular_block[:, None, None] * cross_offset[None, :, None] * cross_slow[None, None, :]
    )
    active = jnp.repeat(
        jnp.repeat(pattern_block.astype(jnp.float32), SPB // PY, axis=1), OBS, axis=2
    )
    weight = jnp.transpose(active, (0, 2, 1)) * amplitude
    inline_table = jnp.concatenate(
        [jnp.cos(phase_inline) * weight, -(jnp.sin(phase_inline) * weight)], axis=2
    ).astype(jnp.bfloat16)
    cross_table = jnp.concatenate([jnp.cos(phase_cross), -jnp.sin(phase_cross)], axis=2).astype(
        jnp.bfloat16
    )
    return (inline_table, cross_table)


def predict(coeffs, angular, pattern, geometry, amplitude, block_len):
    frequencies = coeffs.shape[1]
    blocks = frequencies // block_len
    rounded = coeffs.astype(jnp.bfloat16).reshape(2, frequencies, PX, PY)
    real_turned = jnp.transpose(rounded[0], (0, 2, 1))
    imag_turned = jnp.transpose(rounded[1], (0, 2, 1))
    mixing = jnp.concatenate(
        [
            jnp.concatenate([real_turned, imag_turned], axis=2),
            jnp.concatenate([-imag_turned, real_turned], axis=2),
        ],
        axis=1,
    )

    def predict_one_block(inputs):
        angular_block, pattern_block, mixing_block = inputs
        inline_table, cross_table = build_tables(angular_block, pattern_block, geometry, amplitude)
        partial_sums = jnp.einsum(
            "fxk,fkc->fxc", cross_table, mixing_block, preferred_element_type=jnp.float32
        )
        inline_wide = inline_table.astype(jnp.float32)
        inline_real = inline_wide[:, :, :PX]
        inline_imag = inline_wide[:, :, PX:]
        part_real = partial_sums[:, :, :PX]
        part_imag = partial_sums[:, :, PX:]
        out_real = jnp.sum(inline_real * part_real - inline_imag * part_imag, axis=2)
        out_imag = jnp.sum(inline_real * part_imag + inline_imag * part_real, axis=2)
        return jnp.stack([out_real, out_imag])

    result = lax.map(
        predict_one_block,
        (
            angular.reshape(blocks, block_len),
            pattern.reshape((blocks, block_len) + pattern.shape[1:]),
            mixing.reshape(blocks, block_len, 2 * PY, 2 * PX),
        ),
    )
    return jnp.transpose(result, (1, 0, 2, 3)).reshape(2, frequencies, result.shape[3])


def back_project(residual, angular, pattern, geometry, amplitude, block_len):
    frequencies = residual.shape[1]
    traces = residual.shape[2]
    blocks = frequencies // block_len

    def back_one_block(inputs):
        angular_block, pattern_block, real_block, imag_block = inputs
        inline_table, cross_table = build_tables(angular_block, pattern_block, geometry, amplitude)
        inline_wide = inline_table.astype(jnp.float32)
        inline_real = inline_wide[:, :, :PX]
        inline_imag = inline_wide[:, :, PX:]
        res_real = real_block[:, :, None]
        res_imag = imag_block[:, :, None]
        hidden_real = inline_real * res_real + inline_imag * res_imag
        hidden_imag = inline_real * res_imag - inline_imag * res_real
        weighted = jnp.concatenate([hidden_real, hidden_imag], axis=2).astype(jnp.bfloat16)
        products = jnp.einsum(
            "fxk,fxc->fkc", cross_table, weighted, preferred_element_type=jnp.float32
        )
        grad_real = products[:, :PY, :PX] + products[:, PY:, PX:]
        grad_imag = products[:, :PY, PX:] - products[:, PY:, :PX]
        stacked = jnp.transpose(jnp.stack([grad_real, grad_imag]), (0, 1, 3, 2))
        return stacked.reshape(2, block_len, PX * PY)

    result = lax.map(
        back_one_block,
        (
            angular.reshape(blocks, block_len),
            pattern.reshape((blocks, block_len) + pattern.shape[1:]),
            residual[0].reshape(blocks, block_len, traces),
            residual[1].reshape(blocks, block_len, traces),
        ),
    )
    return jnp.transpose(result, (1, 0, 2, 3)).reshape(2, frequencies, PX * PY)


def blend_edges(predicted, intersection_index):
    highest = lax.Precision.HIGHEST
    traces = predicted.shape[2]
    pairing = intersection_index[0, 0]
    intersection = pairing.shape[0]
    positions = jnp.arange(intersection, dtype=jnp.int32)
    permute = (pairing[:, None] == positions[None, :]).astype(jnp.float32)
    leading = predicted[:, :, :intersection]
    trailing = predicted[:, :, traces - intersection :]
    leading_moved = jnp.einsum("cfj,jk->cfk", leading, permute, precision=highest)
    edge_values = jnp.concatenate([leading_moved, trailing], axis=2)
    padded = extended(edge_values, (("win", 2),), intersection)
    from_lower = jnp.einsum("cfk,jk->cfj", padded[:, :, :intersection], permute, precision=highest)
    from_upper = padded[:, :, 3 * intersection :]
    ramp_own = (positions.astype(jnp.float32) + 0.5) / intersection
    ramp_lead = (pairing.astype(jnp.float32) + 0.5) / intersection
    window_index = lax.axis_index("win")
    window_count = lax.axis_size("win")
    new_lead = jnp.where(
        window_index > 0, (1.0 - ramp_lead) * from_lower + ramp_lead * leading, leading
    )
    new_trail = jnp.where(
        window_index < window_count - 1,
        (1.0 - ramp_own) * trailing + ramp_own * from_upper,
        trailing,
    )
    return jnp.concatenate(
        [new_lead, predicted[:, :, intersection : traces - intersection], new_trail], axis=2
    )


def shrink_partial(values, thresholds, nfreq):
    energy = jnp.sum(values * values, axis=(0, 1))
    total = lax.psum(energy, "freq")
    factor = jnp.maximum(0.0, 1.0 - thresholds / jnp.sqrt(total / nfreq + epsilon))
    return values * factor


def per_device(recorded, geometry, present, intersection_index, pattern, group_scale):
    frequencies = recorded.shape[1]
    traces = recorded.shape[3]
    nfreq = frequencies * lax.axis_size("freq")
    amplitude = 1.0 / math.sqrt(traces * lax.axis_size("rep"))
    first_freq = lax.axis_index("freq") * frequencies
    levels = (first_freq + jnp.arange(frequencies, dtype=jnp.int32)).astype(jnp.float32)
    angular = math.pi * wave_scale * (0.25 + 0.75 * (levels + 0.5) / nfreq)
    block_len = math.gcd(frequencies, 4)
    observed = recorded[:, :, 0, :]
    weight_mask = present[0].astype(jnp.float32)
    slowness = group_scale.shape[0]
    half_len = slowness // 2
    thresholds = lax.dynamic_slice_in_dim(group_scale, lax.axis_index("rep") * half_len, half_len)
    current = jnp.zeros((2, frequencies, thresholds.shape[0]), jnp.float32)
    complete = current
    for iteration in range(ITERS):
        if iteration == 0:
            residual = -(weight_mask * observed)
        else:
            blended = blend_edges(
                predict(complete, angular, pattern, geometry, amplitude, block_len),
                intersection_index,
            )
            residual = weight_mask * (blended - observed)
        partial_grad = back_project(residual, angular, pattern, geometry, amplitude, block_len)
        summed = lax.psum_scatter(partial_grad, "rep", scatter_dimension=2, tiled=True)
        updated = current - step_length * summed
        current = shrink_partial(updated, thresholds, nfreq)
        if iteration + 1 < ITERS:
            complete = lax.all_gather(current.astype(jnp.bfloat16), "rep", axis=2, tiled=True)
        else:
            complete = lax.all_gather(current, "rep", axis=2, tiled=True)
    reconstruction = blend_edges(
        predict(complete, angular, pattern, geometry, amplitude, block_len), intersection_index
    )
    return (complete[:, :, None, :], reconstruction[:, :, None, :])


def solution(mesh):
    return jax.shard_map(
        per_device,
        mesh=mesh,
        in_specs=(
            P(None, "freq", ("dom", "win"), "rep"),
            P(None, ("dom", "win"), "rep"),
            P(("dom", "win"), "rep"),
            P(("dom", "win"), "rep", None),
            P("freq", None, "rep"),
            P(),
        ),
        out_specs=(P(None, "freq", ("dom", "win"), None), P(None, "freq", ("dom", "win"), "rep")),
        check_vma=False,
    )
```

profile of v0, /device:TPU:0, one launch (start us, length us, event | category | flops | bytes accessed | tf_op | source)
XLA Modules:
  0.0 242.2 jit_solution(15074002826373603853)
XLA Ops:
  10.3 21.2 %while.78 = (s32[]{:T(128)}, f32[8,2,4,512]{3,2,1,0:T(4,128)S(1)}, f32[8,4]{1,0:T(8,128)S(1)}, f32[2,1,512]{2,1,0:T(1,128)S(1)}, s32[8,4,8,4]{2,3,1,0:T(4,128)S(...) while((s32[]{:T(128)}, f32[8,2,4,512]{3,2,1,0:T(4,128)S(1)}, f32[8,4]{1,0:T(8,128)S(1)}, ...), condition=%wide.region_1.2_spmd, body=%wide.region_0.1_spmd.sunk | while | flops 10170770 | bytes 2376725 | solution.py:121
  14.0 1.1 fusion.210
  16.7 1.1 fusion.210
  22.0 1.1 fusion.210
  27.3 1.1 fusion.210
  29.9 1.1 fusion.210
  32.3 10.3 %reduce-scatter.4.cloned.1.call-done = f32[2,32,256]{2,1,0:T(8,128)} async-done(((f32[2,32,512]{2,1,0:T(8,128)}), f32[2,32,256]{2,1,0:T(8,128)}) %reduce-scatter.4.cloned.1.call-update) | async-done | bytes 65552 | tf_op jit(solution)/shard_map/reduce_scatter | solution.py:197
  43.5 12.0 %psum.21 = f32[256]{0:T(256)S(1)} all-reduce(f32[256]{0:T(256)S(1)} %multiply_reduce_fusion.2), channel_id=1, replica_groups=mesh['dom'=2,'freq'=4,'win'=2,'rep'=2] {'freq'}, use_global_device_ids=true, to_apply=%region_4.5 | all-reduce | flops 256 | bytes 2048 | tf_op jit(solution)/shard_map/psum | solution.py:166
  55.6 1.9 all_gather.9
  57.9 19.6 %while.79 = (s32[]{:T(128)}, f32[8,2,4,512]{3,2,1,0:T(4,128)S(1)}, f32[8,4]{1,0:T(8,128)S(1)}, f32[2,1,512]{2,1,0:T(1,128)S(1)}, s32[8,4,8,4]{2,3,1,0:T(4,128)S(...) while((s32[]{:T(128)}, f32[8,2,4,512]{3,2,1,0:T(4,128)S(1)}, f32[8,4]{1,0:T(8,128)S(1)}, ...), condition=%wide.region_8.9_spmd, body=%wide.region_5.8_spmd.sunk | while | flops 9900434 | bytes 2491405 | solution.py:86
  61.4 1.1 fusion.218
  66.3 1.1 fusion.218
  68.8 1.1 fusion.218
  73.7 1.1 fusion.218
  78.5 1.3 collective-permute-start.1
  79.8 4.5 %collective-permute-done.1 = f32[2,32,128]{2,1,0:T(8,128)S(1)} collective-permute-done((f32[2,32,128]{2,1,0:T(8,128)S(1)}, f32[2,32,128]{2,1,0:T(8,128)S(1)}, u32[]{:S(2)}, u32[]{:S(2)}) %collective-permute-start.1) | collective-permute-done | bytes 32800 | tf_op jit(solution)/shard_map/ppermute | solution.py:28
  84.3 1.7 collective-permute-start
  86.1 1.5 collective-permute-done
  88.1 21.3 %while.80 = (s32[]{:T(128)}, f32[8,2,4,512]{3,2,1,0:T(4,128)S(1)}, f32[8,4]{1,0:T(8,128)S(1)}, f32[2,1,512]{2,1,0:T(1,128)S(1)}, s32[8,4,8,4]{2,3,1,0:T(4,128)S(...) while((s32[]{:T(128)}, f32[8,2,4,512]{3,2,1,0:T(4,128)S(1)}, ...), condition=%wide.region_10.11_spmd, body=%wide.region_9.10_spmd.sunk | while | flops 10170770 | bytes 2376725 | solution.py:121
  89.2 1.1 fusion.226
  94.5 1.1 fusion.226
  97.2 1.1 fusion.226
  99.8 1.1 fusion.226
  102.5 1.1 fusion.226
  107.8 1.1 fusion.226
  110.2 6.6 %reduce-scatter.6.cloned.1.call-done = f32[2,32,256]{2,1,0:T(8,128)} async-done(((f32[2,32,512]{2,1,0:T(8,128)}), f32[2,32,256]{2,1,0:T(8,128)}) %reduce-scatter.6.cloned.1.call-update) | async-done | bytes 65552 | tf_op jit(solution)/shard_map/reduce_scatter | solution.py:197
  117.6 11.9 %psum.22 = f32[256]{0:T(256)S(1)} all-reduce(f32[256]{0:T(256)S(1)} %get-tuple-element.706), channel_id=1, replica_groups=mesh['dom'=2,'freq'=4,'win'=2,'rep'=2] {'freq'}, use_global_device_ids=true, to_apply=%region_13.14 | all-reduce | flops 256 | bytes 2048 | tf_op jit(solution)/shard_map/psum | solution.py:166
  129.6 1.9 all_gather.10
  132.0 19.6 %while.81 = (s32[]{:T(128)}, f32[8,2,4,512]{3,2,1,0:T(4,128)S(1)}, f32[8,4]{1,0:T(8,128)S(1)}, f32[2,1,512]{2,1,0:T(1,128)S(1)}, s32[8,4,8,4]{2,3,1,0:T(4,128)S(...) while((s32[]{:T(128)}, f32[8,2,4,512]{3,2,1,0:T(4,128)S(1)}, f32[8,4]{1,0:T(8,128)S(1)}, ...), condition=%wide.region_17.18_spmd, body=%wide.region_14.17_spmd.sunk | while | flops 9900434 | bytes 2491405 | solution.py:86
  133.0 1.1 fusion.234
  137.9 1.1 fusion.234
  140.4 1.1 fusion.234
  145.3 1.1 fusion.234
  147.7 1.1 fusion.234
  150.2 1.1 fusion.234
  151.9 1.3 collective-permute-start.3
  153.2 4.5 %collective-permute-done.3 = f32[2,32,128]{2,1,0:T(8,128)S(1)} collective-permute-done((f32[2,32,128]{2,1,0:T(8,128)S(1)}, f32[2,32,128]{2,1,0:T(8,128)S(1)}, u32[]{:S(2)}, u32[]{:S(2)}) %collective-permute-start.3) | collective-permute-done | bytes 32800 | tf_op jit(solution)/shard_map/ppermute | solution.py:28
  157.7 1.6 collective-permute-start.2
  159.4 1.6 collective-permute-done.2
  161.3 21.3 %while.82 = (s32[]{:T(128)}, f32[8,2,4,512]{3,2,1,0:T(4,128)S(1)}, f32[8,4]{1,0:T(8,128)S(1)}, f32[2,1,512]{2,1,0:T(1,128)S(1)}, s32[8,4,8,4]{2,3,1,0:T(4,128)S(...) while((s32[]{:T(128)}, f32[8,2,4,512]{3,2,1,0:T(4,128)S(1)}, ...), condition=%wide.region_19.20_spmd, body=%wide.region_18.19_spmd.sunk | while | flops 10170770 | bytes 2376725 | solution.py:121
  165.1 1.1 fusion.242
  183.3 6.7 %reduce-scatter.8.cloned.1.call-done = f32[2,32,256]{2,1,0:T(8,128)} async-done(((f32[2,32,512]{2,1,0:T(8,128)}), f32[2,32,256]{2,1,0:T(8,128)}) %reduce-scatter.8.cloned.1.call-update) | async-done | bytes 65552 | tf_op jit(solution)/shard_map/reduce_scatter | solution.py:197
  191.0 11.9 %psum.23 = f32[256]{0:T(256)S(1)} all-reduce(f32[256]{0:T(256)S(1)} %multiply_reduce_fusion), channel_id=1, replica_groups=mesh['dom'=2,'freq'=4,'win'=2,'rep'=2] {'freq'}, use_global_device_ids=true, to_apply=%region_22.23 | all-reduce | flops 256 | bytes 2048 | tf_op jit(solution)/shard_map/psum | solution.py:166
  203.0 2.1 all_gather.11
  205.6 19.6 %while.83 = (s32[]{:T(128)}, f32[8,2,4,512]{3,2,1,0:T(4,128)S(1)}, f32[8,4]{1,0:T(8,128)S(1)}, f32[2,1,512]{2,1,0:T(1,128)S(1)}, s32[8,4,8,4]{2,3,1,0:T(4,128)S(...) while((s32[]{:T(128)}, f32[8,2,4,512]{3,2,1,0:T(4,128)S(1)}, f32[8,4]{1,0:T(8,128)S(1)}, ...), condition=%wide.region_26.27_spmd, body=%wide.region_23.26_spmd.sunk | while | flops 9900434 | bytes 2491405 | solution.py:86
  225.5 1.3 collective-permute-start.5
  226.8 4.5 %collective-permute-done.5 = f32[2,32,128]{2,1,0:T(8,128)S(1)} collective-permute-done((f32[2,32,128]{2,1,0:T(8,128)S(1)}, f32[2,32,128]{2,1,0:T(8,128)S(1)}, u32[]{:S(2)}, u32[]{:S(2)}) %collective-permute-start.5) | collective-permute-done | bytes 32800 | tf_op jit(solution)/shard_map/ppermute | solution.py:28
  231.3 1.6 collective-permute-start.4
  (940 shorter events, 107.7 us)
Async XLA Ops:
  7.2 0.7 copy-start.5
  7.2 35.4 %reduce-scatter.4.cloned.1.call-start = ((), (), s32[]{:S(2)}) async-start(), calls=%async_computation.3 | async-start | bytes 196608 | tf_op jit(solution)/shard_map/reduce_scatter | solution.py:197
  7.9 0.7 copy-start.7
  9.6 0.7 copy-start
  32.2 84.5 %reduce-scatter.6.cloned.1.call-start = ((), (), s32[]{:S(2)}) async-start(), calls=%async_computation.4 | async-start | bytes 196608 | tf_op jit(solution)/shard_map/reduce_scatter | solution.py:197
  42.6 13.0 %copy-start.2 = (f32[2,32,256]{2,1,0:T(8,128)S(1)}, f32[2,32,256]{2,1,0:T(8,128)}, u32[]{:S(2)}) copy-start(f32[2,32,256]{2,1,0:T(8,128)} %reduce-scatter.4.cloned.1.call-done) | copy-start | bytes 196612
  43.5 12.0 %copy-start.6 = (f32[512]{0:T(512)S(1)}, f32[512]{0:T(512)}, u32[]{:S(2)}) copy-start(f32[512]{0:T(512)} %param.23) | copy-start | bytes 6148
  77.6 0.7 copy-start.4
  78.5 5.8 %collective-permute-start.1 = (f32[2,32,128]{2,1,0:T(8,128)S(1)}, f32[2,32,128]{2,1,0:T(8,128)S(1)}, u32[]{:S(2)}, u32[]{:S(2)}) collective-permute-start(f32[2,32,128]{2,1,0:T(8,128)S(1)} %fusion.127), channel_id=1, source_target_pairs={{2,0},{3,1},{6,4},{7,5},{10,8},{11,9},{14,12},{15,13},{18,16},{19,... | collective-permute-start | bytes 98312 | tf_op jit(solution)/shard_map/ppermute | solution.py:28
  84.3 3.6 %copy-start.1 = (f32[2,32,1,512]{3,2,1,0:T(1,128)S(1)}, f32[2,32,1,512]{3,2,1,0:T(1,128)}, u32[]{:S(2)}) copy-start(f32[2,32,1,512]{3,2,1,0:T(1,128)} %param.18) | copy-start | bytes 393220
  84.3 3.3 %collective-permute-start = (f32[2,32,128]{2,1,0:T(8,128)S(1)}, f32[2,32,128]{2,1,0:T(8,128)S(1)}, u32[]{:S(2)}, u32[]{:S(2)}) collective-permute-start(f32[2,32,128]{2,1,0:T(8,128)S(1)} %get-tuple-element.782), channel_id=1, source_target_pairs={{0,2},{1,3},{4,6},{5,7},{8,10},{9,11},{12,14},{13,15},{16,18},{17,... | collective-permute-start | bytes 98312 | tf_op jit(solution)/shard_map/ppermute | solution.py:27
  110.1 79.9 %reduce-scatter.8.cloned.1.call-start = ((), (), s32[]{:S(2)}) async-start(), calls=%async_computation.5 | async-start | bytes 196608 | tf_op jit(solution)/shard_map/reduce_scatter | solution.py:197
  151.9 5.8 %collective-permute-start.3 = (f32[2,32,128]{2,1,0:T(8,128)S(1)}, f32[2,32,128]{2,1,0:T(8,128)S(1)}, u32[]{:S(2)}, u32[]{:S(2)}) collective-permute-start(f32[2,32,128]{2,1,0:T(8,128)S(1)} %fusion.124), channel_id=1, source_target_pairs={{2,0},{3,1},{6,4},{7,5},{10,8},{11,9},{14,12},{15,13},{18,16},{19,... | collective-permute-start | bytes 98312 | tf_op jit(solution)/shard_map/ppermute | solution.py:28
  157.7 3.2 %collective-permute-start.2 = (f32[2,32,128]{2,1,0:T(8,128)S(1)}, f32[2,32,128]{2,1,0:T(8,128)S(1)}, u32[]{:S(2)}, u32[]{:S(2)}) collective-permute-start(f32[2,32,128]{2,1,0:T(8,128)S(1)} %get-tuple-element.778), channel_id=1, source_target_pairs={{0,2},{1,3},{4,6},{5,7},{8,10},{9,11},{12,14},{13,15},{16,18},{17,... | collective-permute-start | bytes 98312 | tf_op jit(solution)/shard_map/ppermute | solution.py:27
  190.0 12.9 %copy-start.3 = (f32[2,32,256]{2,1,0:T(8,128)S(1)}, f32[2,32,256]{2,1,0:T(8,128)}, u32[]{:S(2)}) copy-start(f32[2,32,256]{2,1,0:T(8,128)} %reduce-scatter.8.cloned.1.call-done) | copy-start | bytes 196612
  225.5 5.8 %collective-permute-start.5 = (f32[2,32,128]{2,1,0:T(8,128)S(1)}, f32[2,32,128]{2,1,0:T(8,128)S(1)}, u32[]{:S(2)}, u32[]{:S(2)}) collective-permute-start(f32[2,32,128]{2,1,0:T(8,128)S(1)} %fusion.121), channel_id=1, source_target_pairs={{2,0},{3,1},{6,4},{7,5},{10,8},{11,9},{14,12},{15,13},{18,16},{19,... | collective-permute-start | bytes 98312 | tf_op jit(solution)/shard_map/ppermute | solution.py:28
  231.3 3.2 %collective-permute-start.4 = (f32[2,32,128]{2,1,0:T(8,128)S(1)}, f32[2,32,128]{2,1,0:T(8,128)S(1)}, u32[]{:S(2)}, u32[]{:S(2)}) collective-permute-start(f32[2,32,128]{2,1,0:T(8,128)S(1)} %get-tuple-element.774), channel_id=1, source_target_pairs={{0,2},{1,3},{4,6},{5,7},{8,10},{9,11},{12,14},{13,15},{16,18},{17,... | collective-permute-start | bytes 98312 | tf_op jit(solution)/shard_map/ppermute | solution.py:27
Sparse Core Ops, SparseCore 0:
  32.4 10.1 reduce-scatter.3
  110.2 6.4 reduce-scatter.5
  183.5 6.5 reduce-scatter.7
where the time goes:
time: 243 us; the launch traced here: 242 us
  other arithmetic  96.4 us (40%)
  blocking collectives  41.6 us (17%)
  waiting for transfers between devices  41.1 us (17%)
  local copies, waits for them, and re-layouts  25.3 us (10%)
  between operations  14.3 us (6%)
  matrix products  9.69 us (4%)
  starting transfers between devices  8.97 us (4%)
  loops' own time  4.87 us (2%)
    another operation x120, other arithmetic  81.1 us
    psum x3, blocking collectives, shrink_partial(): total = lax.psum(energy, 'freq')  35.8 us
    reduce_scatter x3, waiting for transfers between devices, per_device(): lax.psum_scatter(partial_grad, 'rep', scatter_dimension=2, tiled=True)  23.6 us
    ppermute x3, waiting for transfers between devices, extended(): after = lax.ppermute(leading, axis, down)  13.5 us
    mul x96, local copies, waits for them, and re-layouts, build_tables(): weight = jnp.transpose(active, (0, 2, 1)) * amplitude  7.48 us
    broadcast_in_dim x48, local copies, waits for them, and re-layouts, build_tables(): jnp.repeat(jnp.repeat(pattern_block.astype(jnp.float32), SPB // PY, axis=...  6.16 us
    ppermute x3, starting transfers between devices, extended(): before = lax.ppermute(last, axis, up)  4.98 us
  transfers between devices with their start and end apart: 9, of which 9 were waited for; matrix products, arithmetic and copies ran while one was open for 0% of the time, Pallas kernels for 0%

commit v1 on v0

v1 whole, which is shorter than its diff:
```python
import functools
import math

import jax
import jax.numpy as jnp
from jax import lax
from jax.experimental import pallas as pl
from jax.experimental.pallas import tpu as pltpu
from jax.sharding import PartitionSpec as P

PX = 16
PY = 32
SPB = 64
OBS = 128
ITERS = 3
LANES = 128
GROUP = 4

step_length = 1.0
epsilon = 1e-06
HIGHEST = lax.Precision.HIGHEST
VMEM_LIMIT = 56 * 1024 * 1024


def iota(shape, dim):
    return lax.broadcasted_iota(jnp.int32, shape, dim)


def half_turns(y):
    quarter = jnp.floor(2.0 * y + 0.5)
    r = y - 0.5 * quarter
    q = quarter.astype(jnp.int32)
    r2 = r * r
    pi = math.pi
    sine = r * (
        pi
        + r2
        * (
            -(pi**3) / 6
            + r2 * (pi**5 / 120 + r2 * (-(pi**7) / 5040 + r2 * (pi**9 / 362880)))
        )
    )
    cosine = 1.0 + r2 * (
        -(pi**2) / 2 + r2 * (pi**4 / 24 + r2 * (-(pi**6) / 720 + r2 * (pi**8 / 40320)))
    )
    odd = (q & 1) == 1
    c = jnp.where(odd, sine, cosine)
    s = jnp.where(odd, cosine, sine)
    c = jnp.where(((q + 1) & 2) != 0, -c, c)
    s = jnp.where((q & 2) != 0, s, -s)
    return c, s


def times(p, q):
    return p[0] * q[0] - p[1] * q[1], p[0] * q[1] + p[1] * q[0]


def pack_kernel(place, recorded, geometry, present, intersection, pattern, keep, send):
    half = recorded.shape[1] // 2
    rep = place[1]
    for out, part in ((keep, rep), (send, 1 - rep)):
        for c in range(2):
            out[c * half : (c + 1) * half, :] = recorded[
                c, pl.ds(pl.multiple_of(part * half, 8), half), :
            ]
        base = 2 * half
        out[base : base + 8, :] = jnp.zeros((8, out.shape[1]), jnp.float32)
        pat = pattern[pl.ds(pl.multiple_of(part * half, 8), half), :].astype(jnp.float32)
        for h in range(half // 8):
            out[base : base + 8, h * LANES : h * LANES + pat.shape[1]] = pat[8 * h : 8 * h + 8]
        for t in range(4):
            sl = slice(t * LANES, (t + 1) * LANES)
            out[base + t : base + t + 1, 256:384] = geometry[0:1, sl]
            out[base + 4 + t : base + 5 + t, 256:384] = geometry[1:2, sl]
            out[base + t : base + t + 1, 384:512] = present[0:1, sl].astype(jnp.float32)
        out[base + 4 : base + 5, 384:512] = intersection[...].astype(jnp.float32)


def doubled(rows):
    turned = pltpu.roll(rows, 4, 0)
    low = iota(rows.shape, 0) < 4
    return jnp.where(low, rows, turned), jnp.where(low, turned, rows)


def project_group(hb, cross, low_rows, first_lanes, sign):
    g = lax.dot_general(hb, cross, (((1,), (1,)), ((), ())), preferred_element_type=jnp.float32)
    g = jnp.where(low_rows, g[:, :LANES], g[:, LANES:])
    g = jnp.where(first_lanes, g, 0.0)
    g = g + pltpu.roll(g, 64, 1)
    swapped = pltpu.roll(g, 32, 1)
    half = g.shape[0] // 2
    top = g[:half] + sign * swapped[half:]
    bottom = g[half:] - sign * swapped[:half]
    return top, bottom


def fold_masks():
    rows = iota((2 * PX * GROUP, LANES), 0) % GROUP
    lanes = iota((2 * PX * GROUP, LANES), 1) // 64
    low_rows = rows < 2
    first_lanes = (rows % 2) == lanes
    sign = jnp.where((iota((PX * GROUP, LANES), 1) // 32) % 2 == 0, 1.0, -1.0)
    return low_rows, first_lanes, sign


def weigh(inline, w, g, tile, r_re, r_im, hb):
    half = PX * GROUP
    sl = pl.ds(tile * LANES, LANES)
    for i in range(half // 16):
        rows = slice(16 * i, 16 * i + 16)
        low = slice(half + 16 * i, half + 16 * i + 16)
        a_re = inline[w, g, rows, sl].astype(jnp.float32)
        a_im = inline[w, g, low, sl].astype(jnp.float32)
        rr = jnp.concatenate([r_re, r_re], axis=0)
        ri = jnp.concatenate([r_im, r_im], axis=0)
        hb[w, rows, sl] = (a_re * rr + a_im * ri).astype(jnp.bfloat16)
        hb[w, low, sl] = (a_re * ri - a_im * rr).astype(jnp.bfloat16)


def pack_energy(acc, energy, windows):
    block = iota((16, LANES), 1) // 32
    own = iota((16, LANES), 0) // GROUP
    for w in range(windows):
        both = acc[w] + pltpu.roll(acc[w], 32, 1)
        for j in range(4):
            rows = jnp.where(block == own, both[16 * j : 16 * j + 16], 0.0)
            energy[w * 4 + j : w * 4 + j + 1, :] = jnp.sum(rows, axis=0, keepdims=True)


def table_kernel(
    windows, nfreq, amplitude, count, place, *refs
):
    pays = refs[:count]
    cross, inline, observed, mask, matching, updated, energy, pay, hb, acc, weights = refs[count:]
    win, first = place[0], place[2]
    half = pay.shape[2] - 8
    freqs = half // 2
    groups = freqs // GROUP
    base = half
    if count == 4:
        for s in range(2):
            pay[win, s] = pays[s][...]
            pay[1 - win, s] = pays[2 + s][...]
    else:
        for w in range(windows):
            for s in range(2):
                pay[w, s] = pays[s][w]

    for s in range(2):
        index = pay[win, s, base + 4 : base + 5, 384:512].astype(jnp.int32)
        hot = (iota((LANES, LANES), 0) == index).astype(jnp.float32)
        eye = (iota((LANES, LANES), 0) == iota((LANES, LANES), 1)).astype(jnp.float32)
        matching[s] = jnp.where(win > 0, hot, eye)
    nt = (((1,), (1,)), ((), ()))

    def align(n, _):
        w, s = 1 + n // 2, n % 2
        index = pay[w, s, base + 4 : base + 5, 384:512].astype(jnp.int32)
        hot = (iota((LANES, LANES), 0) == index).astype(jnp.float32)
        dot = functools.partial(
            lax.dot_general,
            dimension_numbers=nt,
            precision=HIGHEST,
            preferred_element_type=jnp.float32,
        )
        pay[w, s, 0:half, 0:LANES] = dot(pay[w, s, 0:half, 0:LANES], hot)
        geo = dot(pay[w, s, base : base + 8, 256:384], hot)
        pay[w, s, base : base + 1, 256:384] = geo[0:1]
        pay[w, s, base + 4 : base + 5, 256:384] = geo[4:5]
        here = dot(pay[w, s, base : base + 8, 384:512], hot)
        pay[w, s, base : base + 1, 384:512] = here[0:1]
        return 0

    lax.fori_loop(0, 2 * (windows - 1), align, 0)

    for s in range(2):
        for h in range(freqs // 8):
            low, high = doubled(pay[0, s, base : base + 8, h * LANES : (h + 1) * LANES])
            weights[s, 2 * h] = low * amplitude
            weights[s, 2 * h + 1] = high * amplitude

    sub = iota((8, LANES), 0)
    delta = 0.75 / nfreq
    start = first.astype(jnp.float32)
    scale0 = 0.25 + 0.75 * ((start + 0.5) / nfreq)
    group_scale0 = 0.25 + 0.75 * ((start + (sub % GROUP).astype(jnp.float32) + 0.5) / nfreq)
    odd_cross = (2 * sub - (PY - 1)).astype(jnp.float32)
    odd_inline = (2 * (2 * (sub // GROUP) - (PX - 1))).astype(jnp.float32)

    def strip_tables(n, _):
        w, s = n // 2, n % 2
        for t in range(4):
            off = pl.multiple_of(s * 512 + t * LANES, LANES)
            sl = pl.ds(off, LANES)
            g0 = pay[w, s, base + t : base + t + 1, 256:384]
            g1 = pay[w, s, base + 4 + t : base + 5 + t, 256:384]
            here = jnp.broadcast_to(pay[w, s, base + t : base + t + 1, 384:512], (8, LANES))
            mask[w, :, sl] = here
            now = half_turns((scale0 * g1) * odd_cross)
            more = half_turns((delta * g1) * odd_cross)
            g1b = jnp.broadcast_to(g1, (8, LANES))
            rot = half_turns((scale0 * g1b) * 16.0)
            rot_more = half_turns((delta * g1b) * 16.0)
            for f in range(freqs):
                v0 = now
                v1 = times(v0, rot)
                v2 = times(v1, rot)
                v3 = times(v2, rot)
                row = (f % GROUP) * 64
                for part in range(2):
                    cross[w, f // GROUP, row + 32 * part : row + 32 * part + 16, sl] = (
                        jnp.concatenate([v0[part], v1[part]], axis=0).astype(jnp.bfloat16)
                    )
                    cross[w, f // GROUP, row + 32 * part + 16 : row + 32 * part + 32, sl] = (
                        jnp.concatenate([v2[part], v3[part]], axis=0).astype(jnp.bfloat16)
                    )
                if f + 1 < freqs:
                    now = times(now, more)
                    rot = times(rot, rot_more)
            now = half_turns((group_scale0 * g0) * odd_inline)
            more = half_turns((GROUP * delta * g0) * odd_inline)
            rot = half_turns((group_scale0 * g0) * 8.0)
            rot_more = half_turns((GROUP * delta * jnp.broadcast_to(g0, (8, LANES))) * 8.0)
            for g in range(groups):
                v = now
                for i in range(PX // 4):
                    u = times(v, rot)
                    cv = weights[s, g, :, 8 * i + t : 8 * i + t + 1]
                    cu = weights[s, g, :, 8 * i + 4 + t : 8 * i + 5 + t]
                    for part in range(2):
                        row = part * PX * GROUP + 16 * i
                        inline[w, g, row : row + 16, sl] = jnp.concatenate(
                            [v[part] * cv, u[part] * cu], axis=0
                        ).astype(jnp.bfloat16)
                    if i + 1 < PX // 4:
                        v = times(u, rot)
                if g + 1 < groups:
                    now = times(now, more)
                    rot = times(rot, rot_more)
        for c in range(2):
            for h in range(freqs // 8):
                for t in range(4):
                    sl = pl.ds(pl.multiple_of(s * 512 + t * LANES, LANES), LANES)
                    here = jnp.broadcast_to(
                        pay[w, s, base + t : base + t + 1, 384:512], (8, LANES)
                    )
                    rows = here * pay[
                        w, s, c * freqs + 8 * h : c * freqs + 8 * h + 8, t * LANES : (t + 1) * LANES
                    ]
                    low, high = doubled(rows)
                    observed[c, w, 2 * h, :, sl] = low
                    observed[c, w, 2 * h + 1, :, sl] = high
        return 0

    lax.fori_loop(0, 2 * windows, strip_tables, 0)

    low_rows, first_lanes, sign = fold_masks()
    rows = PX * GROUP
    acc[...] = jnp.zeros_like(acc)

    def first_group(n, _):
        g, w = n % groups, n // groups
        for tile in range(8):
            sl = slice(tile * LANES, (tile + 1) * LANES)
            weigh(inline, w, g, tile, -observed[0, w, g, :, sl], -observed[1, w, g, :, sl], hb)
        top, bottom = project_group(hb[w], cross[w, g], low_rows, first_lanes, sign)
        top, bottom = -step_length * top, -step_length * bottom
        updated[w, g, :rows] = top
        updated[w, g, rows:] = bottom
        acc[w] += top * top
        return 0

    lax.fori_loop(0, windows * groups, first_group, 0)
    pack_energy(acc, energy, windows)


def spread_factor(energies, threshold, factor, windows, nfreq):
    total = energies[0][...]
    for e in energies[1:]:
        total = total + e[...]
    limit = jnp.concatenate([threshold[...]] * windows, axis=0)
    packed = jnp.maximum(0.0, 1.0 - limit / jnp.sqrt(total / nfreq + epsilon))
    block = iota((8, LANES), 1) // 32
    own = iota((8, LANES), 0) // GROUP
    for w in range(windows):
        for j in range(4):
            row = jnp.broadcast_to(packed[w * 4 + j : w * 4 + j + 1], (8, LANES))
            for k in range(2):
                y = jnp.where(block == own + 2 * k, row, 0.0)
                y = y + pltpu.roll(y, 32, 1)
                y = y + pltpu.roll(y, 64, 1)
                factor[w, 16 * j + 8 * k : 16 * j + 8 * k + 8, :] = y


def mixing_masks():
    rows = iota((2 * PX * GROUP, LANES), 0) % GROUP
    lanes = iota((2 * PX * GROUP, LANES), 1) // 64
    return rows == lanes, rows == lanes + 2


def scaled(updated, factor, w, g):
    rows = PX * GROUP
    shrink = factor[w]
    return updated[w, g, :rows] * shrink, updated[w, g, rows:] * shrink


def predict_group(current, cross, inline, w, g, masks):
    m = jnp.concatenate(current, axis=0)
    mixing = jnp.concatenate(
        [jnp.where(masks[0], m, 0.0), jnp.where(masks[1], m, 0.0)], axis=1
    ).astype(jnp.bfloat16)
    rows = PX * GROUP
    out = []
    for pair in range(4):
        part = jnp.dot(
            mixing,
            cross[w, g, :, pair * 256 : (pair + 1) * 256],
            preferred_element_type=jnp.float32,
        )
        for k in range(2):
            tile = 2 * pair + k
            sl = slice(tile * LANES, (tile + 1) * LANES)
            p_re = p_im = None
            for i in range(rows // 16):
                a_re = inline[w, g, 16 * i : 16 * i + 16, sl].astype(jnp.float32)
                a_im = inline[w, g, rows + 16 * i : rows + 16 * i + 16, sl].astype(jnp.float32)
                b_re = part[16 * i : 16 * i + 16, k * LANES : (k + 1) * LANES]
                b_im = part[rows + 16 * i : rows + 16 * i + 16, k * LANES : (k + 1) * LANES]
                re = a_re * b_re - a_im * b_im
                im = a_re * b_im + a_im * b_re
                p_re = re if p_re is None else p_re + re
                p_im = im if p_im is None else p_im + im
            p_re = p_re[:8] + p_re[8:]
            p_im = p_im[:8] + p_im[8:]
            out.append((p_re + pltpu.roll(p_re, 4, 0), p_im + pltpu.roll(p_im, 4, 0)))
    return out


def blend(predicted, windows):
    ramp = (iota((8, LANES), 1).astype(jnp.float32) + 0.5) / LANES
    for w in range(windows - 1):
        for s in range(2):
            lower, upper = predicted[w][4 * s + 3], predicted[w + 1][4 * s]
            both = tuple((1.0 - ramp) * lower[c] + ramp * upper[c] for c in range(2))
            predicted[w][4 * s + 3] = both
            predicted[w + 1][4 * s] = both
    return predicted


def step_kernel(windows, nfreq, count, *refs):
    energies = refs[:count]
    threshold, updated, cross, inline, observed, mask = refs[count : count + 6]
    new, energy, factor, hb, acc = refs[count + 6 :]
    spread_factor(energies, threshold, factor, windows, nfreq)
    masks = mixing_masks()
    low_rows, first_lanes, sign = fold_masks()
    rows = PX * GROUP
    acc[...] = jnp.zeros_like(acc)

    def one_group(g, _):
        predicted = []
        for w in range(windows):
            current = scaled(updated, factor, w, g)
            predicted.append(predict_group(current, cross, inline, w, g, masks))
        predicted = blend(predicted, windows)
        for w in range(windows):
            for tile in range(8):
                sl = slice(tile * LANES, (tile + 1) * LANES)
                here = mask[w, :, sl]
                p_re, p_im = predicted[w][tile]
                r_re = here * p_re - observed[0, w, g, :, sl]
                r_im = here * p_im - observed[1, w, g, :, sl]
                weigh(inline, w, g, tile, r_re, r_im, hb)
            top, bottom = project_group(hb[w], cross[w, g], low_rows, first_lanes, sign)
            current = scaled(updated, factor, w, g)
            top = current[0] - step_length * top
            bottom = current[1] - step_length * bottom
            new[w, g, :rows] = top
            new[w, g, rows:] = bottom
            acc[w] += top * top
        return 0

    lax.fori_loop(0, updated.shape[1], one_group, 0)
    pack_energy(acc, energy, windows)


def final_kernel(windows, nfreq, count, place, *refs):
    energies = refs[:count]
    threshold, updated, cross, inline, matching = refs[count : count + 5]
    swap, keep, factor = refs[count + 5 :]
    win = place[0]
    spread_factor(energies, threshold, factor, windows, nfreq)
    masks = mixing_masks()
    rows = PX * GROUP
    low = iota((8, LANES), 0) < 4
    even = (iota((rows, LANES), 1) // 32) % 2 == 0
    block = iota((8, LANES), 1) // 32
    own = iota((8, LANES), 0) // GROUP

    def pick(values):
        out = values[0]
        for w in range(1, windows):
            out = jnp.where(win == w, values[w], out)
        return out

    def two_groups(h, _):
        coeffs, traces = [], []
        for k in range(2):
            g = 2 * h + k
            current = [scaled(updated, factor, w, g) for w in range(windows)]
            predicted = blend(
                [predict_group(current[w], cross, inline, w, g, masks) for w in range(windows)],
                windows,
            )
            traces.append(
                [[pick([predicted[w][t][c] for w in range(windows)]) for t in range(8)] for c in range(2)]
            )
            top = pick([current[w][0] for w in range(windows)])
            bottom = pick([current[w][1] for w in range(windows)])
            parts = (jnp.where(even, top, bottom), jnp.where(even, bottom, -top))
            lines = []
            for m in parts:
                line = []
                for j in range(4):
                    v = jnp.where(block == own, m[16 * j : 16 * j + 8], 0.0) + jnp.where(
                        block == own + 2, m[16 * j + 8 : 16 * j + 16], 0.0
                    )
                    line.append(v + pltpu.roll(v, 4, 0))
                lines.append(line)
            coeffs.append(lines)
        sl = pl.ds(pl.multiple_of(8 * h, 8), 8)
        for c in range(2):
            for j in range(4):
                lanes = slice(j * LANES, (j + 1) * LANES)
                both = jnp.where(low, coeffs[0][c][j], coeffs[1][c][j])
                swap[0, c, sl, lanes] = both
                keep[0, c, sl, lanes] = both
            for t in range(8):
                lanes = slice((t % 4) * LANES, (t % 4 + 1) * LANES)
                out = keep if t < 4 else swap
                out[1, c, sl, lanes] = jnp.where(low, traces[0][c][t], traces[1][c][t])
        return 0

    lax.fori_loop(0, updated.shape[1] // 2, two_groups, 0)
    for s, out in enumerate((keep, swap)):
        for c in range(2):
            out[1, c, :, :LANES] = jnp.dot(
                out[1, c, :, :LANES],
                matching[s],
                precision=HIGHEST,
                preferred_element_type=jnp.float32,
            )


VM = pl.BlockSpec(memory_space=pltpu.VMEM)
SM = pl.BlockSpec(memory_space=pltpu.SMEM)
PARAMS = pltpu.CompilerParams(vmem_limit_bytes=VMEM_LIMIT)


def shape(*dims, dtype=jnp.float32):
    return jax.ShapeDtypeStruct(dims, dtype)


def sum_parts(energy):
    swap = [(0, 1), (1, 0)]
    energy = energy + lax.ppermute(energy, "rep", swap)
    size = lax.axis_size("freq")
    if size & (size - 1):
        return [lax.psum(energy, "freq")]
    axes = ("freq", "rep")

    def crossed(k):
        return [(2 * i + r, 2 * (i ^ k) + 1 - r) for i in range(size) for r in range(2)]

    if size <= 4:
        return [energy] + [lax.ppermute(energy, axes, crossed(k)) for k in range(1, size)]
    k = 1
    while k < size:
        energy = energy + lax.ppermute(energy, axes, crossed(k))
        k *= 2
    return [energy]


def per_device(recorded, geometry, present, intersection_index, pattern, group_scale):
    frequencies = recorded.shape[1]
    traces = recorded.shape[3]
    windows = lax.axis_size("win")
    nfreq = frequencies * lax.axis_size("freq")
    half = frequencies // 2
    groups = half // GROUP
    amplitude = 1.0 / math.sqrt(traces * lax.axis_size("rep"))
    win, rep = lax.axis_index("win"), lax.axis_index("rep")
    first = lax.axis_index("freq") * frequencies + rep * half
    place = jnp.stack([win, rep, first]).astype(jnp.int32)
    width = 2 * traces
    swap = [(0, 1), (1, 0)]

    payload = shape(2 * half + 8, traces)
    keep, send = pl.pallas_call(
        pack_kernel,
        out_shape=(payload, payload),
        in_specs=[SM] + [VM] * 5,
        out_specs=(VM, VM),
        compiler_params=PARAMS,
        name="pack",
    )(
        place,
        recorded[:, :, 0, :],
        geometry[:, 0, :],
        present,
        intersection_index[0],
        pattern.reshape(frequencies, -1),
    )
    received = lax.ppermute(send, "rep", swap)
    if windows == 2:
        diagonal = [(2 * i + r, 2 * (1 - i) + 1 - r) for i in range(2) for r in range(2)]
        pays = [
            keep,
            received,
            lax.ppermute(keep, "win", swap),
            lax.ppermute(send, ("win", "rep"), diagonal),
        ]
    else:
        pays = [lax.all_gather(keep, "win"), lax.all_gather(received, "win")]

    rows = 2 * PX * GROUP
    state = shape(windows, groups, rows, LANES)
    energy_shape = shape(4 * windows, LANES)
    scratch = [
        pltpu.VMEM((windows, rows, width), jnp.bfloat16),
        pltpu.VMEM((windows, rows // 2, LANES), jnp.float32),
    ]
    cross, inline, observed, mask, matching, updated, energy = pl.pallas_call(
        functools.partial(table_kernel, windows, nfreq, amplitude, len(pays)),
        out_shape=(
            shape(windows, groups, 2 * PY * GROUP, width, dtype=jnp.bfloat16),
            shape(windows, groups, rows, width, dtype=jnp.bfloat16),
            shape(2, windows, groups, 8, width),
            shape(windows, 8, width),
            shape(2, LANES, LANES),
            state,
            energy_shape,
        ),
        in_specs=[SM] + [VM] * len(pays),
        out_specs=(VM,) * 7,
        scratch_shapes=[pltpu.VMEM((windows, 2, 2 * half + 8, traces), jnp.float32)]
        + scratch
        + [pltpu.VMEM((2, groups, 8, LANES), jnp.float32)],
        compiler_params=PARAMS,
        name="tables",
    )(place, *pays)

    threshold = group_scale.reshape(4, LANES)
    factor_scratch = pltpu.VMEM((windows, rows // 2, LANES), jnp.float32)
    for _ in range(ITERS - 1):
        energies = sum_parts(energy)
        updated, energy = pl.pallas_call(
            functools.partial(step_kernel, windows, nfreq, len(energies)),
            out_shape=(state, energy_shape),
            in_specs=[VM] * (len(energies) + 6),
            out_specs=(VM, VM),
            scratch_shapes=[factor_scratch] + scratch,
            compiler_params=PARAMS,
            name="step",
        )(*energies, threshold, updated, cross, inline, observed, mask)
    energies = sum_parts(energy)
    halves = shape(2, 2, half, traces)
    theirs, mine = pl.pallas_call(
        functools.partial(final_kernel, windows, nfreq, len(energies)),
        out_shape=(halves, halves),
        in_specs=[SM] + [VM] * (len(energies) + 5),
        out_specs=(VM, VM),
        scratch_shapes=[factor_scratch],
        compiler_params=PARAMS,
        name="final",
    )(place, *energies, threshold, updated, cross, inline, matching)
    theirs = lax.ppermute(theirs, "rep", swap)
    both = jnp.where(
        rep == 0,
        jnp.concatenate([mine, theirs], axis=2),
        jnp.concatenate([theirs, mine], axis=2),
    )
    return (both[0][:, :, None, :], both[1][:, :, None, :])


def solution(mesh):
    return jax.shard_map(
        per_device,
        mesh=mesh,
        in_specs=(
            P(None, "freq", ("dom", "win"), "rep"),
            P(None, ("dom", "win"), "rep"),
            P(("dom", "win"), "rep"),
            P(("dom", "win"), "rep", None),
            P("freq", None, "rep"),
            P(),
        ),
        out_specs=(P(None, "freq", ("dom", "win"), None), P(None, "freq", ("dom", "win"), "rep")),
        check_vma=False,
    )
```

time: 243 us -> 81.4 us (0.33)
  other arithmetic: 96.4 us -> 3.71 us
  blocking collectives: 41.6 us -> 0 us
  Pallas kernels: 0 us -> 35.5 us
  waiting for transfers between devices: 41.1 us -> 16.4 us
  local copies, waits for them, and re-layouts: 25.3 us -> 8.86 us
  between operations: 14.3 us -> 0.71 us
  matrix products: 9.69 us -> 0 us
  starting transfers between devices: 8.97 us -> 15.9 us
  loops' own time: 4.87 us -> 0 us
    another operation x144 -> x1, other arithmetic: 83.5 us -> 0.65 us  [per_device(): place = jnp.stack([win, rep, first]).astype(jnp.int32)]
    psum x3 -> x0, blocking collectives: 35.8 us -> none  [shrink_partial(): total = lax.psum(energy, 'freq')]
    pallas_call x0 -> x5, Pallas kernels: none -> 35.5 us  [the longest x2 16.6 us: per_device(): pl.pallas_call(functools.partial(step_kernel, windows, nfreq, len(energie...]
    reduce_scatter x3 -> x0, waiting for transfers between devices: 23.6 us -> none  [per_device(): lax.psum_scatter(partial_grad, 'rep', scatter_dimension=2, tiled=True)]
    broadcast_in_dim x121 -> x0, local copies, waits for them, and re-layouts: 9.92 us -> none  [the longest x48 6.16 us: build_tables(): jnp.repeat(jnp.repeat(pattern_block.astype(jnp.float32), SPB // PY, axis=...]
    dot_general x54 -> x0, matrix products: 9.69 us -> none  [the longest x24 4.38 us: back_one_block(): jnp.einsum('fxk,fxc->fkc', cross_table, weighted, preferred_element_type=...]
    mul x168 -> x0, local copies, waits for them, and re-layouts: 8.09 us -> none  [the longest x96 7.48 us: build_tables(): weight = jnp.transpose(active, (0, 2, 1)) * amplitude]
    ppermute x6 -> x16, starting transfers between devices: 8.85 us -> 15.9 us  [the longest x9 12 us: sum_parts(): lax.ppermute(energy, axes, crossed(k))]
  transfers between devices with their start and end apart: 9 -> 16, of which waited for: 9 -> 13; matrix products, arithmetic and copies ran while one was open for 0% -> 0% of each run, Pallas kernels for 0% -> 0%
where the time goes in v1:
time: 81.4 us; the launch traced here: 81 us
  Pallas kernels  35.5 us (44%)
  waiting for transfers between devices  16.4 us (20%)
  starting transfers between devices  15.9 us (20%)
  local copies, waits for them, and re-layouts  8.86 us (11%)
  other arithmetic  3.71 us (5%)
    pallas_call x2, Pallas kernels, per_device(): pl.pallas_call(functools.partial(step_kernel, windows, nfreq, len(energie...  16.6 us
    ppermute x9, starting transfers between devices, sum_parts(): lax.ppermute(energy, axes, crossed(k))  12 us
    pallas_call x1, Pallas kernels, per_device(): pl.pallas_call(functools.partial(table_kernel, windows, nfreq, amplitude,...  11.4 us
    unnamed x34, local copies, waits for them, and re-layouts  7.46 us
    ppermute x9, waiting for transfers between devices, sum_parts(): lax.ppermute(energy, axes, crossed(k))  6.93 us
    pallas_call x1, Pallas kernels, per_device(): pl.pallas_call(functools.partial(final_kernel, windows, nfreq, len(energi...  5.87 us
    ppermute x3, waiting for transfers between devices, sum_parts(): energy = energy + lax.ppermute(energy, 'rep', swap)  3.64 us
    ppermute x1, starting transfers between devices, per_device(): lax.ppermute(keep, 'win', swap)  2.94 us
  transfers between devices with their start and end apart: 16, of which 13 were waited for; matrix products, arithmetic and copies ran while one was open for 0% of the time, Pallas kernels for 0%

profile of v1, /device:TPU:0, one launch (start us, length us, event | category | flops | bytes accessed | tf_op | source)
XLA Modules:
  0.0 81.0 jit_solution(15230977378109751544)
XLA Ops:
  0.6 1.3 %copy.19 = f32[2,1,512]{2,0,1:T(2,128)} copy(f32[2,1,512]{2,1,0:T(1,128)} %param.7) | data formatting | bytes 8192
  1.9 1.4 %copy.11.pattern = s32[32,32]{1,0:T(8,128)} copy(s32[32,32]{0,1:T(8,128)} %bitcast.21) | data formatting | bytes 8192 | tf_op jit(solution)/shard_map/reshape | solution.py:512
  3.3 1.6 %copy.18 = f32[2,32,1,512]{3,1,2,0:T(8,128)} copy(f32[2,32,1,512]{3,2,1,0:T(1,128)} %param.6) | data formatting | bytes 262144
  4.9 0.6 pad_add_fusion.place
  5.5 1.6 %pack.1 = (f32[40,512]{1,0:T(8,128)}, f32[40,512]{1,0:T(8,128)}) custom-call(s32[3]{0:T(128)} %pad_add_fusion.place, f32[2,32,512]{2,1,0:T(8,128)} %bitcast.16, f32[2,512]{1,0:T(2,128)} %bitcast.20, s32[1,512]{1,0:T(1,128)} %present.1, s32[1,128]{1,0:T(1,128)} %bitcast.22, s32[32,32]{1,0:T(8,128)} %copy.11.pattern), custom_call_target="tpu_custom_call" | custom-call | tf_op jit(solution)/shard_map/pack/pallas_call | solution.py:499
  7.1 2.9 %collective-permute-start.1 = (f32[40,512]{1,0:T(8,128)}, f32[40,512]{1,0:T(8,128)S(1)}, u32[]{:S(2)}, u32[]{:S(2)}) collective-permute-start(f32[40,512]{1,0:T(8,128)} %get-tuple-element.17.refs_0_), channel_id=1, source_target_pairs={{0,2},{2,0},{1,3},{3,1},{4,6},{6,4},{5,7},{7,5},{8,10},{10,8},{9,1... | collective-permute-start | bytes 245768 | tf_op jit(solution)/shard_map/ppermute | solution.py:520
  10.1 0.1 collective-permute-start
  10.2 2.7 %collective-permute-done.1.refs_2_ = f32[40,512]{1,0:T(8,128)S(1)} collective-permute-done((f32[40,512]{1,0:T(8,128)}, f32[40,512]{1,0:T(8,128)S(1)}, u32[]{:S(2)}, u32[]{:S(2)}) %collective-permute-start.1) | collective-permute-done | bytes 81952 | tf_op jit(solution)/shard_map/ppermute | solution.py:520
  13.0 1.8 %collective-permute-done.2.refs_3_ = f32[40,512]{1,0:T(8,128)S(1)} collective-permute-done((f32[40,512]{1,0:T(8,128)}, f32[40,512]{1,0:T(8,128)S(1)}, u32[]{:S(2)}, u32[]{:S(2)}) %collective-permute-start.2) | collective-permute-done | bytes 81952 | tf_op jit(solution)/shard_map/ppermute | solution.py:521
  14.8 0.6 copy-done.1
  15.4 0.6 copy-done.2
  16.0 11.4 %tables.1 = (bf16[2,4,256,1024]{3,2,1,0:T(8,128)(2,1)}, bf16[2,4,128,1024]{3,2,1,0:T(8,128)(2,1)}, f32[2,2,4,8,1024]{4,3,2,1,0:T(8,128)}, f32[2,8,1024]{2,1,0:T(...) custom-call(s32[3]{0:T(128)} %pad_add_fusion.place, ...), custom_call_target="tpu_custom_call" | custom-call | tf_op jit(solution)/shard_map/tables/pallas_call | solution.py:533
  27.4 1.4 %collective-permute-done.3 = f32[8,128]{1,0:T(8,128)S(1)} collective-permute-done((f32[8,128]{1,0:T(8,128)}, f32[8,128]{1,0:T(8,128)S(1)}, u32[]{:S(2)}, u32[]{:S(2)}) %collective-permute-start.3) | collective-permute-done | bytes 4128 | tf_op jit(solution)/shard_map/ppermute | solution.py:466
  28.8 0.7 add.13.refs_0_
  29.5 3.6 %collective-permute-start.6 = (f32[8,128]{1,0:T(8,128)S(1)}, f32[8,128]{1,0:T(8,128)S(1)}, u32[]{:S(2)}, u32[]{:S(2)}) collective-permute-start(f32[8,128]{1,0:T(8,128)S(1)} %add.13.refs_0_), channel_id=1, source_target_pairs={{0,13},{1,12},{4,9},{5,8},{8,5},{9,4},{12,1},{13,0},{2,15},{3,14},... | collective-permute-start | bytes 12296 | tf_op jit(solution)/shard_map/ppermute | solution.py:476
  33.1 0.5 collective-permute-start.4
  33.6 0.8 %collective-permute-done.6.refs_3_ = f32[8,128]{1,0:T(8,128)S(1)} collective-permute-done((f32[8,128]{1,0:T(8,128)S(1)}, f32[8,128]{1,0:T(8,128)S(1)}, u32[]{:S(2)}, u32[]{:S(2)}) %collective-permute-start.6) | collective-permute-done | bytes 4128 | tf_op jit(solution)/shard_map/ppermute | solution.py:476
  34.4 2.6 %collective-permute-done.5.refs_2_ = f32[8,128]{1,0:T(8,128)S(1)} collective-permute-done((f32[8,128]{1,0:T(8,128)S(1)}, f32[8,128]{1,0:T(8,128)S(1)}, u32[]{:S(2)}, u32[]{:S(2)}) %collective-permute-start.5) | collective-permute-done | bytes 4128 | tf_op jit(solution)/shard_map/ppermute | solution.py:476
  37.0 0.6 copy-done.9
  37.6 0.0 copy-done.11
  37.6 8.3 %step.2 = (f32[2,4,128,128]{3,2,1,0:T(8,128)}, f32[8,128]{1,0:T(8,128)}) custom-call(f32[8,128]{1,0:T(8,128)} %copy-done.4, f32[8,128]{1,0:T(8,128)} %copy-done.11, f32[8,128]{1,0:T(8,128)} %copy-done.9, f32[8,128]{1,0:T(8,128)} %copy-done.7, f32[4,128]{1,0:T(4,128)} %bitcast.17, f32[2,4,128,128]{3,2,1,0:T(8,128)} %get-tuple-element.20.refs_5_, ...), custom_call_target="tpu_custom_call" | custom-call | tf_op jit(solution)/shard_map/step/pallas_call | solution.py:557
  45.9 0.3 collective-permute-start.7
  46.3 1.0 %collective-permute-done.7 = f32[8,128]{1,0:T(8,128)S(1)} collective-permute-done((f32[8,128]{1,0:T(8,128)}, f32[8,128]{1,0:T(8,128)S(1)}, u32[]{:S(2)}, u32[]{:S(2)}) %collective-permute-start.7) | collective-permute-done | bytes 4128 | tf_op jit(solution)/shard_map/ppermute | solution.py:466
  47.3 0.7 add.14.refs_0_
  48.0 1.4 %collective-permute-start.10 = (f32[8,128]{1,0:T(8,128)S(1)}, f32[8,128]{1,0:T(8,128)S(1)}, u32[]{:S(2)}, u32[]{:S(2)}) collective-permute-start(f32[8,128]{1,0:T(8,128)S(1)} %add.14.refs_0_), channel_id=1, source_target_pairs={{0,13},{1,12},{4,9},{5,8},{8,5},{9,4},{12,1},{13,0},{2,15},{3,14},... | collective-permute-start | bytes 12296 | tf_op jit(solution)/shard_map/ppermute | solution.py:476
  49.4 0.3 collective-permute-start.9
  49.7 2.3 %collective-permute-start.8 = (f32[8,128]{1,0:T(8,128)S(1)}, f32[8,128]{1,0:T(8,128)S(1)}, u32[]{:S(2)}, u32[]{:S(2)}) collective-permute-start(f32[8,128]{1,0:T(8,128)S(1)} %add.14.refs_0_), channel_id=1, source_target_pairs={{0,5},{1,4},{4,1},{5,0},{8,13},{9,12},{12,9},{13,8},{2,7},{3,6},{6... | collective-permute-start | bytes 12296 | tf_op jit(solution)/shard_map/ppermute | solution.py:476
  52.1 0.8 collective-permute-done.10.refs_3_
  52.8 0.5 collective-permute-done.9.refs_2_
  53.3 0.1 collective-permute-done.8.refs_1_
  53.4 0.5 copy-done.8
  53.9 0.1 copy-done.10
  54.0 8.3 %step.3 = (f32[2,4,128,128]{3,2,1,0:T(8,128)}, f32[8,128]{1,0:T(8,128)}) custom-call(f32[8,128]{1,0:T(8,128)} %copy-done.3, f32[8,128]{1,0:T(8,128)} %copy-done.10, f32[8,128]{1,0:T(8,128)} %copy-done.8, f32[8,128]{1,0:T(8,128)} %copy-done.6, f32[4,128]{1,0:T(4,128)} %bitcast.18, f32[2,4,128,128]{3,2,1,0:T(8,128)} %get-tuple-element.26.refs_5_, ...), custom_call_target="tpu_custom_call" | custom-call | tf_op jit(solution)/shard_map/step/pallas_call | solution.py:557
  62.3 0.1 collective-permute-start.11
  62.4 1.2 %collective-permute-done.11 = f32[8,128]{1,0:T(8,128)S(1)} collective-permute-done((f32[8,128]{1,0:T(8,128)}, f32[8,128]{1,0:T(8,128)S(1)}, u32[]{:S(2)}, u32[]{:S(2)}) %collective-permute-start.11) | collective-permute-done | bytes 4128 | tf_op jit(solution)/shard_map/ppermute | solution.py:466
  63.7 0.7 add.15.refs_0_
  64.4 2.1 %collective-permute-start.14 = (f32[8,128]{1,0:T(8,128)S(1)}, f32[8,128]{1,0:T(8,128)S(1)}, u32[]{:S(2)}, u32[]{:S(2)}) collective-permute-start(f32[8,128]{1,0:T(8,128)S(1)} %add.15.refs_0_), channel_id=1, source_target_pairs={{0,13},{1,12},{4,9},{5,8},{8,5},{9,4},{12,1},{13,0},{2,15},{3,14},... | collective-permute-start | bytes 12296 | tf_op jit(solution)/shard_map/ppermute | solution.py:476
  66.4 0.8 %collective-permute-start.13 = (f32[8,128]{1,0:T(8,128)S(1)}, f32[8,128]{1,0:T(8,128)S(1)}, u32[]{:S(2)}, u32[]{:S(2)}) collective-permute-start(f32[8,128]{1,0:T(8,128)S(1)} %add.15.refs_0_), channel_id=1, source_target_pairs={{0,9},{1,8},{4,13},{5,12},{8,1},{9,0},{12,5},{13,4},{2,11},{3,10},... | collective-permute-start | bytes 12296 | tf_op jit(solution)/shard_map/ppermute | solution.py:476
  67.3 1.0 %collective-permute-start.12 = (f32[8,128]{1,0:T(8,128)S(1)}, f32[8,128]{1,0:T(8,128)S(1)}, u32[]{:S(2)}, u32[]{:S(2)}) collective-permute-start(f32[8,128]{1,0:T(8,128)S(1)} %add.15.refs_0_), channel_id=1, source_target_pairs={{0,5},{1,4},{4,1},{5,0},{8,13},{9,12},{12,9},{13,8},{2,7},{3,6},{6... | collective-permute-start | bytes 12296 | tf_op jit(solution)/shard_map/ppermute | solution.py:476
  68.2 0.9 %collective-permute-done.14.refs_3_ = f32[8,128]{1,0:T(8,128)S(1)} collective-permute-done((f32[8,128]{1,0:T(8,128)S(1)}, f32[8,128]{1,0:T(8,128)S(1)}, u32[]{:S(2)}, u32[]{:S(2)}) %collective-permute-start.14) | collective-permute-done | bytes 4128 | tf_op jit(solution)/shard_map/ppermute | solution.py:476
  69.2 1.2 %collective-permute-done.13.refs_2_ = f32[8,128]{1,0:T(8,128)S(1)} collective-permute-done((f32[8,128]{1,0:T(8,128)S(1)}, f32[8,128]{1,0:T(8,128)S(1)}, u32[]{:S(2)}, u32[]{:S(2)}) %collective-permute-start.13) | collective-permute-done | bytes 4128 | tf_op jit(solution)/shard_map/ppermute | solution.py:476
  70.4 0.6 copy-done.13
  71.0 5.9 %final.1 = (f32[2,2,16,512]{3,2,1,0:T(8,128)}, f32[2,2,16,512]{3,2,1,0:T(8,128)}) custom-call(s32[3]{0:T(128)} %pad_add_fusion.place, f32[8,128]{1,0:T(8,128)} %copy-done.5, f32[8,128]{1,0:T(8,128)} %copy-done.14, f32[8,128]{1,0:T(8,128)} %copy-done.13, f32[8,128]{1,0:T(8,128)} %copy-done.12, f32[4,128]{1,0:T(4,128)} %bitcast.19, ...), custom_call_target="tpu_custom_call" | custom-call | tf_op jit(solution)/shard_map/final/pallas_call | solution.py:568
  76.9 0.3 collective-permute-start.15
  77.2 1.3 %collective-permute-done.15 = f32[2,2,16,512]{3,2,1,0:T(8,128)S(1)} collective-permute-done((f32[2,2,16,512]{3,2,1,0:T(8,128)}, f32[2,2,16,512]{3,2,1,0:T(8,128)S(1)}, u32[]{:S(2)}, u32[]{:S(2)}) %collective-permute-start.15) | collective-permute-done | bytes 131104 | tf_op jit(solution)/shard_map/ppermute | solution.py:577
  78.4 1.0 %maximum_select_fusion = f32[2,2,32,512]{3,2,1,0:T(8,128)S(1)} fusion(f32[2,2,16,512]{3,2,1,0:T(8,128)S(1)} %collective-permute-done.15, f32[2,2,16,512]{3,2,1,0:T(8,128)} %get-tuple-element.30, pred[]{:T(512)S(6)} %eq.3), kind=kLoop, calls=%fused_computation | loop fusion | flops 196608 | bytes 524289 | tf_op jit(solution)/shard_map/jit(_where)/select_n | solution.py:578
  79.5 0.8 copy.13
  80.2 0.8 copy.12
  (30 shorter events, 0.1 us)
Async XLA Ops:
  7.1 5.8 %collective-permute-start.1 = (f32[40,512]{1,0:T(8,128)}, f32[40,512]{1,0:T(8,128)S(1)}, u32[]{:S(2)}, u32[]{:S(2)}) collective-permute-start(f32[40,512]{1,0:T(8,128)} %get-tuple-element.17.refs_0_), channel_id=1, source_target_pairs={{0,2},{2,0},{1,3},{3,1},{4,6},{6,4},{5,7},{7,5},{8,10},{10,8},{9,1... | collective-permute-start | bytes 245768 | tf_op jit(solution)/shard_map/ppermute | solution.py:520
  10.1 4.7 %collective-permute-start.2 = (f32[40,512]{1,0:T(8,128)}, f32[40,512]{1,0:T(8,128)S(1)}, u32[]{:S(2)}, u32[]{:S(2)}) collective-permute-start(f32[40,512]{1,0:T(8,128)} %get-tuple-element.18), channel_id=1, source_target_pairs={{0,3},{1,2},{2,1},{3,0},{4,7},{5,6},{6,5},{7,4},{8,11},{9,10},{10,... | collective-permute-start | bytes 245768 | tf_op jit(solution)/shard_map/ppermute | solution.py:521
  10.1 4.7 %collective-permute-start = (f32[40,512]{1,0:T(8,128)}, f32[40,512]{1,0:T(8,128)S(1)}, u32[]{:S(2)}, u32[]{:S(2)}) collective-permute-start(f32[40,512]{1,0:T(8,128)} %get-tuple-element.18), channel_id=1, source_target_pairs={{0,1},{1,0},{2,3},{3,2},{4,5},{5,4},{6,7},{7,6},{8,9},{9,8},{10,11... | collective-permute-start | bytes 245768 | tf_op jit(solution)/shard_map/ppermute | solution.py:514
  13.0 1.8 %copy-start = (f32[40,512]{1,0:T(8,128)}, f32[40,512]{1,0:T(8,128)S(1)}, u32[]{:S(2)}) copy-start(f32[40,512]{1,0:T(8,128)S(1)} %collective-permute-done.1.refs_2_) | copy-start | bytes 245764
  14.8 0.6 copy-start.1
  15.4 0.6 copy-start.2
  27.4 1.4 %collective-permute-start.3 = (f32[8,128]{1,0:T(8,128)}, f32[8,128]{1,0:T(8,128)S(1)}, u32[]{:S(2)}, u32[]{:S(2)}) collective-permute-start(f32[8,128]{1,0:T(8,128)} %get-tuple-element.19), channel_id=1, source_target_pairs={{0,1},{1,0},{2,3},{3,2},{4,5},{5,4},{6,7},{7,6},{8,9},{9,8},{10,11... | collective-permute-start | bytes 12296 | tf_op jit(solution)/shard_map/ppermute | solution.py:466
  29.5 7.5 %copy-start.4 = (f32[8,128]{1,0:T(8,128)}, f32[8,128]{1,0:T(8,128)S(1)}, u32[]{:S(2)}) copy-start(f32[8,128]{1,0:T(8,128)S(1)} %add.13.refs_0_) | copy-start | bytes 12292
  29.5 4.9 %collective-permute-start.6 = (f32[8,128]{1,0:T(8,128)S(1)}, f32[8,128]{1,0:T(8,128)S(1)}, u32[]{:S(2)}, u32[]{:S(2)}) collective-permute-start(f32[8,128]{1,0:T(8,128)S(1)} %add.13.refs_0_), channel_id=1, source_target_pairs={{0,13},{1,12},{4,9},{5,8},{8,5},{9,4},{12,1},{13,0},{2,15},{3,14},... | collective-permute-start | bytes 12296 | tf_op jit(solution)/shard_map/ppermute | solution.py:476
  33.1 3.9 %collective-permute-start.5 = (f32[8,128]{1,0:T(8,128)S(1)}, f32[8,128]{1,0:T(8,128)S(1)}, u32[]{:S(2)}, u32[]{:S(2)}) collective-permute-start(f32[8,128]{1,0:T(8,128)S(1)} %add.13.refs_0_), channel_id=1, source_target_pairs={{0,9},{1,8},{4,13},{5,12},{8,1},{9,0},{12,5},{13,4},{2,11},{3,10},... | collective-permute-start | bytes 12296 | tf_op jit(solution)/shard_map/ppermute | solution.py:476
  33.1 3.9 %collective-permute-start.4 = (f32[8,128]{1,0:T(8,128)S(1)}, f32[8,128]{1,0:T(8,128)S(1)}, u32[]{:S(2)}, u32[]{:S(2)}) collective-permute-start(f32[8,128]{1,0:T(8,128)S(1)} %add.13.refs_0_), channel_id=1, source_target_pairs={{0,5},{1,4},{4,1},{5,0},{8,13},{9,12},{12,9},{13,8},{2,7},{3,6},{6... | collective-permute-start | bytes 12296 | tf_op jit(solution)/shard_map/ppermute | solution.py:476
  34.4 2.6 %copy-start.7 = (f32[8,128]{1,0:T(8,128)}, f32[8,128]{1,0:T(8,128)S(1)}, u32[]{:S(2)}) copy-start(f32[8,128]{1,0:T(8,128)S(1)} %collective-permute-done.6.refs_3_) | copy-start | bytes 12292
  37.0 0.6 copy-start.9
  37.0 0.6 copy-start.11
  45.9 1.4 %collective-permute-start.7 = (f32[8,128]{1,0:T(8,128)}, f32[8,128]{1,0:T(8,128)S(1)}, u32[]{:S(2)}, u32[]{:S(2)}) collective-permute-start(f32[8,128]{1,0:T(8,128)} %get-tuple-element.25), channel_id=1, source_target_pairs={{0,1},{1,0},{2,3},{3,2},{4,5},{5,4},{6,7},{7,6},{8,9},{9,8},{10,11... | collective-permute-start | bytes 12296 | tf_op jit(solution)/shard_map/ppermute | solution.py:466
  48.0 5.4 %copy-start.3 = (f32[8,128]{1,0:T(8,128)}, f32[8,128]{1,0:T(8,128)S(1)}, u32[]{:S(2)}) copy-start(f32[8,128]{1,0:T(8,128)S(1)} %add.14.refs_0_) | copy-start | bytes 12292
  48.0 4.8 %collective-permute-start.10 = (f32[8,128]{1,0:T(8,128)S(1)}, f32[8,128]{1,0:T(8,128)S(1)}, u32[]{:S(2)}, u32[]{:S(2)}) collective-permute-start(f32[8,128]{1,0:T(8,128)S(1)} %add.14.refs_0_), channel_id=1, source_target_pairs={{0,13},{1,12},{4,9},{5,8},{8,5},{9,4},{12,1},{13,0},{2,15},{3,14},... | collective-permute-start | bytes 12296 | tf_op jit(solution)/shard_map/ppermute | solution.py:476
  49.4 3.9 %collective-permute-start.9 = (f32[8,128]{1,0:T(8,128)S(1)}, f32[8,128]{1,0:T(8,128)S(1)}, u32[]{:S(2)}, u32[]{:S(2)}) collective-permute-start(f32[8,128]{1,0:T(8,128)S(1)} %add.14.refs_0_), channel_id=1, source_target_pairs={{0,9},{1,8},{4,13},{5,12},{8,1},{9,0},{12,5},{13,4},{2,11},{3,10},... | collective-permute-start | bytes 12296 | tf_op jit(solution)/shard_map/ppermute | solution.py:476
  49.7 3.7 %collective-permute-start.8 = (f32[8,128]{1,0:T(8,128)S(1)}, f32[8,128]{1,0:T(8,128)S(1)}, u32[]{:S(2)}, u32[]{:S(2)}) collective-permute-start(f32[8,128]{1,0:T(8,128)S(1)} %add.14.refs_0_), channel_id=1, source_target_pairs={{0,5},{1,4},{4,1},{5,0},{8,13},{9,12},{12,9},{13,8},{2,7},{3,6},{6... | collective-permute-start | bytes 12296 | tf_op jit(solution)/shard_map/ppermute | solution.py:476
  52.8 0.6 copy-start.6
  53.3 0.6 copy-start.8
  53.4 0.6 copy-start.10
  62.3 1.4 %collective-permute-start.11 = (f32[8,128]{1,0:T(8,128)}, f32[8,128]{1,0:T(8,128)S(1)}, u32[]{:S(2)}, u32[]{:S(2)}) collective-permute-start(f32[8,128]{1,0:T(8,128)} %get-tuple-element.27), channel_id=1, source_target_pairs={{0,1},{1,0},{2,3},{3,2},{4,5},{5,4},{6,7},{7,6},{8,9},{9,8},{10,11... | collective-permute-start | bytes 12296 | tf_op jit(solution)/shard_map/ppermute | solution.py:466
  64.4 6.0 %copy-start.5 = (f32[8,128]{1,0:T(8,128)}, f32[8,128]{1,0:T(8,128)S(1)}, u32[]{:S(2)}) copy-start(f32[8,128]{1,0:T(8,128)S(1)} %add.15.refs_0_) | copy-start | bytes 12292
  64.4 4.8 %collective-permute-start.14 = (f32[8,128]{1,0:T(8,128)S(1)}, f32[8,128]{1,0:T(8,128)S(1)}, u32[]{:S(2)}, u32[]{:S(2)}) collective-permute-start(f32[8,128]{1,0:T(8,128)S(1)} %add.15.refs_0_), channel_id=1, source_target_pairs={{0,13},{1,12},{4,9},{5,8},{8,5},{9,4},{12,1},{13,0},{2,15},{3,14},... | collective-permute-start | bytes 12296 | tf_op jit(solution)/shard_map/ppermute | solution.py:476
  66.4 4.0 %collective-permute-start.13 = (f32[8,128]{1,0:T(8,128)S(1)}, f32[8,128]{1,0:T(8,128)S(1)}, u32[]{:S(2)}, u32[]{:S(2)}) collective-permute-start(f32[8,128]{1,0:T(8,128)S(1)} %add.15.refs_0_), channel_id=1, source_target_pairs={{0,9},{1,8},{4,13},{5,12},{8,1},{9,0},{12,5},{13,4},{2,11},{3,10},... | collective-permute-start | bytes 12296 | tf_op jit(solution)/shard_map/ppermute | solution.py:476
  67.3 3.1 %collective-permute-start.12 = (f32[8,128]{1,0:T(8,128)S(1)}, f32[8,128]{1,0:T(8,128)S(1)}, u32[]{:S(2)}, u32[]{:S(2)}) collective-permute-start(f32[8,128]{1,0:T(8,128)S(1)} %add.15.refs_0_), channel_id=1, source_target_pairs={{0,5},{1,4},{4,1},{5,0},{8,13},{9,12},{12,9},{13,8},{2,7},{3,6},{6... | collective-permute-start | bytes 12296 | tf_op jit(solution)/shard_map/ppermute | solution.py:476
  69.2 1.2 %copy-start.12 = (f32[8,128]{1,0:T(8,128)}, f32[8,128]{1,0:T(8,128)S(1)}, u32[]{:S(2)}) copy-start(f32[8,128]{1,0:T(8,128)S(1)} %collective-permute-done.14.refs_3_) | copy-start | bytes 12292
  70.4 0.6 copy-start.13
  70.4 0.6 copy-start.14
  76.9 1.6 %collective-permute-start.15 = (f32[2,2,16,512]{3,2,1,0:T(8,128)}, f32[2,2,16,512]{3,2,1,0:T(8,128)S(1)}, u32[]{:S(2)}, u32[]{:S(2)}) collective-permute-start(f32[2,2,16,512]{3,2,1,0:T(8,128)} %get-tuple-element.31), channel_id=1, source_target_pairs={{0,1},{1,0},{2,3},{3,2},{4,5},{5,4},{6,7},{7,6},{8,9},{9,8},{10,11... | collective-permute-start | bytes 393224 | tf_op jit(solution)/shard_map/ppermute | solution.py:577

commit v2 on v1

--- a/solution.py
+++ b/solution.py
@@ -19,7 +19,6 @@
 step_length = 1.0
 epsilon = 1e-06
 HIGHEST = lax.Precision.HIGHEST
-VMEM_LIMIT = 56 * 1024 * 1024
 
 
 def iota(shape, dim):
@@ -454,7 +453,10 @@
 
 VM = pl.BlockSpec(memory_space=pltpu.VMEM)
 SM = pl.BlockSpec(memory_space=pltpu.SMEM)
-PARAMS = pltpu.CompilerParams(vmem_limit_bytes=VMEM_LIMIT)
+
+
+def params(windows):
+    return pltpu.CompilerParams(vmem_limit_bytes=(16 if windows == 2 else 40) * 1024 * 1024)
 
 
 def shape(*dims, dtype=jnp.float32):
@@ -501,7 +503,7 @@
         out_shape=(payload, payload),
         in_specs=[SM] + [VM] * 5,
         out_specs=(VM, VM),
-        compiler_params=PARAMS,
+        compiler_params=params(windows),
         name="pack",
     )(
         place,
@@ -546,7 +548,7 @@
         scratch_shapes=[pltpu.VMEM((windows, 2, 2 * half + 8, traces), jnp.float32)]
         + scratch
         + [pltpu.VMEM((2, groups, 8, LANES), jnp.float32)],
-        compiler_params=PARAMS,
+        compiler_params=params(windows),
         name="tables",
     )(place, *pays)
 
@@ -560,7 +562,7 @@
             in_specs=[VM] * (len(energies) + 6),
             out_specs=(VM, VM),
             scratch_shapes=[factor_scratch] + scratch,
-            compiler_params=PARAMS,
+            compiler_params=params(windows),
             name="step",
         )(*energies, threshold, updated, cross, inline, observed, mask)
     energies = sum_parts(energy)
@@ -571,7 +573,7 @@
         in_specs=[SM] + [VM] * (len(energies) + 5),
         out_specs=(VM, VM),
         scratch_shapes=[factor_scratch],
-        compiler_params=PARAMS,
+        compiler_params=params(windows),
         name="final",
     )(place, *energies, threshold, updated, cross, inline, matching)
     theirs = lax.ppermute(theirs, "rep", swap)

time: 81.4 us -> 59.7 us (0.73)
  Pallas kernels: 35.5 us -> 21.1 us
  other arithmetic: 3.71 us -> 0.11 us
  local copies, waits for them, and re-layouts: 8.86 us -> 6.02 us
  waiting for transfers between devices: 16.4 us -> 15.3 us
    pallas_call x2, Pallas kernels: 16.6 us -> 9.34 us  [per_device(): pl.pallas_call(functools.partial(step_kernel, windows, nfreq, len(energie...]
    pallas_call x1, Pallas kernels: 5.87 us -> 2.75 us  [per_device(): pl.pallas_call(functools.partial(final_kernel, windows, nfreq, len(energi...]
    pallas_call x1, Pallas kernels: 11.4 us -> 8.41 us  [per_device(): pl.pallas_call(functools.partial(table_kernel, windows, nfreq, amplitude,...]
    unnamed x34 -> x10, local copies, waits for them, and re-layouts: 7.46 us -> 5.21 us
    add x3, other arithmetic: 2.06 us -> 0.01 us  [sum_parts(): energy = energy + lax.ppermute(energy, 'rep', swap)]
    pallas_call x1, Pallas kernels: 1.62 us -> 0.56 us  [per_device(): pl.pallas_call(pack_kernel, out_shape=(payload, payload), in_specs=[SM] +...]
    select_n x1, other arithmetic: 1.01 us -> 0.02 us  [per_device(): jnp.where(rep == 0, jnp.concatenate([mine, theirs], axis=2), jnp.concaten...]
where the time goes in v2:
time: 59.7 us; the launch traced here: 59.4 us
  Pallas kernels  21.1 us (35%)
  starting transfers between devices  16.2 us (27%)
  waiting for transfers between devices  15.3 us (26%)
  local copies, waits for them, and re-layouts  6.02 us (10%)
  between operations  0.71 us (1%)
    ppermute x9, starting transfers between devices, sum_parts(): lax.ppermute(energy, axes, crossed(k))  12 us
    pallas_call x2, Pallas kernels, per_device(): pl.pallas_call(functools.partial(step_kernel, windows, nfreq, len(energie...  9.34 us
    pallas_call x1, Pallas kernels, per_device(): pl.pallas_call(functools.partial(table_kernel, windows, nfreq, amplitude,...  8.41 us
    ppermute x9, waiting for transfers between devices, sum_parts(): lax.ppermute(energy, axes, crossed(k))  6.94 us
    unnamed x10, local copies, waits for them, and re-layouts  5.21 us
    ppermute x3, waiting for transfers between devices, sum_parts(): energy = energy + lax.ppermute(energy, 'rep', swap)  3.01 us
    ppermute x1, starting transfers between devices, per_device(): lax.ppermute(keep, 'win', swap)  3 us
    pallas_call x1, Pallas kernels, per_device(): pl.pallas_call(functools.partial(final_kernel, windows, nfreq, len(energi...  2.75 us
  transfers between devices with their start and end apart: 16, of which 13 were waited for; matrix products, arithmetic and copies ran while one was open for 0% of the time, Pallas kernels for 0%

profile of v2, /device:TPU:0, one launch (start us, length us, event | category | flops | bytes accessed | tf_op | source)
XLA Modules:
  0.0 59.4 jit_solution(6752771662369167728)
XLA Ops:
  0.6 0.7 %copy.19 = f32[2,1,512]{2,0,1:T(2,128)S(1)} copy(f32[2,1,512]{2,1,0:T(1,128)} %param.7) | data formatting | bytes 8192
  1.3 0.8 %copy.11.pattern = s32[32,32]{1,0:T(8,128)S(1)} copy(s32[32,32]{0,1:T(8,128)} %bitcast.22) | data formatting | bytes 8192 | tf_op jit(solution)/shard_map/reshape | solution.py:514
  2.1 0.9 %copy.18 = f32[2,32,1,512]{3,1,2,0:T(8,128)S(1)} copy(f32[2,32,1,512]{3,2,1,0:T(1,128)} %param.6) | data formatting | bytes 262144
  3.0 0.1 pad_add_fusion.place
  3.1 0.0 copy-start.1
  3.1 0.7 %copy-done.1 = s32[1,512]{1,0:T(1,128)S(1)} copy-done((s32[1,512]{1,0:T(1,128)S(1)}, s32[1,512]{1,0:T(1,128)}, u32[]{:S(2)}) %copy-start.1) | copy-done | bytes 2072
  3.8 0.0 copy-start.2
  3.8 0.7 %copy-done.2 = s32[1,1,128]{2,1,0:T(1,128)S(1)} copy-done((s32[1,1,128]{2,1,0:T(1,128)S(1)}, s32[1,1,128]{2,1,0:T(1,128)}, u32[]{:S(2)}) %copy-start.2) | copy-done | bytes 536
  4.5 0.6 pack.1
  5.0 3.0 %collective-permute-start.1 = (f32[40,512]{1,0:T(8,128)S(1)}, f32[40,512]{1,0:T(8,128)S(1)}, u32[]{:S(2)}, u32[]{:S(2)}) collective-permute-start(f32[40,512]{1,0:T(8,128)S(1)} %get-tuple-element.17.refs_0_), channel_id=1, source_target_pairs={{0,2},{2,0},{1,3},{3,1},{4,6},{6,4},{5,7},{7,5},{8,10},{10,8},{9,1... | collective-permute-start | bytes 245768 | tf_op jit(solution)/shard_map/ppermute | solution.py:522
  8.0 0.0 collective-permute-start.2
  8.0 0.2 collective-permute-start
  8.2 2.4 %collective-permute-done.1.refs_2_ = f32[40,512]{1,0:T(8,128)S(1)} collective-permute-done((f32[40,512]{1,0:T(8,128)S(1)}, f32[40,512]{1,0:T(8,128)S(1)}, u32[]{:S(2)}, u32[]{:S(2)}) %collective-permute-start.1) | collective-permute-done | bytes 81952 | tf_op jit(solution)/shard_map/ppermute | solution.py:522
  10.6 1.9 %collective-permute-done.2.refs_3_ = f32[40,512]{1,0:T(8,128)S(1)} collective-permute-done((f32[40,512]{1,0:T(8,128)S(1)}, f32[40,512]{1,0:T(8,128)S(1)}, u32[]{:S(2)}, u32[]{:S(2)}) %collective-permute-start.2) | collective-permute-done | bytes 81952 | tf_op jit(solution)/shard_map/ppermute | solution.py:523
  12.5 0.0 collective-permute-done.refs_1_
  12.5 8.4 %tables.1 = (bf16[2,4,256,1024]{3,2,1,0:T(8,128)(2,1)S(1)}, bf16[2,4,128,1024]{3,2,1,0:T(8,128)(2,1)S(1)}, f32[2,2,4,8,1024]{4,3,2,1,0:T(8,128)S(1)}, f32[2,8,10...) custom-call(s32[3]{0:T(128)S(1)} %pad_add_fusion.place, ...), custom_call_target="tpu_custom_call" | custom-call | tf_op jit(solution)/shard_map/tables/pallas_call | solution.py:535
  20.9 0.1 collective-permute-start.3
  21.0 1.2 %collective-permute-done.3 = f32[8,128]{1,0:T(8,128)S(1)} collective-permute-done((f32[8,128]{1,0:T(8,128)S(1)}, f32[8,128]{1,0:T(8,128)S(1)}, u32[]{:S(2)}, u32[]{:S(2)}) %collective-permute-start.3) | collective-permute-done | bytes 4128 | tf_op jit(solution)/shard_map/ppermute | solution.py:468
  22.2 3.6 %collective-permute-start.6 = (f32[8,128]{1,0:T(8,128)S(1)}, f32[8,128]{1,0:T(8,128)S(1)}, u32[]{:S(2)}, u32[]{:S(2)}) collective-permute-start(f32[8,128]{1,0:T(8,128)S(1)} %add.13.refs_0_), channel_id=1, source_target_pairs={{0,13},{1,12},{4,9},{5,8},{8,5},{9,4},{12,1},{13,0},{2,15},{3,14},... | collective-permute-start | bytes 12296 | tf_op jit(solution)/shard_map/ppermute | solution.py:478
  25.8 0.0 collective-permute-start.5
  25.8 0.5 collective-permute-start.4
  26.3 0.8 %collective-permute-done.6.refs_3_ = f32[8,128]{1,0:T(8,128)S(1)} collective-permute-done((f32[8,128]{1,0:T(8,128)S(1)}, f32[8,128]{1,0:T(8,128)S(1)}, u32[]{:S(2)}, u32[]{:S(2)}) %collective-permute-start.6) | collective-permute-done | bytes 4128 | tf_op jit(solution)/shard_map/ppermute | solution.py:478
  27.1 2.6 %collective-permute-done.5.refs_2_ = f32[8,128]{1,0:T(8,128)S(1)} collective-permute-done((f32[8,128]{1,0:T(8,128)S(1)}, f32[8,128]{1,0:T(8,128)S(1)}, u32[]{:S(2)}, u32[]{:S(2)}) %collective-permute-start.5) | collective-permute-done | bytes 4128 | tf_op jit(solution)/shard_map/ppermute | solution.py:478
  29.7 0.0 collective-permute-done.4.refs_1_
  29.7 0.7 %copy-done = f32[512]{0:T(512)S(1)} copy-done((f32[512]{0:T(512)S(1)}, f32[512]{0:T(512)}, u32[]{:S(2)}) %copy-start) | copy-done | bytes 2072
  30.4 4.7 %step.2 = (f32[2,4,128,128]{3,2,1,0:T(8,128)S(1)}, f32[8,128]{1,0:T(8,128)S(1)}) custom-call(f32[8,128]{1,0:T(8,128)S(1)} %add.13.refs_0_, f32[8,128]{1,0:T(8,128)S(1)} %collective-permute-done.4.refs_1_, f32[8,128]{1,0:T(8,128)S(1)} %collective-permute-done.5.refs_2_, f32[8,128]{1,0:T(8,128)S(1)} %collective-permute-done.6.refs_3_, f32[4,128]{1,0:T(4,128)S(1)} %bitcast.17, ...), custom_call_target="tpu_custom_call" | custom-call | tf_op jit(solution)/shard_map/step/pallas_call | solution.py:559
  35.1 0.4 collective-permute-start.7
  35.5 0.8 %collective-permute-done.7 = f32[8,128]{1,0:T(8,128)S(1)} collective-permute-done((f32[8,128]{1,0:T(8,128)S(1)}, f32[8,128]{1,0:T(8,128)S(1)}, u32[]{:S(2)}, u32[]{:S(2)}) %collective-permute-start.7) | collective-permute-done | bytes 4128 | tf_op jit(solution)/shard_map/ppermute | solution.py:468
  36.3 1.4 %collective-permute-start.10 = (f32[8,128]{1,0:T(8,128)S(1)}, f32[8,128]{1,0:T(8,128)S(1)}, u32[]{:S(2)}, u32[]{:S(2)}) collective-permute-start(f32[8,128]{1,0:T(8,128)S(1)} %add.14.refs_0_), channel_id=1, source_target_pairs={{0,13},{1,12},{4,9},{5,8},{8,5},{9,4},{12,1},{13,0},{2,15},{3,14},... | collective-permute-start | bytes 12296 | tf_op jit(solution)/shard_map/ppermute | solution.py:478
  37.7 0.3 collective-permute-start.9
  38.1 2.3 %collective-permute-start.8 = (f32[8,128]{1,0:T(8,128)S(1)}, f32[8,128]{1,0:T(8,128)S(1)}, u32[]{:S(2)}, u32[]{:S(2)}) collective-permute-start(f32[8,128]{1,0:T(8,128)S(1)} %add.14.refs_0_), channel_id=1, source_target_pairs={{0,5},{1,4},{4,1},{5,0},{8,13},{9,12},{12,9},{13,8},{2,7},{3,6},{6... | collective-permute-start | bytes 12296 | tf_op jit(solution)/shard_map/ppermute | solution.py:478
  40.4 0.8 %collective-permute-done.10.refs_3_ = f32[8,128]{1,0:T(8,128)S(1)} collective-permute-done((f32[8,128]{1,0:T(8,128)S(1)}, f32[8,128]{1,0:T(8,128)S(1)}, u32[]{:S(2)}, u32[]{:S(2)}) %collective-permute-start.10) | collective-permute-done | bytes 4128 | tf_op jit(solution)/shard_map/ppermute | solution.py:478
  41.1 0.5 collective-permute-done.9.refs_2_
  41.6 0.1 collective-permute-done.8.refs_1_
  41.7 4.7 %step.3 = (f32[2,4,128,128]{3,2,1,0:T(8,128)S(1)}, f32[8,128]{1,0:T(8,128)S(1)}) custom-call(f32[8,128]{1,0:T(8,128)S(1)} %add.14.refs_0_, f32[8,128]{1,0:T(8,128)S(1)} %collective-permute-done.8.refs_1_, f32[8,128]{1,0:T(8,128)S(1)} %collective-permute-done.9.refs_2_, f32[8,128]{1,0:T(8,128)S(1)} %collective-permute-done.10.refs_3_, f32[4,128]{1,0:T(4,128)S(1)} %bitcast.18, ...), custom_call_target="tpu_custom_call" | custom-call | tf_op jit(solution)/shard_map/step/pallas_call | solution.py:559
  46.4 0.2 collective-permute-start.11
  46.6 1.0 %collective-permute-done.11 = f32[8,128]{1,0:T(8,128)S(1)} collective-permute-done((f32[8,128]{1,0:T(8,128)S(1)}, f32[8,128]{1,0:T(8,128)S(1)}, u32[]{:S(2)}, u32[]{:S(2)}) %collective-permute-start.11) | collective-permute-done | bytes 4128 | tf_op jit(solution)/shard_map/ppermute | solution.py:468
  47.6 2.1 %collective-permute-start.14 = (f32[8,128]{1,0:T(8,128)S(1)}, f32[8,128]{1,0:T(8,128)S(1)}, u32[]{:S(2)}, u32[]{:S(2)}) collective-permute-start(f32[8,128]{1,0:T(8,128)S(1)} %add.15.refs_0_), channel_id=1, source_target_pairs={{0,13},{1,12},{4,9},{5,8},{8,5},{9,4},{12,1},{13,0},{2,15},{3,14},... | collective-permute-start | bytes 12296 | tf_op jit(solution)/shard_map/ppermute | solution.py:478
  49.7 0.8 %collective-permute-start.13 = (f32[8,128]{1,0:T(8,128)S(1)}, f32[8,128]{1,0:T(8,128)S(1)}, u32[]{:S(2)}, u32[]{:S(2)}) collective-permute-start(f32[8,128]{1,0:T(8,128)S(1)} %add.15.refs_0_), channel_id=1, source_target_pairs={{0,9},{1,8},{4,13},{5,12},{8,1},{9,0},{12,5},{13,4},{2,11},{3,10},... | collective-permute-start | bytes 12296 | tf_op jit(solution)/shard_map/ppermute | solution.py:478
  50.5 1.0 %collective-permute-start.12 = (f32[8,128]{1,0:T(8,128)S(1)}, f32[8,128]{1,0:T(8,128)S(1)}, u32[]{:S(2)}, u32[]{:S(2)}) collective-permute-start(f32[8,128]{1,0:T(8,128)S(1)} %add.15.refs_0_), channel_id=1, source_target_pairs={{0,5},{1,4},{4,1},{5,0},{8,13},{9,12},{12,9},{13,8},{2,7},{3,6},{6... | collective-permute-start | bytes 12296 | tf_op jit(solution)/shard_map/ppermute | solution.py:478
  51.5 0.9 %collective-permute-done.14.refs_3_ = f32[8,128]{1,0:T(8,128)S(1)} collective-permute-done((f32[8,128]{1,0:T(8,128)S(1)}, f32[8,128]{1,0:T(8,128)S(1)}, u32[]{:S(2)}, u32[]{:S(2)}) %collective-permute-start.14) | collective-permute-done | bytes 4128 | tf_op jit(solution)/shard_map/ppermute | solution.py:478
  52.5 1.2 %collective-permute-done.13.refs_2_ = f32[8,128]{1,0:T(8,128)S(1)} collective-permute-done((f32[8,128]{1,0:T(8,128)S(1)}, f32[8,128]{1,0:T(8,128)S(1)}, u32[]{:S(2)}, u32[]{:S(2)}) %collective-permute-start.13) | collective-permute-done | bytes 4128 | tf_op jit(solution)/shard_map/ppermute | solution.py:478
  53.7 0.0 collective-permute-done.12.refs_1_
  53.7 2.7 %final.1 = (f32[2,2,16,512]{3,2,1,0:T(8,128)S(1)}, f32[2,2,16,512]{3,2,1,0:T(8,128)S(1)}) custom-call(s32[3]{0:T(128)S(1)} %pad_add_fusion.place, f32[8,128]{1,0:T(8,128)S(1)} %add.15.refs_0_, f32[8,128]{1,0:T(8,128)S(1)} %collective-permute-done.12.refs_1_, f32[8,128]{1,0:T(8,128)S(1)} %collective-permute-done.13.refs_2_, ...), custom_call_target="tpu_custom_call" | custom-call | tf_op jit(solution)/shard_map/final/pallas_call | solution.py:570
  56.4 0.3 collective-permute-start.15
  56.7 1.0 %collective-permute-done.15 = f32[2,2,16,512]{3,2,1,0:T(8,128)S(1)} collective-permute-done((f32[2,2,16,512]{3,2,1,0:T(8,128)S(1)}, f32[2,2,16,512]{3,2,1,0:T(8,128)S(1)}, u32[]{:S(2)}, u32[]{:S(2)}) %collective-permute-start.15) | collective-permute-done | bytes 131104 | tf_op jit(solution)/shard_map/ppermute | solution.py:579
  57.8 0.8 %copy.13 = f32[2,32,1,512]{3,2,1,0:T(1,128)} copy(f32[2,32,1,512]{3,1,0,2:T(8,128)S(1)} %get-tuple-element.36) | data formatting | bytes 262144
  58.6 0.8 %copy.12 = f32[2,32,1,512]{3,2,1,0:T(1,128)} copy(f32[2,32,1,512]{3,1,0,2:T(8,128)S(1)} %get-tuple-element.37) | data formatting | bytes 262144
  (6 shorter events, 0.1 us)
Async XLA Ops:
  3.1 0.7 %copy-start.1 = (s32[1,512]{1,0:T(1,128)S(1)}, s32[1,512]{1,0:T(1,128)}, u32[]{:S(2)}) copy-start(s32[1,512]{1,0:T(1,128)} %present.1) | copy-start | bytes 6148
  3.8 0.7 %copy-start.2 = (s32[1,1,128]{2,1,0:T(1,128)S(1)}, s32[1,1,128]{2,1,0:T(1,128)}, u32[]{:S(2)}) copy-start(s32[1,1,128]{2,1,0:T(1,128)} %param.9) | copy-start | bytes 1540
  5.0 5.6 %collective-permute-start.1 = (f32[40,512]{1,0:T(8,128)S(1)}, f32[40,512]{1,0:T(8,128)S(1)}, u32[]{:S(2)}, u32[]{:S(2)}) collective-permute-start(f32[40,512]{1,0:T(8,128)S(1)} %get-tuple-element.17.refs_0_), channel_id=1, source_target_pairs={{0,2},{2,0},{1,3},{3,1},{4,6},{6,4},{5,7},{7,5},{8,10},{10,8},{9,1... | collective-permute-start | bytes 245768 | tf_op jit(solution)/shard_map/ppermute | solution.py:522
  8.0 4.5 %collective-permute-start.2 = (f32[40,512]{1,0:T(8,128)S(1)}, f32[40,512]{1,0:T(8,128)S(1)}, u32[]{:S(2)}, u32[]{:S(2)}) collective-permute-start(f32[40,512]{1,0:T(8,128)S(1)} %get-tuple-element.18), channel_id=1, source_target_pairs={{0,3},{1,2},{2,1},{3,0},{4,7},{5,6},{6,5},{7,4},{8,11},{9,10},{10,... | collective-permute-start | bytes 245768 | tf_op jit(solution)/shard_map/ppermute | solution.py:523
  8.0 4.5 %collective-permute-start = (f32[40,512]{1,0:T(8,128)S(1)}, f32[40,512]{1,0:T(8,128)S(1)}, u32[]{:S(2)}, u32[]{:S(2)}) collective-permute-start(f32[40,512]{1,0:T(8,128)S(1)} %get-tuple-element.18), channel_id=1, source_target_pairs={{0,1},{1,0},{2,3},{3,2},{4,5},{5,4},{6,7},{7,6},{8,9},{9,8},{10,11... | collective-permute-start | bytes 245768 | tf_op jit(solution)/shard_map/ppermute | solution.py:516
  20.9 1.2 %collective-permute-start.3 = (f32[8,128]{1,0:T(8,128)S(1)}, f32[8,128]{1,0:T(8,128)S(1)}, u32[]{:S(2)}, u32[]{:S(2)}) collective-permute-start(f32[8,128]{1,0:T(8,128)S(1)} %get-tuple-element.19), channel_id=1, source_target_pairs={{0,1},{1,0},{2,3},{3,2},{4,5},{5,4},{6,7},{7,6},{8,9},{9,8},{10,11... | collective-permute-start | bytes 12296 | tf_op jit(solution)/shard_map/ppermute | solution.py:468
  22.2 4.9 %collective-permute-start.6 = (f32[8,128]{1,0:T(8,128)S(1)}, f32[8,128]{1,0:T(8,128)S(1)}, u32[]{:S(2)}, u32[]{:S(2)}) collective-permute-start(f32[8,128]{1,0:T(8,128)S(1)} %add.13.refs_0_), channel_id=1, source_target_pairs={{0,13},{1,12},{4,9},{5,8},{8,5},{9,4},{12,1},{13,0},{2,15},{3,14},... | collective-permute-start | bytes 12296 | tf_op jit(solution)/shard_map/ppermute | solution.py:478
  25.8 3.9 %collective-permute-start.5 = (f32[8,128]{1,0:T(8,128)S(1)}, f32[8,128]{1,0:T(8,128)S(1)}, u32[]{:S(2)}, u32[]{:S(2)}) collective-permute-start(f32[8,128]{1,0:T(8,128)S(1)} %add.13.refs_0_), channel_id=1, source_target_pairs={{0,9},{1,8},{4,13},{5,12},{8,1},{9,0},{12,5},{13,4},{2,11},{3,10},... | collective-permute-start | bytes 12296 | tf_op jit(solution)/shard_map/ppermute | solution.py:478
  25.8 3.9 %collective-permute-start.4 = (f32[8,128]{1,0:T(8,128)S(1)}, f32[8,128]{1,0:T(8,128)S(1)}, u32[]{:S(2)}, u32[]{:S(2)}) collective-permute-start(f32[8,128]{1,0:T(8,128)S(1)} %add.13.refs_0_), channel_id=1, source_target_pairs={{0,5},{1,4},{4,1},{5,0},{8,13},{9,12},{12,9},{13,8},{2,7},{3,6},{6... | collective-permute-start | bytes 12296 | tf_op jit(solution)/shard_map/ppermute | solution.py:478
  29.7 0.7 %copy-start = (f32[512]{0:T(512)S(1)}, f32[512]{0:T(512)}, u32[]{:S(2)}) copy-start(f32[512]{0:T(512)} %param.11) | copy-start | bytes 6148
  35.1 1.2 %collective-permute-start.7 = (f32[8,128]{1,0:T(8,128)S(1)}, f32[8,128]{1,0:T(8,128)S(1)}, u32[]{:S(2)}, u32[]{:S(2)}) collective-permute-start(f32[8,128]{1,0:T(8,128)S(1)} %get-tuple-element.25), channel_id=1, source_target_pairs={{0,1},{1,0},{2,3},{3,2},{4,5},{5,4},{6,7},{7,6},{8,9},{9,8},{10,11... | collective-permute-start | bytes 12296 | tf_op jit(solution)/shard_map/ppermute | solution.py:468
  36.3 4.8 %collective-permute-start.10 = (f32[8,128]{1,0:T(8,128)S(1)}, f32[8,128]{1,0:T(8,128)S(1)}, u32[]{:S(2)}, u32[]{:S(2)}) collective-permute-start(f32[8,128]{1,0:T(8,128)S(1)} %add.14.refs_0_), channel_id=1, source_target_pairs={{0,13},{1,12},{4,9},{5,8},{8,5},{9,4},{12,1},{13,0},{2,15},{3,14},... | collective-permute-start | bytes 12296 | tf_op jit(solution)/shard_map/ppermute | solution.py:478
  37.7 3.9 %collective-permute-start.9 = (f32[8,128]{1,0:T(8,128)S(1)}, f32[8,128]{1,0:T(8,128)S(1)}, u32[]{:S(2)}, u32[]{:S(2)}) collective-permute-start(f32[8,128]{1,0:T(8,128)S(1)} %add.14.refs_0_), channel_id=1, source_target_pairs={{0,9},{1,8},{4,13},{5,12},{8,1},{9,0},{12,5},{13,4},{2,11},{3,10},... | collective-permute-start | bytes 12296 | tf_op jit(solution)/shard_map/ppermute | solution.py:478
  38.1 3.7 %collective-permute-start.8 = (f32[8,128]{1,0:T(8,128)S(1)}, f32[8,128]{1,0:T(8,128)S(1)}, u32[]{:S(2)}, u32[]{:S(2)}) collective-permute-start(f32[8,128]{1,0:T(8,128)S(1)} %add.14.refs_0_), channel_id=1, source_target_pairs={{0,5},{1,4},{4,1},{5,0},{8,13},{9,12},{12,9},{13,8},{2,7},{3,6},{6... | collective-permute-start | bytes 12296 | tf_op jit(solution)/shard_map/ppermute | solution.py:478
  46.4 1.2 %collective-permute-start.11 = (f32[8,128]{1,0:T(8,128)S(1)}, f32[8,128]{1,0:T(8,128)S(1)}, u32[]{:S(2)}, u32[]{:S(2)}) collective-permute-start(f32[8,128]{1,0:T(8,128)S(1)} %get-tuple-element.27), channel_id=1, source_target_pairs={{0,1},{1,0},{2,3},{3,2},{4,5},{5,4},{6,7},{7,6},{8,9},{9,8},{10,11... | collective-permute-start | bytes 12296 | tf_op jit(solution)/shard_map/ppermute | solution.py:468
  47.6 4.8 %collective-permute-start.14 = (f32[8,128]{1,0:T(8,128)S(1)}, f32[8,128]{1,0:T(8,128)S(1)}, u32[]{:S(2)}, u32[]{:S(2)}) collective-permute-start(f32[8,128]{1,0:T(8,128)S(1)} %add.15.refs_0_), channel_id=1, source_target_pairs={{0,13},{1,12},{4,9},{5,8},{8,5},{9,4},{12,1},{13,0},{2,15},{3,14},... | collective-permute-start | bytes 12296 | tf_op jit(solution)/shard_map/ppermute | solution.py:478
  49.7 4.0 %collective-permute-start.13 = (f32[8,128]{1,0:T(8,128)S(1)}, f32[8,128]{1,0:T(8,128)S(1)}, u32[]{:S(2)}, u32[]{:S(2)}) collective-permute-start(f32[8,128]{1,0:T(8,128)S(1)} %add.15.refs_0_), channel_id=1, source_target_pairs={{0,9},{1,8},{4,13},{5,12},{8,1},{9,0},{12,5},{13,4},{2,11},{3,10},... | collective-permute-start | bytes 12296 | tf_op jit(solution)/shard_map/ppermute | solution.py:478
  50.5 3.1 %collective-permute-start.12 = (f32[8,128]{1,0:T(8,128)S(1)}, f32[8,128]{1,0:T(8,128)S(1)}, u32[]{:S(2)}, u32[]{:S(2)}) collective-permute-start(f32[8,128]{1,0:T(8,128)S(1)} %add.15.refs_0_), channel_id=1, source_target_pairs={{0,5},{1,4},{4,1},{5,0},{8,13},{9,12},{12,9},{13,8},{2,7},{3,6},{6... | collective-permute-start | bytes 12296 | tf_op jit(solution)/shard_map/ppermute | solution.py:478
  56.4 1.4 %collective-permute-start.15 = (f32[2,2,16,512]{3,2,1,0:T(8,128)S(1)}, f32[2,2,16,512]{3,2,1,0:T(8,128)S(1)}, u32[]{:S(2)}, u32[]{:S(2)}) collective-permute-start(f32[2,2,16,512]{3,2,1,0:T(8,128)S(1)} %get-tuple-element.31), channel_id=1, source_target_pairs={{0,1},{1,0},{2,3},{3,2},{4,5},{5,4},{6,7},{7,6},{8,9},{9,8},{10,11... | collective-permute-start | bytes 393224 | tf_op jit(solution)/shard_map/ppermute | solution.py:579

commit v3 on v2

--- a/solution.py
+++ b/solution.py
@@ -54,25 +54,54 @@
     return p[0] * q[0] - p[1] * q[1], p[0] * q[1] + p[1] * q[0]
 
 
-def pack_kernel(place, recorded, geometry, present, intersection, pattern, keep, send):
-    half = recorded.shape[1] // 2
+def pack_kernel(
+    place, recorded, geometry, present, intersection, pattern, keep, send, *scratch
+):
+    sources = (recorded, geometry, present, intersection, pattern)
+    local, sems, turned = scratch[:5], scratch[5], scratch[6]
+    copies = [
+        pltpu.make_async_copy(src, dst, sems.at[n]) for n, (src, dst) in enumerate(zip(sources, local))
+    ]
+    for copy in copies:
+        copy.start()
+    for copy in copies:
+        copy.wait()
+    recorded, geometry, present, intersection, pattern = local
+    frequencies = recorded.shape[1]
+    half = frequencies // 2
     rep = place[1]
+    blocks, span = pattern.shape[:2]
+    for i in range(blocks):
+        turned[span * i : span * (i + 1), :] = pattern[i].astype(jnp.float32)
+    base = 2 * half
     for out, part in ((keep, rep), (send, 1 - rep)):
         for c in range(2):
-            out[c * half : (c + 1) * half, :] = recorded[
-                c, pl.ds(pl.multiple_of(part * half, 8), half), :
-            ]
-        base = 2 * half
+            out[c * half : (c + 1) * half, :] = recorded[c, pl.ds(part * half, half), 0, :]
         out[base : base + 8, :] = jnp.zeros((8, out.shape[1]), jnp.float32)
-        pat = pattern[pl.ds(pl.multiple_of(part * half, 8), half), :].astype(jnp.float32)
+        chosen = iota((half, frequencies), 0) + part * half == iota((half, frequencies), 1)
+        pat = lax.dot_general(
+            chosen.astype(jnp.float32),
+            turned[...],
+            (((1,), (1,)), ((), ())),
+            preferred_element_type=jnp.float32,
+        )
         for h in range(half // 8):
             out[base : base + 8, h * LANES : h * LANES + pat.shape[1]] = pat[8 * h : 8 * h + 8]
         for t in range(4):
             sl = slice(t * LANES, (t + 1) * LANES)
-            out[base + t : base + t + 1, 256:384] = geometry[0:1, sl]
-            out[base + 4 + t : base + 5 + t, 256:384] = geometry[1:2, sl]
-            out[base + t : base + t + 1, 384:512] = present[0:1, sl].astype(jnp.float32)
-        out[base + 4 : base + 5, 384:512] = intersection[...].astype(jnp.float32)
+            out[base + t : base + t + 1, 256:384] = geometry[0, :, sl]
+            out[base + 4 + t : base + 5 + t, 256:384] = geometry[1, :, sl]
+            out[base + t : base + t + 1, 384:512] = present[:, sl].astype(jnp.float32)
+        out[base + 4 : base + 5, 384:512] = intersection[0].astype(jnp.float32)
+
+
+def unpack_kernel(place, mine, theirs, coefficients, reconstruction):
+    rep = place[1]
+    half = mine.shape[2]
+    for n, out in enumerate((coefficients, reconstruction)):
+        for c in range(2):
+            out[c, pl.ds(rep * half, half), 0, :] = mine[n, c]
+            out[c, pl.ds((1 - rep) * half, half), 0, :] = theirs[n, c]
 
 
 def doubled(rows):
@@ -112,65 +141,68 @@
         a_im = inline[w, g, low, sl].astype(jnp.float32)
         rr = jnp.concatenate([r_re, r_re], axis=0)
         ri = jnp.concatenate([r_im, r_im], axis=0)
-        hb[w, rows, sl] = (a_re * rr + a_im * ri).astype(jnp.bfloat16)
-        hb[w, low, sl] = (a_re * ri - a_im * rr).astype(jnp.bfloat16)
-
-
-def pack_energy(acc, energy, windows):
+        hb[rows, sl] = (a_re * rr + a_im * ri).astype(jnp.bfloat16)
+        hb[low, sl] = (a_re * ri - a_im * rr).astype(jnp.bfloat16)
+
+
+def pack_energy(values, energy, row):
     block = iota((16, LANES), 1) // 32
     own = iota((16, LANES), 0) // GROUP
-    for w in range(windows):
-        both = acc[w] + pltpu.roll(acc[w], 32, 1)
-        for j in range(4):
-            rows = jnp.where(block == own, both[16 * j : 16 * j + 16], 0.0)
-            energy[w * 4 + j : w * 4 + j + 1, :] = jnp.sum(rows, axis=0, keepdims=True)
-
-
-def table_kernel(
-    windows, nfreq, amplitude, count, place, *refs
-):
-    pays = refs[:count]
-    cross, inline, observed, mask, matching, updated, energy, pay, hb, acc, weights = refs[count:]
+    both = values + pltpu.roll(values, 32, 1)
+    for j in range(4):
+        rows = jnp.where(block == own, both[16 * j : 16 * j + 16], 0.0)
+        energy[pl.ds(row + j, 1), :] = jnp.sum(rows, axis=0, keepdims=True)
+
+
+def table_kernel(windows, nfreq, amplitude, own, place, *refs):
+    pays, refs = refs[:2], refs[2:]
+    if own:
+        cross, inline, observed, mask, updated, energy, matching = refs[:7]
+        pay, hb, acc, weights = refs[7:]
+    else:
+        cross, inline, observed, mask, updated, energy = refs[6:12]
+        pay, hb, acc, weights = refs[12:]
     win, first = place[0], place[2]
+    many = pay.shape[0]
     half = pay.shape[2] - 8
     freqs = half // 2
     groups = freqs // GROUP
     base = half
-    if count == 4:
+
+    def window(n):
+        return win if own else lax.rem(win + 1 + n, windows)
+
+    for n in range(many):
         for s in range(2):
-            pay[win, s] = pays[s][...]
-            pay[1 - win, s] = pays[2 + s][...]
-    else:
-        for w in range(windows):
-            for s in range(2):
-                pay[w, s] = pays[s][w]
-
-    for s in range(2):
-        index = pay[win, s, base + 4 : base + 5, 384:512].astype(jnp.int32)
-        hot = (iota((LANES, LANES), 0) == index).astype(jnp.float32)
-        eye = (iota((LANES, LANES), 0) == iota((LANES, LANES), 1)).astype(jnp.float32)
-        matching[s] = jnp.where(win > 0, hot, eye)
-    nt = (((1,), (1,)), ((), ()))
+            pay[n, s] = pays[s][...] if pays[s].shape == pay.shape[2:] else pays[s][window(n)]
+
+    def pairing(n, s):
+        index = pay[n, s, base + 4 : base + 5, 384:512].astype(jnp.int32)
+        index = jnp.where(window(n) > 0, index, iota((1, LANES), 1))
+        return (iota((LANES, LANES), 0) == index).astype(jnp.float32)
+
+    if own:
+        for s in range(2):
+            matching[s] = pairing(0, s)
 
     def align(n, _):
-        w, s = 1 + n // 2, n % 2
-        index = pay[w, s, base + 4 : base + 5, 384:512].astype(jnp.int32)
-        hot = (iota((LANES, LANES), 0) == index).astype(jnp.float32)
+        n, s = n // 2, n % 2
+        hot = pairing(n, s)
         dot = functools.partial(
             lax.dot_general,
-            dimension_numbers=nt,
+            dimension_numbers=(((1,), (1,)), ((), ())),
             precision=HIGHEST,
             preferred_element_type=jnp.float32,
         )
-        pay[w, s, 0:half, 0:LANES] = dot(pay[w, s, 0:half, 0:LANES], hot)
-        geo = dot(pay[w, s, base : base + 8, 256:384], hot)
-        pay[w, s, base : base + 1, 256:384] = geo[0:1]
-        pay[w, s, base + 4 : base + 5, 256:384] = geo[4:5]
-        here = dot(pay[w, s, base : base + 8, 384:512], hot)
-        pay[w, s, base : base + 1, 384:512] = here[0:1]
+        pay[n, s, 0:half, 0:LANES] = dot(pay[n, s, 0:half, 0:LANES], hot)
+        geo = dot(pay[n, s, base : base + 8, 256:384], hot)
+        pay[n, s, base : base + 1, 256:384] = geo[0:1]
+        pay[n, s, base + 4 : base + 5, 256:384] = geo[4:5]
+        here = dot(pay[n, s, base : base + 8, 384:512], hot)
+        pay[n, s, base : base + 1, 384:512] = here[0:1]
         return 0
 
-    lax.fori_loop(0, 2 * (windows - 1), align, 0)
+    lax.fori_loop(0, 2 * many, align, 0)
 
     for s in range(2):
         for h in range(freqs // 8):
@@ -187,13 +219,14 @@
     odd_inline = (2 * (2 * (sub // GROUP) - (PX - 1))).astype(jnp.float32)
 
     def strip_tables(n, _):
-        w, s = n // 2, n % 2
+        n, s = n // 2, n % 2
+        w = window(n)
         for t in range(4):
             off = pl.multiple_of(s * 512 + t * LANES, LANES)
             sl = pl.ds(off, LANES)
-            g0 = pay[w, s, base + t : base + t + 1, 256:384]
-            g1 = pay[w, s, base + 4 + t : base + 5 + t, 256:384]
-            here = jnp.broadcast_to(pay[w, s, base + t : base + t + 1, 384:512], (8, LANES))
+            g0 = pay[n, s, base + t : base + t + 1, 256:384]
+            g1 = pay[n, s, base + 4 + t : base + 5 + t, 256:384]
+            here = jnp.broadcast_to(pay[n, s, base + t : base + t + 1, 384:512], (8, LANES))
             mask[w, :, sl] = here
             now = half_turns((scale0 * g1) * odd_cross)
             more = half_turns((delta * g1) * odd_cross)
@@ -241,36 +274,40 @@
                 for t in range(4):
                     sl = pl.ds(pl.multiple_of(s * 512 + t * LANES, LANES), LANES)
                     here = jnp.broadcast_to(
-                        pay[w, s, base + t : base + t + 1, 384:512], (8, LANES)
+                        pay[n, s, base + t : base + t + 1, 384:512], (8, LANES)
                     )
                     rows = here * pay[
-                        w, s, c * freqs + 8 * h : c * freqs + 8 * h + 8, t * LANES : (t + 1) * LANES
+                        n, s, c * freqs + 8 * h : c * freqs + 8 * h + 8, t * LANES : (t + 1) * LANES
                     ]
                     low, high = doubled(rows)
                     observed[c, w, 2 * h, :, sl] = low
                     observed[c, w, 2 * h + 1, :, sl] = high
         return 0
 
-    lax.fori_loop(0, 2 * windows, strip_tables, 0)
+    lax.fori_loop(0, 2 * many, strip_tables, 0)
 
     low_rows, first_lanes, sign = fold_masks()
     rows = PX * GROUP
     acc[...] = jnp.zeros_like(acc)
 
     def first_group(n, _):
-        g, w = n % groups, n // groups
+        g, n = n % groups, n // groups
+        w = window(n)
         for tile in range(8):
             sl = slice(tile * LANES, (tile + 1) * LANES)
-            weigh(inline, w, g, tile, -observed[0, w, g, :, sl], -observed[1, w, g, :, sl], hb)
-        top, bottom = project_group(hb[w], cross[w, g], low_rows, first_lanes, sign)
+            weigh(
+                inline, w, g, tile, -observed[0, w, g, :, sl], -observed[1, w, g, :, sl], hb.at[n]
+            )
+        top, bottom = project_group(hb[n], cross[w, g], low_rows, first_lanes, sign)
         top, bottom = -step_length * top, -step_length * bottom
         updated[w, g, :rows] = top
         updated[w, g, rows:] = bottom
-        acc[w] += top * top
+        acc[n] += top * top
         return 0
 
-    lax.fori_loop(0, windows * groups, first_group, 0)
-    pack_energy(acc, energy, windows)
+    lax.fori_loop(0, many * groups, first_group, 0, unroll=True)
+    for n in range(many):
+        pack_energy(acc[n], energy, window(n) * 4)
 
 
 def spread_factor(energies, threshold, factor, windows, nfreq):
@@ -369,7 +406,7 @@
                 p_re, p_im = predicted[w][tile]
                 r_re = here * p_re - observed[0, w, g, :, sl]
                 r_im = here * p_im - observed[1, w, g, :, sl]
-                weigh(inline, w, g, tile, r_re, r_im, hb)
+                weigh(inline, w, g, tile, r_re, r_im, hb.at[w])
             top, bottom = project_group(hb[w], cross[w, g], low_rows, first_lanes, sign)
             current = scaled(updated, factor, w, g)
             top = current[0] - step_length * top
@@ -379,8 +416,9 @@
             acc[w] += top * top
         return 0
 
-    lax.fori_loop(0, updated.shape[1], one_group, 0)
-    pack_energy(acc, energy, windows)
+    lax.fori_loop(0, updated.shape[1], one_group, 0, unroll=True)
+    for w in range(windows):
+        pack_energy(acc[w], energy, 4 * w)
 
 
 def final_kernel(windows, nfreq, count, place, *refs):
@@ -440,7 +478,7 @@
                 out[1, c, sl, lanes] = jnp.where(low, traces[0][c][t], traces[1][c][t])
         return 0
 
-    lax.fori_loop(0, updated.shape[1] // 2, two_groups, 0)
+    lax.fori_loop(0, updated.shape[1] // 2, two_groups, 0, unroll=True)
     for s, out in enumerate((keep, swap)):
         for c in range(2):
             out[1, c, :, :LANES] = jnp.dot(
@@ -452,6 +490,7 @@
 
 
 VM = pl.BlockSpec(memory_space=pltpu.VMEM)
+HB = pl.BlockSpec(memory_space=pltpu.HBM)
 SM = pl.BlockSpec(memory_space=pltpu.SMEM)
 
 
@@ -498,59 +537,67 @@
     swap = [(0, 1), (1, 0)]
 
     payload = shape(2 * half + 8, traces)
+    turned = jnp.transpose(pattern, (1, 2, 0))
+    sources = (recorded, geometry, present, intersection_index, turned)
     keep, send = pl.pallas_call(
         pack_kernel,
         out_shape=(payload, payload),
-        in_specs=[SM] + [VM] * 5,
+        in_specs=[SM] + [HB] * 5,
         out_specs=(VM, VM),
-        compiler_params=params(windows),
+        scratch_shapes=[pltpu.VMEM(x.shape, x.dtype) for x in sources]
+        + [
+            pltpu.SemaphoreType.DMA((5,)),
+            pltpu.VMEM((turned.shape[0] * turned.shape[1], frequencies), jnp.float32),
+        ],
+        compiler_params=pltpu.CompilerParams(vmem_limit_bytes=60 * 1024 * 1024),
         name="pack",
-    )(
-        place,
-        recorded[:, :, 0, :],
-        geometry[:, 0, :],
-        present,
-        intersection_index[0],
-        pattern.reshape(frequencies, -1),
-    )
+    )(place, *sources)
     received = lax.ppermute(send, "rep", swap)
     if windows == 2:
         diagonal = [(2 * i + r, 2 * (1 - i) + 1 - r) for i in range(2) for r in range(2)]
-        pays = [
-            keep,
-            received,
-            lax.ppermute(keep, "win", swap),
-            lax.ppermute(send, ("win", "rep"), diagonal),
-        ]
+        others = [lax.ppermute(keep, "win", swap), lax.ppermute(send, ("win", "rep"), diagonal)]
     else:
-        pays = [lax.all_gather(keep, "win"), lax.all_gather(received, "win")]
+        others = [lax.all_gather(keep, "win"), lax.all_gather(received, "win")]
 
     rows = 2 * PX * GROUP
     state = shape(windows, groups, rows, LANES)
     energy_shape = shape(4 * windows, LANES)
-    scratch = [
-        pltpu.VMEM((windows, rows, width), jnp.bfloat16),
-        pltpu.VMEM((windows, rows // 2, LANES), jnp.float32),
-    ]
-    cross, inline, observed, mask, matching, updated, energy = pl.pallas_call(
-        functools.partial(table_kernel, windows, nfreq, amplitude, len(pays)),
-        out_shape=(
-            shape(windows, groups, 2 * PY * GROUP, width, dtype=jnp.bfloat16),
-            shape(windows, groups, rows, width, dtype=jnp.bfloat16),
-            shape(2, windows, groups, 8, width),
-            shape(windows, 8, width),
-            shape(2, LANES, LANES),
-            state,
-            energy_shape,
-        ),
-        in_specs=[SM] + [VM] * len(pays),
-        out_specs=(VM,) * 7,
-        scratch_shapes=[pltpu.VMEM((windows, 2, 2 * half + 8, traces), jnp.float32)]
-        + scratch
-        + [pltpu.VMEM((2, groups, 8, LANES), jnp.float32)],
-        compiler_params=params(windows),
-        name="tables",
-    )(place, *pays)
+    tables = (
+        shape(windows, groups, 2 * PY * GROUP, width, dtype=jnp.bfloat16),
+        shape(windows, groups, rows, width, dtype=jnp.bfloat16),
+        shape(2, windows, groups, 8, width),
+        shape(windows, 8, width),
+        state,
+        energy_shape,
+    )
+
+    def scratch(many):
+        return [
+            pltpu.VMEM((many, rows, width), jnp.bfloat16),
+            pltpu.VMEM((many, rows // 2, LANES), jnp.float32),
+        ]
+
+    def build(own, inputs, many):
+        return pl.pallas_call(
+            functools.partial(table_kernel, windows, nfreq, amplitude, own),
+            out_shape=tables + ((shape(2, LANES, LANES),) if own else ()),
+            in_specs=[SM] + [VM] * (len(inputs)),
+            out_specs=(VM,) * (len(tables) + own),
+            scratch_shapes=[pltpu.VMEM((many, 2, 2 * half + 8, traces), jnp.float32)]
+            + scratch(many)
+            + [pltpu.VMEM((2, groups, 8, LANES), jnp.float32)],
+            input_output_aliases={} if own else {3 + n: n for n in range(len(tables))},
+            compiler_params=params(windows),
+            cost_estimate=pl.CostEstimate(flops=4 * 10**9, bytes_accessed=0, transcendentals=0),
+            name="tables",
+        )(place, *inputs)
+
+    *mine, matching = build(True, [keep, received], 1)
+    cross, inline, observed, mask, updated, energy = mine
+    if windows > 1:
+        cross, inline, observed, mask, updated, energy = build(
+            False, others + list(mine), windows - 1
+        )
 
     threshold = group_scale.reshape(4, LANES)
     factor_scratch = pltpu.VMEM((windows, rows // 2, LANES), jnp.float32)
@@ -561,7 +608,7 @@
             out_shape=(state, energy_shape),
             in_specs=[VM] * (len(energies) + 6),
             out_specs=(VM, VM),
-            scratch_shapes=[factor_scratch] + scratch,
+            scratch_shapes=[factor_scratch] + scratch(windows),
             compiler_params=params(windows),
             name="step",
         )(*energies, threshold, updated, cross, inline, observed, mask)
@@ -577,12 +624,15 @@
         name="final",
     )(place, *energies, threshold, updated, cross, inline, matching)
     theirs = lax.ppermute(theirs, "rep", swap)
-    both = jnp.where(
-        rep == 0,
-        jnp.concatenate([mine, theirs], axis=2),
-        jnp.concatenate([theirs, mine], axis=2),
-    )
-    return (both[0][:, :, None, :], both[1][:, :, None, :])
+    out = shape(2, frequencies, 1, traces)
+    return pl.pallas_call(
+        unpack_kernel,
+        out_shape=(out, out),
+        in_specs=[SM, VM, VM],
+        out_specs=(VM, VM),
+        compiler_params=params(windows),
+        name="unpack",
+    )(place, mine, theirs)
 
 
 def solution(mesh):

time: 59.7 us -> 52.7 us (0.88)
  local copies, waits for them, and re-layouts: 6.02 us -> 1.58 us
  waiting for transfers between devices: 15.3 us -> 10.9 us
  Pallas kernels: 21.1 us -> 22 us
    unnamed x10 -> x6, local copies, waits for them, and re-layouts: 5.21 us -> 1.58 us
    ppermute x1, starting transfers between devices: 3 us -> 0.04 us  [per_device(): lax.ppermute(keep, 'win', swap)]
    ppermute x1, starting transfers between devices: 0.01 us -> 2.61 us  [per_device(): lax.ppermute(send, ('win', 'rep'), diagonal)]
    ppermute x1, waiting for transfers between devices: 2.39 us -> 0.01 us  [per_device(): lax.ppermute(keep, 'win', swap)]
    pallas_call x2, Pallas kernels: 9.34 us -> 7.35 us  [per_device(): pl.pallas_call(functools.partial(step_kernel, windows, nfreq, len(energie...]
    ppermute x1, waiting for transfers between devices: 1.9 us -> 0.01 us  [per_device(): lax.ppermute(send, ('win', 'rep'), diagonal)]
    pallas_call x1, Pallas kernels: 0.56 us -> 2.41 us  [per_device(): pl.pallas_call(pack_kernel, out_shape=(payload, payload), in_specs=[SM] +...]
    pallas_call x1 -> x3, Pallas kernels: 8.41 us -> 9.7 us  [the longest x2 8.41 us: build(): pl.pallas_call(functools.partial(table_kernel, windows, nfreq, amplitude,...]
  transfers between devices with their start and end apart: 16 -> 16, of which waited for: 13 -> 11; matrix products, arithmetic and copies ran while one was open for 0% -> 0% of each run, Pallas kernels for 0% -> 8%
where the time goes in v3:
time: 52.7 us; the launch traced here: 52.5 us
  Pallas kernels  22 us (42%)
  starting transfers between devices  16.6 us (31%)
  waiting for transfers between devices  10.9 us (21%)
  local copies, waits for them, and re-layouts  1.58 us (3%)
  between operations  0.72 us (1%)
  other arithmetic  0.68 us (1%)
    ppermute x9, starting transfers between devices, sum_parts(): lax.ppermute(energy, axes, crossed(k))  12.3 us
    pallas_call x2, Pallas kernels, build(): pl.pallas_call(functools.partial(table_kernel, windows, nfreq, amplitude,...  8.41 us
    pallas_call x2, Pallas kernels, per_device(): pl.pallas_call(functools.partial(step_kernel, windows, nfreq, len(energie...  7.35 us
    ppermute x9, waiting for transfers between devices, sum_parts(): lax.ppermute(energy, axes, crossed(k))  6.93 us
    ppermute x3, waiting for transfers between devices, sum_parts(): energy = energy + lax.ppermute(energy, 'rep', swap)  2.92 us
    ppermute x1, starting transfers between devices, per_device(): lax.ppermute(send, ('win', 'rep'), diagonal)  2.61 us
    pallas_call x1, Pallas kernels, per_device(): pl.pallas_call(functools.partial(final_kernel, windows, nfreq, len(energi...  2.54 us
    pallas_call x1, Pallas kernels, per_device(): pl.pallas_call(pack_kernel, out_shape=(payload, payload), in_specs=[SM] +...  2.41 us
  transfers between devices with their start and end apart: 16, of which 11 were waited for; matrix products, arithmetic and copies ran while one was open for 0% of the time, Pallas kernels for 8%

profile of v3, /device:TPU:0, one launch (start us, length us, event | category | flops | bytes accessed | tf_op | source)
XLA Modules:
  0.0 52.5 jit_solution(12804767800942954417)
XLA Ops:
  0.6 0.7 %pad_add_fusion.place = s32[3]{0:T(128)} fusion(s32[1]{0:T(128)} %bitcast.2, s32[1]{0:T(128)} %bitcast.1, s32[1]{0:T(128)} %bitcast), kind=kLoop, calls=%fused_computation | loop fusion | flops 6 | bytes 24 | tf_op jit(solution)/shard_map/stack | solution.py:535
  1.3 2.4 %pack.1 = (f32[40,512]{1,0:T(8,128)}, f32[40,512]{1,0:T(8,128)}) custom-call(s32[3]{0:T(128)} %pad_add_fusion.place, f32[2,32,1,512]{3,2,1,0:T(1,128)} %recorded.1, f32[2,1,512]{2,1,0:T(1,128)} %geometry.1, s32[1,512]{1,0:T(1,128)} %present.1, s32[1,1,128]{2,1,0:T(1,128)} %intersection.1, s32[8,4,32]{2,1,0:T(4,128)} %bitcast.8), custom_call_target="tpu_custom_call" | custom-call | tf_op jit(solution)/shard_map/pack/pallas_call | solution.py:542
  3.7 0.5 collective-permute-start.2
  4.2 2.6 %collective-permute-start.1 = (f32[40,512]{1,0:T(8,128)}, f32[40,512]{1,0:T(8,128)S(1)}, u32[]{:S(2)}, u32[]{:S(2)}) collective-permute-start(f32[40,512]{1,0:T(8,128)} %get-tuple-element.24), channel_id=1, source_target_pairs={{0,3},{1,2},{2,1},{3,0},{4,7},{5,6},{6,5},{7,4},{8,11},{9,10},{10,... | collective-permute-start | bytes 245768 | tf_op jit(solution)/shard_map/ppermute | solution.py:558
  6.9 0.0 collective-permute-start
  6.9 0.0 collective-permute-done.2.refs_1_
  6.9 0.0 copy-start.1
  6.9 0.7 %copy-done.1 = s32[3]{0:T(128)S(1)} copy-done((s32[3]{0:T(128)S(1)}, s32[3]{0:T(128)}, u32[]{:S(2)}) %copy-start.1) | copy-done | bytes 36
  7.6 0.0 copy-start.2
  7.6 0.9 %copy-done.2 = f32[40,512]{1,0:T(8,128)S(1)} copy-done((f32[40,512]{1,0:T(8,128)S(1)}, f32[40,512]{1,0:T(8,128)}, u32[]{:S(2)}) %copy-start.2) | copy-done | bytes 81944
  8.5 4.1 %tables.2 = (bf16[2,4,256,1024]{3,2,1,0:T(8,128)(2,1)S(1)}, bf16[2,4,128,1024]{3,2,1,0:T(8,128)(2,1)S(1)}, f32[2,2,4,8,1024]{4,3,2,1,0:T(8,128)S(1)}, f32[2,8,10...) custom-call(s32[3]{0:T(128)S(1)} %copy-done.1, ...), custom_call_target="tpu_custom_call" | custom-call | flops 4000000000 | tf_op jit(solution)/shard_map/tables/pallas_call | solution.py:581
  12.6 0.0 collective-permute-done.refs_0_
  12.6 0.0 collective-permute-done.1.refs_1_
  12.6 0.0 copy-start
  12.6 4.3 %tables.3 = (bf16[2,4,256,1024]{3,2,1,0:T(8,128)(2,1)S(1)}, bf16[2,4,128,1024]{3,2,1,0:T(8,128)(2,1)S(1)}, f32[2,2,4,8,1024]{4,3,2,1,0:T(8,128)S(1)}, f32[2,8,10...) custom-call(s32[3]{0:T(128)S(1)} %copy-done.1, ...), custom_call_target="tpu_custom_call", output_to_operand_aliasing={{0}: (3, {}), {1}: (4, {}), {2}: (5, {}), {3}: (6, {}), {4}... | custom-call | flops 4000000000 | tf_op jit(solution)/shard_map/tables/pallas_call | solution.py:581
  16.9 0.2 collective-permute-start.3
  17.1 1.1 %collective-permute-done.3 = f32[8,128]{1,0:T(8,128)S(1)} collective-permute-done((f32[8,128]{1,0:T(8,128)S(1)}, f32[8,128]{1,0:T(8,128)S(1)}, u32[]{:S(2)}, u32[]{:S(2)}) %collective-permute-start.3) | collective-permute-done | bytes 4128 | tf_op jit(solution)/shard_map/ppermute | solution.py:507
  18.2 3.9 %collective-permute-start.6 = (f32[8,128]{1,0:T(8,128)S(1)}, f32[8,128]{1,0:T(8,128)S(1)}, u32[]{:S(2)}, u32[]{:S(2)}) collective-permute-start(f32[8,128]{1,0:T(8,128)S(1)} %add.13.refs_0_), channel_id=1, source_target_pairs={{0,13},{1,12},{4,9},{5,8},{8,5},{9,4},{12,1},{13,0},{2,15},{3,14},... | collective-permute-start | bytes 12296 | tf_op jit(solution)/shard_map/ppermute | solution.py:517
  22.0 0.0 collective-permute-start.5
  22.0 0.5 collective-permute-start.4
  22.6 0.8 %collective-permute-done.6.refs_3_ = f32[8,128]{1,0:T(8,128)S(1)} collective-permute-done((f32[8,128]{1,0:T(8,128)S(1)}, f32[8,128]{1,0:T(8,128)S(1)}, u32[]{:S(2)}, u32[]{:S(2)}) %collective-permute-start.6) | collective-permute-done | bytes 4128 | tf_op jit(solution)/shard_map/ppermute | solution.py:517
  23.4 2.6 %collective-permute-done.5.refs_2_ = f32[8,128]{1,0:T(8,128)S(1)} collective-permute-done((f32[8,128]{1,0:T(8,128)S(1)}, f32[8,128]{1,0:T(8,128)S(1)}, u32[]{:S(2)}, u32[]{:S(2)}) %collective-permute-start.5) | collective-permute-done | bytes 4128 | tf_op jit(solution)/shard_map/ppermute | solution.py:517
  26.0 0.0 collective-permute-done.4.refs_1_
  26.0 0.0 copy-done
  26.0 3.7 %step.2 = (f32[2,4,128,128]{3,2,1,0:T(8,128)S(1)}, f32[8,128]{1,0:T(8,128)S(1)}) custom-call(f32[8,128]{1,0:T(8,128)S(1)} %add.13.refs_0_, f32[8,128]{1,0:T(8,128)S(1)} %collective-permute-done.4.refs_1_, f32[8,128]{1,0:T(8,128)S(1)} %collective-permute-done.5.refs_2_, f32[8,128]{1,0:T(8,128)S(1)} %collective-permute-done.6.refs_3_, f32[4,128]{1,0:T(4,128)S(1)} %bitcast.5, ...), custom_call_target="tpu_custom_call" | custom-call | tf_op jit(solution)/shard_map/step/pallas_call | solution.py:606
  29.7 0.4 collective-permute-start.7
  30.1 0.8 %collective-permute-done.7 = f32[8,128]{1,0:T(8,128)S(1)} collective-permute-done((f32[8,128]{1,0:T(8,128)S(1)}, f32[8,128]{1,0:T(8,128)S(1)}, u32[]{:S(2)}, u32[]{:S(2)}) %collective-permute-start.7) | collective-permute-done | bytes 4128 | tf_op jit(solution)/shard_map/ppermute | solution.py:507
  30.9 1.4 %collective-permute-start.10 = (f32[8,128]{1,0:T(8,128)S(1)}, f32[8,128]{1,0:T(8,128)S(1)}, u32[]{:S(2)}, u32[]{:S(2)}) collective-permute-start(f32[8,128]{1,0:T(8,128)S(1)} %add.14.refs_0_), channel_id=1, source_target_pairs={{0,13},{1,12},{4,9},{5,8},{8,5},{9,4},{12,1},{13,0},{2,15},{3,14},... | collective-permute-start | bytes 12296 | tf_op jit(solution)/shard_map/ppermute | solution.py:517
  32.3 0.3 collective-permute-start.9
  32.6 2.3 %collective-permute-start.8 = (f32[8,128]{1,0:T(8,128)S(1)}, f32[8,128]{1,0:T(8,128)S(1)}, u32[]{:S(2)}, u32[]{:S(2)}) collective-permute-start(f32[8,128]{1,0:T(8,128)S(1)} %add.14.refs_0_), channel_id=1, source_target_pairs={{0,5},{1,4},{4,1},{5,0},{8,13},{9,12},{12,9},{13,8},{2,7},{3,6},{6... | collective-permute-start | bytes 12296 | tf_op jit(solution)/shard_map/ppermute | solution.py:517
  35.0 0.8 %collective-permute-done.10.refs_3_ = f32[8,128]{1,0:T(8,128)S(1)} collective-permute-done((f32[8,128]{1,0:T(8,128)S(1)}, f32[8,128]{1,0:T(8,128)S(1)}, u32[]{:S(2)}, u32[]{:S(2)}) %collective-permute-start.10) | collective-permute-done | bytes 4128 | tf_op jit(solution)/shard_map/ppermute | solution.py:517
  35.7 0.5 collective-permute-done.9.refs_2_
  36.3 0.1 collective-permute-done.8.refs_1_
  36.3 3.7 %step.3 = (f32[2,4,128,128]{3,2,1,0:T(8,128)S(1)}, f32[8,128]{1,0:T(8,128)S(1)}) custom-call(f32[8,128]{1,0:T(8,128)S(1)} %add.14.refs_0_, f32[8,128]{1,0:T(8,128)S(1)} %collective-permute-done.8.refs_1_, f32[8,128]{1,0:T(8,128)S(1)} %collective-permute-done.9.refs_2_, f32[8,128]{1,0:T(8,128)S(1)} %collective-permute-done.10.refs_3_, f32[4,128]{1,0:T(4,128)S(1)} %bitcast.6, ...), custom_call_target="tpu_custom_call" | custom-call | tf_op jit(solution)/shard_map/step/pallas_call | solution.py:606
  40.0 0.2 collective-permute-start.11
  40.2 1.0 %collective-permute-done.11 = f32[8,128]{1,0:T(8,128)S(1)} collective-permute-done((f32[8,128]{1,0:T(8,128)S(1)}, f32[8,128]{1,0:T(8,128)S(1)}, u32[]{:S(2)}, u32[]{:S(2)}) %collective-permute-start.11) | collective-permute-done | bytes 4128 | tf_op jit(solution)/shard_map/ppermute | solution.py:507
  41.2 2.1 %collective-permute-start.14 = (f32[8,128]{1,0:T(8,128)S(1)}, f32[8,128]{1,0:T(8,128)S(1)}, u32[]{:S(2)}, u32[]{:S(2)}) collective-permute-start(f32[8,128]{1,0:T(8,128)S(1)} %add.15.refs_0_), channel_id=1, source_target_pairs={{0,13},{1,12},{4,9},{5,8},{8,5},{9,4},{12,1},{13,0},{2,15},{3,14},... | collective-permute-start | bytes 12296 | tf_op jit(solution)/shard_map/ppermute | solution.py:517
  43.3 0.8 %collective-permute-start.13 = (f32[8,128]{1,0:T(8,128)S(1)}, f32[8,128]{1,0:T(8,128)S(1)}, u32[]{:S(2)}, u32[]{:S(2)}) collective-permute-start(f32[8,128]{1,0:T(8,128)S(1)} %add.15.refs_0_), channel_id=1, source_target_pairs={{0,9},{1,8},{4,13},{5,12},{8,1},{9,0},{12,5},{13,4},{2,11},{3,10},... | collective-permute-start | bytes 12296 | tf_op jit(solution)/shard_map/ppermute | solution.py:517
  44.1 1.0 %collective-permute-start.12 = (f32[8,128]{1,0:T(8,128)S(1)}, f32[8,128]{1,0:T(8,128)S(1)}, u32[]{:S(2)}, u32[]{:S(2)}) collective-permute-start(f32[8,128]{1,0:T(8,128)S(1)} %add.15.refs_0_), channel_id=1, source_target_pairs={{0,5},{1,4},{4,1},{5,0},{8,13},{9,12},{12,9},{13,8},{2,7},{3,6},{6... | collective-permute-start | bytes 12296 | tf_op jit(solution)/shard_map/ppermute | solution.py:517
  45.1 0.9 %collective-permute-done.14.refs_3_ = f32[8,128]{1,0:T(8,128)S(1)} collective-permute-done((f32[8,128]{1,0:T(8,128)S(1)}, f32[8,128]{1,0:T(8,128)S(1)}, u32[]{:S(2)}, u32[]{:S(2)}) %collective-permute-start.14) | collective-permute-done | bytes 4128 | tf_op jit(solution)/shard_map/ppermute | solution.py:517
  46.1 1.2 %collective-permute-done.13.refs_2_ = f32[8,128]{1,0:T(8,128)S(1)} collective-permute-done((f32[8,128]{1,0:T(8,128)S(1)}, f32[8,128]{1,0:T(8,128)S(1)}, u32[]{:S(2)}, u32[]{:S(2)}) %collective-permute-start.13) | collective-permute-done | bytes 4128 | tf_op jit(solution)/shard_map/ppermute | solution.py:517
  47.3 0.0 collective-permute-done.12.refs_1_
  47.3 2.5 %final.1 = (f32[2,2,16,512]{3,2,1,0:T(8,128)S(1)}, f32[2,2,16,512]{3,2,1,0:T(8,128)S(1)}) custom-call(s32[3]{0:T(128)S(1)} %copy-done.1, f32[8,128]{1,0:T(8,128)S(1)} %add.15.refs_0_, f32[8,128]{1,0:T(8,128)S(1)} %collective-permute-done.12.refs_1_, f32[8,128]{1,0:T(8,128)S(1)} %collective-permute-done.13.refs_2_, ...), custom_call_target="tpu_custom_call" | custom-call | tf_op jit(solution)/shard_map/final/pallas_call | solution.py:617
  49.8 0.3 collective-permute-start.15
  50.1 1.0 %collective-permute-done.15.theirs = f32[2,2,16,512]{3,2,1,0:T(8,128)S(1)} collective-permute-done((f32[2,2,16,512]{3,2,1,0:T(8,128)S(1)}, f32[2,2,16,512]{3,2,1,0:T(8,128)S(1)}, u32[]{:S(2)}, u32[]{:S(2)}) %collective-permute-start.15) | collective-permute-done | bytes 131104 | tf_op jit(solution)/shard_map/ppermute | solution.py:626
  51.2 1.3 %unpack.1 = (f32[2,32,1,512]{3,2,1,0:T(1,128)}, f32[2,32,1,512]{3,2,1,0:T(1,128)}) custom-call(s32[3]{0:T(128)S(1)} %copy-done.1, f32[2,2,16,512]{3,2,1,0:T(8,128)S(1)} %get-tuple-element.42.mine, f32[2,2,16,512]{3,2,1,0:T(8,128)S(1)} %collective-permute-done.15.theirs), custom_call_target="tpu_custom_call" | custom-call | tf_op jit(solution)/shard_map/unpack/pallas_call | solution.py:628
  (3 shorter events, 0.0 us)
Async XLA Ops:
  3.7 3.2 %collective-permute-start.2 = (f32[40,512]{1,0:T(8,128)}, f32[40,512]{1,0:T(8,128)S(1)}, u32[]{:S(2)}, u32[]{:S(2)}) collective-permute-start(f32[40,512]{1,0:T(8,128)} %get-tuple-element.24), channel_id=1, source_target_pairs={{0,1},{1,0},{2,3},{3,2},{4,5},{5,4},{6,7},{7,6},{8,9},{9,8},{10,11... | collective-permute-start | bytes 245768 | tf_op jit(solution)/shard_map/ppermute | solution.py:555
  4.2 8.4 %collective-permute-start.1 = (f32[40,512]{1,0:T(8,128)}, f32[40,512]{1,0:T(8,128)S(1)}, u32[]{:S(2)}, u32[]{:S(2)}) collective-permute-start(f32[40,512]{1,0:T(8,128)} %get-tuple-element.24), channel_id=1, source_target_pairs={{0,3},{1,2},{2,1},{3,0},{4,7},{5,6},{6,5},{7,4},{8,11},{9,10},{10,... | collective-permute-start | bytes 245768 | tf_op jit(solution)/shard_map/ppermute | solution.py:558
  6.9 5.8 %collective-permute-start = (f32[40,512]{1,0:T(8,128)}, f32[40,512]{1,0:T(8,128)S(1)}, u32[]{:S(2)}, u32[]{:S(2)}) collective-permute-start(f32[40,512]{1,0:T(8,128)} %get-tuple-element.23.refs_0_), channel_id=1, source_target_pairs={{0,2},{2,0},{1,3},{3,1},{4,6},{6,4},{5,7},{7,5},{8,10},{10,8},{9,1... | collective-permute-start | bytes 245768 | tf_op jit(solution)/shard_map/ppermute | solution.py:558
  6.9 0.7 %copy-start.1 = (s32[3]{0:T(128)S(1)}, s32[3]{0:T(128)}, u32[]{:S(2)}) copy-start(s32[3]{0:T(128)} %pad_add_fusion.place) | copy-start | bytes 40
  7.6 0.9 %copy-start.2 = (f32[40,512]{1,0:T(8,128)S(1)}, f32[40,512]{1,0:T(8,128)}, u32[]{:S(2)}) copy-start(f32[40,512]{1,0:T(8,128)} %get-tuple-element.23.refs_0_) | copy-start | bytes 245764
  12.6 13.4 %copy-start = (f32[512]{0:T(512)S(1)}, f32[512]{0:T(512)}, u32[]{:S(2)}) copy-start(f32[512]{0:T(512)} %param.11) | copy-start | bytes 6148
  16.9 1.2 %collective-permute-start.3 = (f32[8,128]{1,0:T(8,128)S(1)}, f32[8,128]{1,0:T(8,128)S(1)}, u32[]{:S(2)}, u32[]{:S(2)}) collective-permute-start(f32[8,128]{1,0:T(8,128)S(1)} %get-tuple-element.31), channel_id=1, source_target_pairs={{0,1},{1,0},{2,3},{3,2},{4,5},{5,4},{6,7},{7,6},{8,9},{9,8},{10,11... | collective-permute-start | bytes 12296 | tf_op jit(solution)/shard_map/ppermute | solution.py:507
  18.2 5.2 %collective-permute-start.6 = (f32[8,128]{1,0:T(8,128)S(1)}, f32[8,128]{1,0:T(8,128)S(1)}, u32[]{:S(2)}, u32[]{:S(2)}) collective-permute-start(f32[8,128]{1,0:T(8,128)S(1)} %add.13.refs_0_), channel_id=1, source_target_pairs={{0,13},{1,12},{4,9},{5,8},{8,5},{9,4},{12,1},{13,0},{2,15},{3,14},... | collective-permute-start | bytes 12296 | tf_op jit(solution)/shard_map/ppermute | solution.py:517
  22.0 3.9 %collective-permute-start.5 = (f32[8,128]{1,0:T(8,128)S(1)}, f32[8,128]{1,0:T(8,128)S(1)}, u32[]{:S(2)}, u32[]{:S(2)}) collective-permute-start(f32[8,128]{1,0:T(8,128)S(1)} %add.13.refs_0_), channel_id=1, source_target_pairs={{0,9},{1,8},{4,13},{5,12},{8,1},{9,0},{12,5},{13,4},{2,11},{3,10},... | collective-permute-start | bytes 12296 | tf_op jit(solution)/shard_map/ppermute | solution.py:517
  22.0 3.9 %collective-permute-start.4 = (f32[8,128]{1,0:T(8,128)S(1)}, f32[8,128]{1,0:T(8,128)S(1)}, u32[]{:S(2)}, u32[]{:S(2)}) collective-permute-start(f32[8,128]{1,0:T(8,128)S(1)} %add.13.refs_0_), channel_id=1, source_target_pairs={{0,5},{1,4},{4,1},{5,0},{8,13},{9,12},{12,9},{13,8},{2,7},{3,6},{6... | collective-permute-start | bytes 12296 | tf_op jit(solution)/shard_map/ppermute | solution.py:517
  29.7 1.2 %collective-permute-start.7 = (f32[8,128]{1,0:T(8,128)S(1)}, f32[8,128]{1,0:T(8,128)S(1)}, u32[]{:S(2)}, u32[]{:S(2)}) collective-permute-start(f32[8,128]{1,0:T(8,128)S(1)} %get-tuple-element.37), channel_id=1, source_target_pairs={{0,1},{1,0},{2,3},{3,2},{4,5},{5,4},{6,7},{7,6},{8,9},{9,8},{10,11... | collective-permute-start | bytes 12296 | tf_op jit(solution)/shard_map/ppermute | solution.py:507
  30.9 4.8 %collective-permute-start.10 = (f32[8,128]{1,0:T(8,128)S(1)}, f32[8,128]{1,0:T(8,128)S(1)}, u32[]{:S(2)}, u32[]{:S(2)}) collective-permute-start(f32[8,128]{1,0:T(8,128)S(1)} %add.14.refs_0_), channel_id=1, source_target_pairs={{0,13},{1,12},{4,9},{5,8},{8,5},{9,4},{12,1},{13,0},{2,15},{3,14},... | collective-permute-start | bytes 12296 | tf_op jit(solution)/shard_map/ppermute | solution.py:517
  32.3 3.9 %collective-permute-start.9 = (f32[8,128]{1,0:T(8,128)S(1)}, f32[8,128]{1,0:T(8,128)S(1)}, u32[]{:S(2)}, u32[]{:S(2)}) collective-permute-start(f32[8,128]{1,0:T(8,128)S(1)} %add.14.refs_0_), channel_id=1, source_target_pairs={{0,9},{1,8},{4,13},{5,12},{8,1},{9,0},{12,5},{13,4},{2,11},{3,10},... | collective-permute-start | bytes 12296 | tf_op jit(solution)/shard_map/ppermute | solution.py:517
  32.6 3.7 %collective-permute-start.8 = (f32[8,128]{1,0:T(8,128)S(1)}, f32[8,128]{1,0:T(8,128)S(1)}, u32[]{:S(2)}, u32[]{:S(2)}) collective-permute-start(f32[8,128]{1,0:T(8,128)S(1)} %add.14.refs_0_), channel_id=1, source_target_pairs={{0,5},{1,4},{4,1},{5,0},{8,13},{9,12},{12,9},{13,8},{2,7},{3,6},{6... | collective-permute-start | bytes 12296 | tf_op jit(solution)/shard_map/ppermute | solution.py:517
  40.0 1.2 %collective-permute-start.11 = (f32[8,128]{1,0:T(8,128)S(1)}, f32[8,128]{1,0:T(8,128)S(1)}, u32[]{:S(2)}, u32[]{:S(2)}) collective-permute-start(f32[8,128]{1,0:T(8,128)S(1)} %get-tuple-element.39), channel_id=1, source_target_pairs={{0,1},{1,0},{2,3},{3,2},{4,5},{5,4},{6,7},{7,6},{8,9},{9,8},{10,11... | collective-permute-start | bytes 12296 | tf_op jit(solution)/shard_map/ppermute | solution.py:507
  41.2 4.8 %collective-permute-start.14 = (f32[8,128]{1,0:T(8,128)S(1)}, f32[8,128]{1,0:T(8,128)S(1)}, u32[]{:S(2)}, u32[]{:S(2)}) collective-permute-start(f32[8,128]{1,0:T(8,128)S(1)} %add.15.refs_0_), channel_id=1, source_target_pairs={{0,13},{1,12},{4,9},{5,8},{8,5},{9,4},{12,1},{13,0},{2,15},{3,14},... | collective-permute-start | bytes 12296 | tf_op jit(solution)/shard_map/ppermute | solution.py:517
  43.3 4.0 %collective-permute-start.13 = (f32[8,128]{1,0:T(8,128)S(1)}, f32[8,128]{1,0:T(8,128)S(1)}, u32[]{:S(2)}, u32[]{:S(2)}) collective-permute-start(f32[8,128]{1,0:T(8,128)S(1)} %add.15.refs_0_), channel_id=1, source_target_pairs={{0,9},{1,8},{4,13},{5,12},{8,1},{9,0},{12,5},{13,4},{2,11},{3,10},... | collective-permute-start | bytes 12296 | tf_op jit(solution)/shard_map/ppermute | solution.py:517
  44.1 3.1 %collective-permute-start.12 = (f32[8,128]{1,0:T(8,128)S(1)}, f32[8,128]{1,0:T(8,128)S(1)}, u32[]{:S(2)}, u32[]{:S(2)}) collective-permute-start(f32[8,128]{1,0:T(8,128)S(1)} %add.15.refs_0_), channel_id=1, source_target_pairs={{0,5},{1,4},{4,1},{5,0},{8,13},{9,12},{12,9},{13,8},{2,7},{3,6},{6... | collective-permute-start | bytes 12296 | tf_op jit(solution)/shard_map/ppermute | solution.py:517
  49.8 1.4 %collective-permute-start.15 = (f32[2,2,16,512]{3,2,1,0:T(8,128)S(1)}, f32[2,2,16,512]{3,2,1,0:T(8,128)S(1)}, u32[]{:S(2)}, u32[]{:S(2)}) collective-permute-start(f32[2,2,16,512]{3,2,1,0:T(8,128)S(1)} %get-tuple-element.43), channel_id=1, source_target_pairs={{0,1},{1,0},{2,3},{3,2},{4,5},{5,4},{6,7},{7,6},{8,9},{9,8},{10,11... | collective-permute-start | bytes 393224 | tf_op jit(solution)/shard_map/ppermute | solution.py:626

commit v4 on v3

v4 whole, which is shorter than its diff:
```python
import functools
import math

import jax
import jax.numpy as jnp
from jax import lax
from jax.experimental import pallas as pl
from jax.experimental.pallas import tpu as pltpu
from jax.sharding import PartitionSpec as P

PX = 16
PY = 32
SPB = 64
OBS = 128
ITERS = 3
LANES = 128
GROUP = 8
HALF = PX * GROUP
FOLD = PY // 2
SPAN = 2 * FOLD

step_length = 1.0
epsilon = 1e-06
HIGHEST = lax.Precision.HIGHEST


def iota(shape, dim):
    return lax.broadcasted_iota(jnp.int32, shape, dim)


def half_turns(y):
    quarter = jnp.floor(2.0 * y + 0.5)
    r = y - 0.5 * quarter
    q = quarter.astype(jnp.int32)
    r2 = r * r
    pi = math.pi
    sine = r * (
        pi
        + r2
        * (
            -(pi**3) / 6
            + r2 * (pi**5 / 120 + r2 * (-(pi**7) / 5040 + r2 * (pi**9 / 362880)))
        )
    )
    cosine = 1.0 + r2 * (
        -(pi**2) / 2 + r2 * (pi**4 / 24 + r2 * (-(pi**6) / 720 + r2 * (pi**8 / 40320)))
    )
    odd = (q & 1) == 1
    c = jnp.where(odd, sine, cosine)
    s = jnp.where(odd, cosine, sine)
    c = jnp.where(((q + 1) & 2) != 0, -c, c)
    s = jnp.where((q & 2) != 0, s, -s)
    return c, s


def rounded(x):
    return x.astype(jnp.bfloat16).astype(jnp.float32)


def times(p, q):
    return p[0] * q[0] - p[1] * q[1], p[0] * q[1] + p[1] * q[0]


def pack_kernel(
    recorded, geometry, present, intersection, pattern, keep, send, *scratch
):
    sources = (recorded, geometry, present, intersection, pattern)
    local, sems, turned = scratch[:5], scratch[5], scratch[6]
    copies = [
        pltpu.make_async_copy(src, dst, sems.at[n]) for n, (src, dst) in enumerate(zip(sources, local))
    ]
    for copy in copies:
        copy.start()
    for copy in copies:
        copy.wait()
    recorded, geometry, present, intersection, pattern = local
    frequencies = recorded.shape[1]
    half = frequencies // 2
    rep = lax.axis_index("rep")
    blocks, span = pattern.shape[:2]
    for i in range(blocks):
        turned[span * i : span * (i + 1), :] = pattern[i].astype(jnp.float32)
    base = 2 * half
    for out, part in ((keep, rep), (send, 1 - rep)):
        for c in range(2):
            out[c * half : (c + 1) * half, :] = recorded[c, pl.ds(part * half, half), 0, :]
        out[base : base + 8, :] = jnp.zeros((8, out.shape[1]), jnp.float32)
        chosen = iota((half, frequencies), 0) + part * half == iota((half, frequencies), 1)
        pat = lax.dot_general(
            chosen.astype(jnp.float32),
            turned[...],
            (((1,), (1,)), ((), ())),
            preferred_element_type=jnp.float32,
        )
        for h in range(half // 8):
            out[base : base + 8, h * LANES : h * LANES + pat.shape[1]] = pat[8 * h : 8 * h + 8]
        for t in range(4):
            sl = slice(t * LANES, (t + 1) * LANES)
            out[base + t : base + t + 1, 256:384] = geometry[0, :, sl]
            out[base + 4 + t : base + 5 + t, 256:384] = geometry[1, :, sl]
            out[base + t : base + t + 1, 384:512] = present[:, sl].astype(jnp.float32)
        out[base + 4 : base + 5, 384:512] = intersection[0].astype(jnp.float32)


def unpack_kernel(mine, theirs, coefficients, reconstruction):
    rep = lax.axis_index("rep")
    half = mine.shape[2]
    for n, out in enumerate((coefficients, reconstruction)):
        for c in range(2):
            out[c, pl.ds(rep * half, half), 0, :] = mine[n, c]
            out[c, pl.ds((1 - rep) * half, half), 0, :] = theirs[n, c]


def low_half(dims):
    return (iota(dims, 1) // FOLD) % 2 == 0


def swapped(values):
    return pltpu.roll(values, FOLD, 1)


def side_by_side(ref, w, g, first, count):
    return jnp.concatenate([ref[w][g, first + n] for n in range(count)], axis=1)


def project_group(hb, cross, w, g, masks, sign):
    tiles = hb.shape[0]
    g = lax.dot_general(
        jnp.concatenate([hb[n] for n in range(tiles)], axis=1),
        side_by_side(cross, w, g, 0, tiles),
        (((1,), (1,)), ((), ())),
        preferred_element_type=jnp.float32,
    )
    g = jnp.where(masks[0], g[:, :LANES], jnp.where(masks[1], g[:, LANES:], 0.0))
    g = g + pltpu.roll(g, 32, 1)
    g = g + pltpu.roll(g, 64, 1)
    top, bottom = g[:HALF], sign * swapped(g[HALF:])
    return top + bottom, top - bottom


def group_masks():
    rows = iota((2 * HALF, LANES), 0) % GROUP
    lanes = iota((2 * HALF, LANES), 1) // SPAN
    return rows == lanes, rows == lanes + 4


def half_sign():
    return jnp.where(low_half((HALF, LANES)), 1.0, -1.0)


def weigh(inline, g, tile, r_re, r_im, hb):
    sl = pl.ds(tile * LANES, LANES)
    for i in range(HALF // 16):
        rows = slice(16 * i, 16 * i + 16)
        low = slice(HALF + 16 * i, HALF + 16 * i + 16)
        a_re = inline[g, rows, sl]
        a_im = inline[g, low, sl]
        rr = jnp.concatenate([r_re, r_re], axis=0)
        ri = jnp.concatenate([r_im, r_im], axis=0)
        hb[tile, rows, :] = (a_re * rr + a_im * ri).astype(jnp.bfloat16)
        hb[tile, low, :] = (a_re * ri - a_im * rr).astype(jnp.bfloat16)


def pack_energy(values, energy, row):
    both = values + swapped(values)
    both = jnp.where(low_half((HALF, LANES)), both[:HALF], both[HALF:])
    block = iota((GROUP, LANES), 1) // SPAN
    for j in range(4):
        total = None
        for q in range(4):
            a = 4 * j + q
            part = jnp.where(block == q, both[GROUP * a : GROUP * (a + 1)], 0.0)
            total = part if total is None else total + part
        energy[pl.ds(row + j, 1), :] = jnp.sum(total, axis=0, keepdims=True)


def table_kernel(windows, nfreq, amplitude, own, *refs):
    pays, refs = refs[:2], refs[2:]
    extra, refs = refs[0], refs[1:]
    cross, inline, observed, mask, updated, energy, *refs = refs
    if own:
        matching, threshold, pay, hb, acc = refs
        lane = iota((LANES, LANES), 1)
        at = lane % SPAN
        source = jnp.where(at < FOLD, lane, lane + PY - 1 + FOLD - 2 * at)
        order = (iota((LANES, LANES), 0) == source).astype(jnp.float32)
        threshold[...] = jnp.dot(
            extra[...], order, precision=HIGHEST, preferred_element_type=jnp.float32
        )
    else:
        pay, hb, acc = refs
        energy[0:4, :] = extra[...]
    many = pay.shape[0]
    half = pay.shape[2] - 8
    freqs = half // 2
    win = lax.axis_index("win")
    first = (2 * lax.axis_index("freq") + lax.axis_index("rep")) * freqs
    groups = freqs // GROUP
    base = half

    def window(n):
        return win if own else lax.rem(win + 1 + n, windows)

    for n in range(many):
        for s in range(2):
            pay[n, s] = pays[s][...] if pays[s].shape == pay.shape[2:] else pays[s][window(n)]

    def pairing(n, s):
        index = pay[n, s, base + 4 : base + 5, 384:512].astype(jnp.int32)
        index = jnp.where(window(n) > 0, index, iota((1, LANES), 1))
        return (iota((LANES, LANES), 0) == index).astype(jnp.float32)

    if own:
        for s in range(2):
            matching[s] = pairing(0, s)

    def align(n, _):
        n, s = n // 2, n % 2
        hot = pairing(n, s)
        dot = functools.partial(
            lax.dot_general,
            dimension_numbers=(((1,), (1,)), ((), ())),
            precision=HIGHEST,
            preferred_element_type=jnp.float32,
        )
        pay[n, s, 0:half, 0:LANES] = dot(pay[n, s, 0:half, 0:LANES], hot)
        geo = dot(pay[n, s, base : base + 8, 256:384], hot)
        pay[n, s, base : base + 1, 256:384] = geo[0:1]
        pay[n, s, base + 4 : base + 5, 256:384] = geo[4:5]
        here = dot(pay[n, s, base : base + 8, 384:512], hot)
        pay[n, s, base : base + 1, 384:512] = here[0:1]
        return 0

    lax.fori_loop(0, 2 * many, align, 0)

    sub = iota((8, LANES), 0)
    delta = 0.75 / nfreq
    start = first.astype(jnp.float32)
    scale0 = 0.25 + 0.75 * ((start + 0.5) / nfreq)
    odd_cross = (2 * sub - (PY - 1)).astype(jnp.float32)

    def strip_tables(n, _):
        n, s = n // 2, n % 2
        for t in range(4):
            off = pl.multiple_of(s * 512 + t * LANES, LANES)
            sl = pl.ds(off, LANES)
            g0 = pay[n, s, base + t : base + t + 1, 256:384]
            g1 = pay[n, s, base + 4 + t : base + 5 + t, 256:384]
            here = jnp.broadcast_to(pay[n, s, base + t : base + t + 1, 384:512], (8, LANES))
            mask[n, :, sl] = here
            now = half_turns((scale0 * g1) * odd_cross)
            more = half_turns((delta * g1) * odd_cross)
            g1b = jnp.broadcast_to(g1, (8, LANES))
            rot = half_turns((scale0 * g1b) * 16.0)
            rot_more = half_turns((delta * g1b) * 16.0)
            for f in range(freqs):
                v0 = now
                v1 = times(v0, rot)
                row = (f % GROUP) * SPAN
                for part in range(2):
                    cross[n, f // GROUP, 4 * s + t, row + FOLD * part : row + FOLD * (part + 1), :] = (
                        jnp.concatenate([v0[part], v1[part]], axis=0).astype(jnp.bfloat16)
                    )
                if f + 1 < freqs:
                    now = times(now, more)
                    rot = times(rot, rot_more)
            for g in range(groups):
                level = start + (sub + g * GROUP).astype(jnp.float32)
                scale = 0.25 + 0.75 * ((level + 0.5) / nfreq)
                v = half_turns((scale * g0) * 2.0)
                rot = half_turns((scale * g0) * 4.0)
                v = (v[0] * amplitude, v[1] * amplitude)
                for a in range(PX // 2, PX, 2):
                    u = times(v, rot)
                    i, mirror = a // 2, (PX - 1 - a) // 2
                    lane = g * LANES + t
                    col = pay[n, s, base : base + 8, lane + 4 * i : lane + 4 * i + 1]
                    other = pay[n, s, base : base + 8, lane + 4 * mirror : lane + 4 * mirror + 1]
                    low = GROUP * (PX - 2 - a)
                    for part in range(2):
                        row = part * HALF
                        inline[n, g, row + GROUP * a : row + GROUP * (a + 2), sl] = (
                            rounded(jnp.concatenate([v[part] * col, u[part] * col], axis=0))
                        )
                        turn = -other if part else other
                        inline[n, g, row + low : row + low + 2 * GROUP, sl] = (
                            rounded(jnp.concatenate([u[part] * turn, v[part] * turn], axis=0))
                        )
                    if a + 2 < PX:
                        v = times(u, rot)
            for c in range(2):
                for g in range(groups):
                    row = c * freqs + GROUP * g
                    observed[n, c, g, :, sl] = (
                        here * pay[n, s, row : row + GROUP, t * LANES : (t + 1) * LANES]
                    )
        return 0

    lax.fori_loop(0, 2 * many, strip_tables, 0)

    masks, sign = group_masks(), half_sign()
    acc[...] = jnp.zeros_like(acc)

    def first_group(k, _):
        g, n = k % groups, k // groups
        buffer = hb.at[k % hb.shape[0]]
        for tile in range(8):
            sl = slice(tile * LANES, (tile + 1) * LANES)
            r_re, r_im = -observed[n, 0, g, :, sl], -observed[n, 1, g, :, sl]
            weigh(inline.at[n], g, tile, r_re, r_im, buffer)
        slopes = project_group(buffer, [cross.at[n]], 0, g, masks, sign)
        for part, slope in enumerate(slopes):
            rows = slice(part * HALF, (part + 1) * HALF)
            value = -step_length * slope
            updated[n, g, rows] = value
            acc[n, rows] += value * value
        return 0

    lax.fori_loop(0, many * groups, first_group, 0, unroll=True)
    for n in range(many):
        pack_energy(acc[n], energy, 4 * (n + (not own)))


def spread_factor(energies, threshold, factor, windows, nfreq):
    total = energies[0][...]
    for e in energies[1:]:
        total = total + e[...]
    limit = jnp.concatenate([threshold[...]] * windows, axis=0)
    packed = jnp.maximum(0.0, 1.0 - limit / jnp.sqrt(total / nfreq + epsilon))
    block = iota((8, LANES), 1) // SPAN
    low = low_half((8, LANES))
    for w in range(windows):
        for a in range(PX):
            row = w * 4 + a // 4
            y = jnp.where(block == a % 4, jnp.broadcast_to(packed[row : row + 1], (8, LANES)), 0.0)
            y = y + pltpu.roll(y, 32, 1)
            y = y + pltpu.roll(y, 64, 1)
            turned = swapped(y)
            factor[w, GROUP * a : GROUP * (a + 1), :] = jnp.where(low, y, turned)
            factor[w, HALF + GROUP * a : HALF + GROUP * (a + 1), :] = jnp.where(low, turned, y)


def mix(current, masks, sign):
    first, second = current[:HALF], current[HALF:]
    m = jnp.concatenate([first + second, swapped(sign * (first - second))], axis=0)
    return jnp.concatenate(
        [jnp.where(masks[0], m, 0.0), jnp.where(masks[1], m, 0.0)], axis=1
    ).astype(jnp.bfloat16)


def predict_tile(inline, part):
    p_re = p_im = None
    for i in range(HALF // 16):
        a_re = inline[16 * i : 16 * i + 16]
        a_im = inline[HALF + 16 * i : HALF + 16 * i + 16]
        b_re = part[16 * i : 16 * i + 16]
        b_im = part[HALF + 16 * i : HALF + 16 * i + 16]
        re = a_re * b_re - a_im * b_im
        im = a_re * b_im + a_im * b_re
        p_re = re if p_re is None else p_re + re
        p_im = im if p_im is None else p_im + im
    return p_re[:8] + p_re[8:], p_im[:8] + p_im[8:]


def predict_strip(mixing, cross, inline, w, g, s):
    out = []
    for first in (4 * s, 4 * s + 2):
        part = jnp.dot(
            mixing, side_by_side(cross, w, g, first, 2), preferred_element_type=jnp.float32
        )
        for k in range(2):
            table = inline[w][g, :, (first + k) * LANES : (first + k + 1) * LANES]
            out.append(predict_tile(table, part[:, k * LANES : (k + 1) * LANES]))
    return out


def predict_edges(mixing, cross, inline, w, g, tile):
    out = []
    for s in range(2):
        sl = slice((tile + 4 * s) * LANES, (tile + 4 * s + 1) * LANES)
        part = jnp.dot(mixing, cross[w][g, tile + 4 * s], preferred_element_type=jnp.float32)
        out.append(predict_tile(inline[w][g, :, sl], part))
    return out


def join(lower, upper):
    ramp = (iota((8, LANES), 1).astype(jnp.float32) + 0.5) / LANES
    return tuple((1.0 - ramp) * lower[c] + ramp * upper[c] for c in range(2))


def both_orders(own, others, windows):
    return [own.at[0]] + [others.at[n] for n in range(windows - 1)]


def blend(predicted, windows, win):
    joined = {}
    for n in range(windows if windows > 1 else 0):
        above = (n + 1) % windows
        apart = lax.rem(win + n, windows) == windows - 1
        trail, lead = predicted[n][3], predicted[above][0]
        both = join(trail, lead)
        joined[n, 3] = tuple(jnp.where(apart, trail[c], both[c]) for c in range(2))
        joined[above, 0] = tuple(jnp.where(apart, lead[c], both[c]) for c in range(2))
    for (n, tile), value in joined.items():
        predicted[n][tile] = value
    return predicted


def step_kernel(windows, nfreq, count, *refs):
    energies, refs = refs[:count], refs[count:]
    threshold, refs = refs[0], refs[1:]
    if windows > 1:
        cross, inline, observed, mask, updated = (
            both_orders(refs[n], refs[5 + n], windows) for n in range(5)
        )
        new = both_orders(refs[10], refs[11], windows)
        energy, factor, hb, acc = refs[12:]
    else:
        cross, inline, observed, mask, updated = ([refs[n].at[0]] for n in range(5))
        new = [refs[5].at[0]]
        energy, factor, hb, acc = refs[6:]
    win = lax.axis_index("win")
    spread_factor(energies, threshold, factor, windows, nfreq)
    masks, sign = group_masks(), half_sign()
    acc[...] = jnp.zeros_like(acc)
    for g in range(updated[0].shape[0]):
        mixing = [mix(updated[w][g] * factor[w], masks, sign) for w in range(windows)]
        buffers = [hb.at[(g * windows + w) % hb.shape[0]] for w in range(windows)]
        for s in range(2):
            predicted = blend(
                [predict_strip(mixing[w], cross, inline, w, g, s) for w in range(windows)],
                windows,
                win,
            )
            for w in range(windows):
                for t in range(4):
                    tile = 4 * s + t
                    sl = slice(tile * LANES, (tile + 1) * LANES)
                    here = mask[w][:, sl]
                    p_re, p_im = predicted[w][t]
                    r_re = here * p_re - observed[w][0, g, :, sl]
                    r_im = here * p_im - observed[w][1, g, :, sl]
                    weigh(inline[w], g, tile, r_re, r_im, buffers[w])
        for w in range(windows):
            slopes = project_group(buffers[w], cross, w, g, masks, sign)
            for part, slope in enumerate(slopes):
                rows = slice(part * HALF, (part + 1) * HALF)
                value = updated[w][g, rows] * factor[w, rows] - step_length * slope
                new[w][g, rows] = value
                acc[w, rows] += value * value
    for w in range(windows):
        pack_energy(acc[w], energy, 4 * w)


def final_kernel(windows, nfreq, count, *refs):
    energies, refs = refs[:count], refs[count:]
    threshold, matching, refs = refs[0], refs[1], refs[2:]
    if windows > 1:
        cross, inline, updated = (both_orders(refs[n], refs[3 + n], windows) for n in range(3))
        refs = refs[6:]
    else:
        cross, inline, updated = ([refs[n].at[0]] for n in range(3))
        refs = refs[3:]
    swap, keep, factor = refs
    win = lax.axis_index("win")
    spread_factor(energies, threshold, factor, windows, nfreq)
    masks, sign = group_masks(), half_sign()
    block = iota((GROUP, LANES), 1) // SPAN
    wide = iota((HALF, LANES), 1) // SPAN
    line, lane = iota((LANES, 2 * LANES), 0), iota((LANES, 2 * LANES), 1)
    b, imag = lane % PY, lane // LANES
    source = jnp.where(b < FOLD, b, SPAN + PY - 1 - b) + FOLD * imag
    value = jnp.where((imag == 1) & (b < FOLD), -1.0, 1.0)
    order = jnp.where(line == source, value, 0.0)

    for g in range(updated[0].shape[0]):
        current = updated[0][g] * factor[0]
        mixing = mix(current, masks, sign)
        traces = [x for s in range(2) for x in predict_strip(mixing, cross, inline, 0, g, s)]
        if windows > 1:
            mixed = [
                mix(updated[w][g] * factor[w], masks, sign) for w in sorted({1, windows - 1})
            ]
            above = predict_edges(mixed[0], cross, inline, 1, g, 0)
            below = predict_edges(mixed[-1], cross, inline, windows - 1, g, 3)
            for s in range(2):
                lead, trail = traces[4 * s], traces[4 * s + 3]
                low, high = join(below[s], lead), join(trail, above[s])
                traces[4 * s] = tuple(jnp.where(win > 0, low[c], lead[c]) for c in range(2))
                traces[4 * s + 3] = tuple(
                    jnp.where(win < windows - 1, high[c], trail[c]) for c in range(2)
                )
        spans = jnp.where(wide == 0, current[:HALF], jnp.where(wide == 1, current[HALF:], 0.0))
        spans = jnp.dot(spans, order, precision=HIGHEST, preferred_element_type=jnp.float32)
        sl = slice(GROUP * g, GROUP * (g + 1))
        for c in range(2):
            for j in range(4):
                lanes = slice(j * LANES, (j + 1) * LANES)
                values = None
                for q in range(4):
                    a = 4 * j + q
                    part = spans[GROUP * a : GROUP * (a + 1), c * LANES : (c + 1) * LANES]
                    part = jnp.where(block == q, part, 0.0)
                    values = part if values is None else values + part
                swap[0, c, sl, lanes] = values
                keep[0, c, sl, lanes] = values
            for t in range(8):
                lanes = slice((t % 4) * LANES, (t % 4 + 1) * LANES)
                out = keep if t < 4 else swap
                out[1, c, sl, lanes] = traces[t][c]
    for s, out in enumerate((keep, swap)):
        for c in range(2):
            out[1, c, :, :LANES] = jnp.dot(
                out[1, c, :, :LANES],
                matching[s],
                precision=HIGHEST,
                preferred_element_type=jnp.float32,
            )


VM = pl.BlockSpec(memory_space=pltpu.VMEM)
HB = pl.BlockSpec(memory_space=pltpu.HBM)


def params(windows):
    return pltpu.CompilerParams(vmem_limit_bytes=(16 if windows <= 2 else 60) * 1024 * 1024)


def shape(*dims, dtype=jnp.float32):
    return jax.ShapeDtypeStruct(dims, dtype)


def sum_parts(energy):
    swap = [(0, 1), (1, 0)]
    energy = energy + lax.ppermute(energy, "rep", swap)
    size = lax.axis_size("freq")
    if size & (size - 1):
        return [lax.psum(energy, "freq")]
    axes = ("freq", "rep")

    def crossed(k):
        return [(2 * i + r, 2 * (i ^ k) + 1 - r) for i in range(size) for r in range(2)]

    if size <= 4:
        return [energy] + [lax.ppermute(energy, axes, crossed(k)) for k in range(1, size)]
    k = 1
    while k < size:
        energy = energy + lax.ppermute(energy, axes, crossed(k))
        k *= 2
    return [energy]


def per_device(recorded, geometry, present, intersection_index, pattern, group_scale):
    frequencies = recorded.shape[1]
    traces = recorded.shape[3]
    windows = lax.axis_size("win")
    nfreq = frequencies * lax.axis_size("freq")
    half = frequencies // 2
    groups = half // GROUP
    amplitude = 1.0 / math.sqrt(traces * lax.axis_size("rep"))
    width = 2 * traces
    swap = [(0, 1), (1, 0)]

    payload = shape(2 * half + 8, traces)
    turned = jnp.transpose(pattern, (1, 2, 0))
    sources = tuple(
        pltpu.with_memory_space_constraint(x, pltpu.HBM)
        for x in (recorded, geometry, present, intersection_index, turned)
    )
    keep, send = pl.pallas_call(
        pack_kernel,
        out_shape=(payload, payload),
        in_specs=[HB] * 5,
        out_specs=(VM, VM),
        scratch_shapes=[pltpu.VMEM(x.shape, x.dtype) for x in sources]
        + [
            pltpu.SemaphoreType.DMA((5,)),
            pltpu.VMEM((turned.shape[0] * turned.shape[1], frequencies), jnp.float32),
        ],
        compiler_params=params(windows),
        name="pack",
    )(*sources)
    received = lax.ppermute(send, "rep", swap)
    if windows == 2:
        diagonal = [(2 * i + r, 2 * (1 - i) + 1 - r) for i in range(2) for r in range(2)]
        others = [lax.ppermute(keep, "win", swap), lax.ppermute(send, ("win", "rep"), diagonal)]
    else:
        others = [lax.all_gather(keep, "win"), lax.all_gather(received, "win")]

    rows = 2 * HALF
    energy_shape = shape(4 * windows, LANES)

    def scratch(many):
        buffers = many * groups if windows <= 2 else windows
        return [
            pltpu.VMEM((buffers, width // LANES, rows, LANES), jnp.bfloat16),
            pltpu.VMEM((many, rows, LANES), jnp.float32),
        ]

    def build(own, inputs):
        many = 1 if own else windows - 1
        out_shape = (
            shape(many, groups, width // LANES, SPAN * GROUP, LANES, dtype=jnp.bfloat16),
            shape(many, groups, rows, width),
            shape(many, 2, groups, GROUP, width),
            shape(many, 8, width),
            shape(many, groups, rows, LANES),
            shape(4, LANES) if own else energy_shape,
        )
        if own:
            out_shape += (shape(2, LANES, LANES), shape(4, LANES))
        return pl.pallas_call(
            functools.partial(table_kernel, windows, nfreq, amplitude, own),
            out_shape=out_shape,
            in_specs=[VM] * len(inputs),
            out_specs=(VM,) * len(out_shape),
            scratch_shapes=[pltpu.VMEM((many, 2, 2 * half + 8, traces), jnp.float32)]
            + scratch(many),
            compiler_params=params(windows),
            cost_estimate=pl.CostEstimate(flops=4 * 10**9, bytes_accessed=0, transcendentals=0),
            name="tables",
        )(*inputs)

    *tables, updated, energy, matching, threshold = build(
        True, [keep, received, group_scale.reshape(4, LANES)]
    )
    tables, states = [tables], [updated]
    if windows > 1:
        *others, updated, energy = build(False, others + [energy])
        tables.append(others)
        states.append(updated)

    factor_scratch = pltpu.VMEM((windows, rows, LANES), jnp.float32)
    for _ in range(ITERS - 1):
        inputs = [threshold]
        for table, state in zip(tables, states):
            inputs += [*table, state]
        energies = sum_parts(energy)
        *states, energy = pl.pallas_call(
            functools.partial(step_kernel, windows, nfreq, len(energies)),
            out_shape=tuple(shape(*x.shape) for x in states) + (energy_shape,),
            in_specs=[VM] * (len(energies) + len(inputs)),
            out_specs=(VM,) * (len(states) + 1),
            scratch_shapes=[factor_scratch] + scratch(windows),
            compiler_params=params(windows),
            name="step",
        )(*energies, *inputs)
    energies = sum_parts(energy)
    halves = shape(2, 2, half, traces)
    inputs = [threshold, matching]
    for table, state in zip(tables, states):
        inputs += [*table[:2], state]
    theirs, mine = pl.pallas_call(
        functools.partial(final_kernel, windows, nfreq, len(energies)),
        out_shape=(halves, halves),
        in_specs=[VM] * (len(energies) + len(inputs)),
        out_specs=(VM, VM),
        scratch_shapes=[factor_scratch],
        compiler_params=params(windows),
        name="final",
    )(*energies, *inputs)
    theirs = lax.ppermute(theirs, "rep", swap)
    out = shape(2, frequencies, 1, traces)
    return pl.pallas_call(
        unpack_kernel,
        out_shape=(out, out),
        in_specs=[VM, VM],
        out_specs=(VM, VM),
        compiler_params=params(windows),
        name="unpack",
    )(mine, theirs)


def solution(mesh):
    return jax.shard_map(
        per_device,
        mesh=mesh,
        in_specs=(
            P(None, "freq", ("dom", "win"), "rep"),
            P(None, ("dom", "win"), "rep"),
            P(("dom", "win"), "rep"),
            P(("dom", "win"), "rep", None),
            P("freq", None, "rep"),
            P(),
        ),
        out_specs=(P(None, "freq", ("dom", "win"), None), P(None, "freq", ("dom", "win"), "rep")),
        check_vma=False,
    )
```

time: 52.7 us -> 45.8 us (0.87)
  Pallas kernels: 22 us -> 16 us
  waiting for transfers between devices: 10.9 us -> 12 us
  local copies, waits for them, and re-layouts: 1.58 us -> 0.68 us
  other arithmetic: 0.68 us -> 0.01 us
    pallas_call x2, Pallas kernels: 8.41 us -> 5.77 us  [build(): pl.pallas_call(functools.partial(table_kernel, windows, nfreq, amplitude,...]
    pallas_call x2, Pallas kernels: 3.7 us -> 1.83 us  [the longest x1 1.09 us: per_device(): pl.pallas_call(pack_kernel, out_shape=(payload, payload), in_specs=[HB] *...]
    ppermute x1, waiting for transfers between devices: 0.01 us -> 1.05 us  [per_device(): lax.ppermute(keep, 'win', swap)]
    unnamed x6 -> x2, local copies, waits for them, and re-layouts: 1.58 us -> 0.68 us
    pallas_call x2, Pallas kernels: 7.35 us -> 6.52 us  [per_device(): pl.pallas_call(functools.partial(step_kernel, windows, nfreq, len(energie...]
    pallas_call x1, Pallas kernels: 2.54 us -> 1.83 us  [per_device(): pl.pallas_call(functools.partial(final_kernel, windows, nfreq, len(energi...]
    another operation x1 -> x0, other arithmetic: 0.67 us -> none  [per_device(): place = jnp.stack([win, rep, first]).astype(jnp.int32)]
  transfers between devices with their start and end apart: 16 -> 16, of which waited for: 11 -> 12; matrix products, arithmetic and copies ran while one was open for 0% -> 0% of each run, Pallas kernels for 8% -> 6%
where the time goes in v4:
time: 45.8 us; the launch traced here: 45.6 us
  starting transfers between devices  16.2 us (35%)
  Pallas kernels  16 us (35%)
  waiting for transfers between devices  12 us (26%)
  between operations  0.69 us (2%)
  local copies, waits for them, and re-layouts  0.68 us (1%)
    ppermute x9, starting transfers between devices, sum_parts(): lax.ppermute(energy, axes, crossed(k))  12 us
    ppermute x9, waiting for transfers between devices, sum_parts(): lax.ppermute(energy, axes, crossed(k))  6.92 us
    pallas_call x2, Pallas kernels, per_device(): pl.pallas_call(functools.partial(step_kernel, windows, nfreq, len(energie...  6.52 us
    pallas_call x2, Pallas kernels, build(): pl.pallas_call(functools.partial(table_kernel, windows, nfreq, amplitude,...  5.77 us
    ppermute x3, waiting for transfers between devices, sum_parts(): energy = energy + lax.ppermute(energy, 'rep', swap)  3.02 us
    ppermute x1, starting transfers between devices, per_device(): lax.ppermute(send, ('win', 'rep'), diagonal)  2.61 us
    pallas_call x1, Pallas kernels, per_device(): pl.pallas_call(functools.partial(final_kernel, windows, nfreq, len(energi...  1.83 us
    pallas_call x1, Pallas kernels, per_device(): pl.pallas_call(pack_kernel, out_shape=(payload, payload), in_specs=[HB] *...  1.09 us
  transfers between devices with their start and end apart: 16, of which 12 were waited for; matrix products, arithmetic and copies ran while one was open for 0% of the time, Pallas kernels for 6%

profile of v4, /device:TPU:0, one launch (start us, length us, event | category | flops | bytes accessed | tf_op | source)
XLA Modules:
  0.0 45.6 jit_solution(16192411137414739018)
XLA Ops:
  0.6 1.1 %pack.1 = (f32[40,512]{1,0:T(8,128)S(1)}, f32[40,512]{1,0:T(8,128)S(1)}) custom-call(f32[2,32,1,512]{3,2,1,0:T(1,128)} %recorded.1, f32[2,1,512]{2,1,0:T(1,128)} %geometry.1, s32[1,512]{1,0:T(1,128)} %present.1, s32[1,1,128]{2,1,0:T(1,128)} %intersection.1, s32[8,4,32]{2,1,0:T(4,128)} %bitcast.3), custom_call_target="tpu_custom_call" | custom-call | tf_op jit(solution)/shard_map/pack/pallas_call | solution.py:570
  1.7 0.5 %collective-permute-start.2 = (f32[40,512]{1,0:T(8,128)S(1)}, f32[40,512]{1,0:T(8,128)S(1)}, u32[]{:S(2)}, u32[]{:S(2)}) collective-permute-start(f32[40,512]{1,0:T(8,128)S(1)} %get-tuple-element.27), channel_id=1, source_target_pairs={{0,1},{1,0},{2,3},{3,2},{4,5},{5,4},{6,7},{7,6},{8,9},{9,8},{10,11... | collective-permute-start | bytes 245768 | tf_op jit(solution)/shard_map/ppermute | solution.py:583
  2.2 2.6 %collective-permute-start.1 = (f32[40,512]{1,0:T(8,128)S(1)}, f32[40,512]{1,0:T(8,128)S(1)}, u32[]{:S(2)}, u32[]{:S(2)}) collective-permute-start(f32[40,512]{1,0:T(8,128)S(1)} %get-tuple-element.27), channel_id=1, source_target_pairs={{0,3},{1,2},{2,1},{3,0},{4,7},{5,6},{6,5},{7,4},{8,11},{9,10},{10,... | collective-permute-start | bytes 245768 | tf_op jit(solution)/shard_map/ppermute | solution.py:586
  4.9 0.0 collective-permute-start
  4.9 0.0 collective-permute-done.2.refs_1_
  4.9 0.0 copy-start
  4.9 0.7 %copy-done = f32[512]{0:T(512)S(1)} copy-done((f32[512]{0:T(512)S(1)}, f32[512]{0:T(512)}, u32[]{:S(2)}) %copy-start) | copy-done | bytes 2072
  5.6 3.0 %tables.2 = (bf16[1,2,8,256,128]{4,3,2,1,0:T(8,128)(2,1)S(1)}, f32[1,2,256,1024]{3,2,1,0:T(8,128)S(1)}, f32[1,2,2,8,1024]{4,3,2,1,0:T(8,128)S(1)}, f32[1,8,1024]...) custom-call(f32[40,512]{1,0:T(8,128)S(1)} %get-tuple-element.26.refs, ...), custom_call_target="tpu_custom_call" | custom-call | flops 4000000000 | tf_op jit(solution)/shard_map/tables/pallas_call | solution.py:612
  8.6 1.0 %collective-permute-done.refs_0_ = f32[40,512]{1,0:T(8,128)S(1)} collective-permute-done((f32[40,512]{1,0:T(8,128)S(1)}, f32[40,512]{1,0:T(8,128)S(1)}, u32[]{:S(2)}, u32[]{:S(2)}) %collective-permute-start) | collective-permute-done | bytes 81952 | tf_op jit(solution)/shard_map/ppermute | solution.py:586
  9.6 0.0 collective-permute-done.1.refs_1_
  9.6 2.8 %tables.3 = (bf16[1,2,8,256,128]{4,3,2,1,0:T(8,128)(2,1)S(1)}, f32[1,2,256,1024]{3,2,1,0:T(8,128)S(1)}, f32[1,2,2,8,1024]{4,3,2,1,0:T(8,128)S(1)}, f32[1,8,1024]...) custom-call(f32[40,512]{1,0:T(8,128)S(1)} %collective-permute-done.refs_0_, ...), custom_call_target="tpu_custom_call" | custom-call | flops 4000000000 | tf_op jit(solution)/shard_map/tables/pallas_call | solution.py:612
  12.4 0.1 collective-permute-start.3
  12.5 1.2 %collective-permute-done.3 = f32[8,128]{1,0:T(8,128)S(1)} collective-permute-done((f32[8,128]{1,0:T(8,128)S(1)}, f32[8,128]{1,0:T(8,128)S(1)}, u32[]{:S(2)}, u32[]{:S(2)}) %collective-permute-start.3) | collective-permute-done | bytes 4128 | tf_op jit(solution)/shard_map/ppermute | solution.py:535
  13.7 3.6 %collective-permute-start.6 = (f32[8,128]{1,0:T(8,128)S(1)}, f32[8,128]{1,0:T(8,128)S(1)}, u32[]{:S(2)}, u32[]{:S(2)}) collective-permute-start(f32[8,128]{1,0:T(8,128)S(1)} %add.9.refs_0_), channel_id=1, source_target_pairs={{0,13},{1,12},{4,9},{5,8},{8,5},{9,4},{12,1},{13,0},{2,15},{3,14},... | collective-permute-start | bytes 12296 | tf_op jit(solution)/shard_map/ppermute | solution.py:545
  17.2 0.0 collective-permute-start.5
  17.3 0.5 %collective-permute-start.4 = (f32[8,128]{1,0:T(8,128)S(1)}, f32[8,128]{1,0:T(8,128)S(1)}, u32[]{:S(2)}, u32[]{:S(2)}) collective-permute-start(f32[8,128]{1,0:T(8,128)S(1)} %add.9.refs_0_), channel_id=1, source_target_pairs={{0,5},{1,4},{4,1},{5,0},{8,13},{9,12},{12,9},{13,8},{2,7},{3,6},{6... | collective-permute-start | bytes 12296 | tf_op jit(solution)/shard_map/ppermute | solution.py:545
  17.8 0.8 %collective-permute-done.6.refs_3_ = f32[8,128]{1,0:T(8,128)S(1)} collective-permute-done((f32[8,128]{1,0:T(8,128)S(1)}, f32[8,128]{1,0:T(8,128)S(1)}, u32[]{:S(2)}, u32[]{:S(2)}) %collective-permute-start.6) | collective-permute-done | bytes 4128 | tf_op jit(solution)/shard_map/ppermute | solution.py:545
  18.6 2.6 %collective-permute-done.5.refs_2_ = f32[8,128]{1,0:T(8,128)S(1)} collective-permute-done((f32[8,128]{1,0:T(8,128)S(1)}, f32[8,128]{1,0:T(8,128)S(1)}, u32[]{:S(2)}, u32[]{:S(2)}) %collective-permute-start.5) | collective-permute-done | bytes 4128 | tf_op jit(solution)/shard_map/ppermute | solution.py:545
  21.2 0.0 collective-permute-done.4.refs_1_
  21.2 3.3 %step.2 = (f32[1,2,256,128]{3,2,1,0:T(8,128)S(1)}, f32[1,2,256,128]{3,2,1,0:T(8,128)S(1)}, f32[8,128]{1,0:T(8,128)S(1)}) custom-call(f32[8,128]{1,0:T(8,128)S(1)} %add.9.refs_0_, f32[8,128]{1,0:T(8,128)S(1)} %collective-permute-done.4.refs_1_, f32[8,128]{1,0:T(8,128)S(1)} %collective-permute-done.5.refs_2_, f32[8,128]{1,0:T(8,128)S(1)} %collective-permute-done.6.refs_3_, ...), custom_call_target="tpu_custom_call" | custom-call | tf_op jit(solution)/shard_map/step/pallas_call | solution.py:639
  24.4 0.4 collective-permute-start.7
  24.9 0.8 %collective-permute-done.7 = f32[8,128]{1,0:T(8,128)S(1)} collective-permute-done((f32[8,128]{1,0:T(8,128)S(1)}, f32[8,128]{1,0:T(8,128)S(1)}, u32[]{:S(2)}, u32[]{:S(2)}) %collective-permute-start.7) | collective-permute-done | bytes 4128 | tf_op jit(solution)/shard_map/ppermute | solution.py:535
  25.7 1.4 %collective-permute-start.10 = (f32[8,128]{1,0:T(8,128)S(1)}, f32[8,128]{1,0:T(8,128)S(1)}, u32[]{:S(2)}, u32[]{:S(2)}) collective-permute-start(f32[8,128]{1,0:T(8,128)S(1)} %add.10.refs_0_), channel_id=1, source_target_pairs={{0,13},{1,12},{4,9},{5,8},{8,5},{9,4},{12,1},{13,0},{2,15},{3,14},... | collective-permute-start | bytes 12296 | tf_op jit(solution)/shard_map/ppermute | solution.py:545
  27.1 0.3 collective-permute-start.9
  27.4 2.3 %collective-permute-start.8 = (f32[8,128]{1,0:T(8,128)S(1)}, f32[8,128]{1,0:T(8,128)S(1)}, u32[]{:S(2)}, u32[]{:S(2)}) collective-permute-start(f32[8,128]{1,0:T(8,128)S(1)} %add.10.refs_0_), channel_id=1, source_target_pairs={{0,5},{1,4},{4,1},{5,0},{8,13},{9,12},{12,9},{13,8},{2,7},{3,6},{6... | collective-permute-start | bytes 12296 | tf_op jit(solution)/shard_map/ppermute | solution.py:545
  29.7 0.8 %collective-permute-done.10.refs_3_ = f32[8,128]{1,0:T(8,128)S(1)} collective-permute-done((f32[8,128]{1,0:T(8,128)S(1)}, f32[8,128]{1,0:T(8,128)S(1)}, u32[]{:S(2)}, u32[]{:S(2)}) %collective-permute-start.10) | collective-permute-done | bytes 4128 | tf_op jit(solution)/shard_map/ppermute | solution.py:545
  30.5 0.5 %collective-permute-done.9.refs_2_ = f32[8,128]{1,0:T(8,128)S(1)} collective-permute-done((f32[8,128]{1,0:T(8,128)S(1)}, f32[8,128]{1,0:T(8,128)S(1)}, u32[]{:S(2)}, u32[]{:S(2)}) %collective-permute-start.9) | collective-permute-done | bytes 4128 | tf_op jit(solution)/shard_map/ppermute | solution.py:545
  31.0 0.1 collective-permute-done.8.refs_1_
  31.1 3.3 %step.3 = (f32[1,2,256,128]{3,2,1,0:T(8,128)S(1)}, f32[1,2,256,128]{3,2,1,0:T(8,128)S(1)}, f32[8,128]{1,0:T(8,128)S(1)}) custom-call(f32[8,128]{1,0:T(8,128)S(1)} %add.10.refs_0_, f32[8,128]{1,0:T(8,128)S(1)} %collective-permute-done.8.refs_1_, f32[8,128]{1,0:T(8,128)S(1)} %collective-permute-done.9.refs_2_, f32[8,128]{1,0:T(8,128)S(1)} %collective-permute-done.10.refs_3_, ...), custom_call_target="tpu_custom_call" | custom-call | tf_op jit(solution)/shard_map/step/pallas_call | solution.py:639
  34.4 0.2 collective-permute-start.11
  34.6 1.0 %collective-permute-done.11 = f32[8,128]{1,0:T(8,128)S(1)} collective-permute-done((f32[8,128]{1,0:T(8,128)S(1)}, f32[8,128]{1,0:T(8,128)S(1)}, u32[]{:S(2)}, u32[]{:S(2)}) %collective-permute-start.11) | collective-permute-done | bytes 4128 | tf_op jit(solution)/shard_map/ppermute | solution.py:535
  35.6 2.1 %collective-permute-start.14 = (f32[8,128]{1,0:T(8,128)S(1)}, f32[8,128]{1,0:T(8,128)S(1)}, u32[]{:S(2)}, u32[]{:S(2)}) collective-permute-start(f32[8,128]{1,0:T(8,128)S(1)} %add.11.refs_0_), channel_id=1, source_target_pairs={{0,13},{1,12},{4,9},{5,8},{8,5},{9,4},{12,1},{13,0},{2,15},{3,14},... | collective-permute-start | bytes 12296 | tf_op jit(solution)/shard_map/ppermute | solution.py:545
  37.7 0.8 %collective-permute-start.13 = (f32[8,128]{1,0:T(8,128)S(1)}, f32[8,128]{1,0:T(8,128)S(1)}, u32[]{:S(2)}, u32[]{:S(2)}) collective-permute-start(f32[8,128]{1,0:T(8,128)S(1)} %add.11.refs_0_), channel_id=1, source_target_pairs={{0,9},{1,8},{4,13},{5,12},{8,1},{9,0},{12,5},{13,4},{2,11},{3,10},... | collective-permute-start | bytes 12296 | tf_op jit(solution)/shard_map/ppermute | solution.py:545
  38.5 1.0 %collective-permute-start.12 = (f32[8,128]{1,0:T(8,128)S(1)}, f32[8,128]{1,0:T(8,128)S(1)}, u32[]{:S(2)}, u32[]{:S(2)}) collective-permute-start(f32[8,128]{1,0:T(8,128)S(1)} %add.11.refs_0_), channel_id=1, source_target_pairs={{0,5},{1,4},{4,1},{5,0},{8,13},{9,12},{12,9},{13,8},{2,7},{3,6},{6... | collective-permute-start | bytes 12296 | tf_op jit(solution)/shard_map/ppermute | solution.py:545
  39.5 0.9 %collective-permute-done.14.refs_3_ = f32[8,128]{1,0:T(8,128)S(1)} collective-permute-done((f32[8,128]{1,0:T(8,128)S(1)}, f32[8,128]{1,0:T(8,128)S(1)}, u32[]{:S(2)}, u32[]{:S(2)}) %collective-permute-start.14) | collective-permute-done | bytes 4128 | tf_op jit(solution)/shard_map/ppermute | solution.py:545
  40.4 1.2 %collective-permute-done.13.refs_2_ = f32[8,128]{1,0:T(8,128)S(1)} collective-permute-done((f32[8,128]{1,0:T(8,128)S(1)}, f32[8,128]{1,0:T(8,128)S(1)}, u32[]{:S(2)}, u32[]{:S(2)}) %collective-permute-start.13) | collective-permute-done | bytes 4128 | tf_op jit(solution)/shard_map/ppermute | solution.py:545
  41.6 0.0 collective-permute-done.12.refs_1_
  41.6 1.8 %final.1 = (f32[2,2,16,512]{3,2,1,0:T(8,128)S(1)}, f32[2,2,16,512]{3,2,1,0:T(8,128)S(1)}) custom-call(f32[8,128]{1,0:T(8,128)S(1)} %add.11.refs_0_, f32[8,128]{1,0:T(8,128)S(1)} %collective-permute-done.12.refs_1_, f32[8,128]{1,0:T(8,128)S(1)} %collective-permute-done.13.refs_2_, f32[8,128]{1,0:T(8,128)S(1)} %collective-permute-done.14.refs_3_, ...), custom_call_target="tpu_custom_call" | custom-call | tf_op jit(solution)/shard_map/final/pallas_call | solution.py:653
  43.5 0.3 collective-permute-start.15
  43.8 1.0 %collective-permute-done.15.theirs = f32[2,2,16,512]{3,2,1,0:T(8,128)S(1)} collective-permute-done((f32[2,2,16,512]{3,2,1,0:T(8,128)S(1)}, f32[2,2,16,512]{3,2,1,0:T(8,128)S(1)}, u32[]{:S(2)}, u32[]{:S(2)}) %collective-permute-start.15) | collective-permute-done | bytes 131104 | tf_op jit(solution)/shard_map/ppermute | solution.py:662
  44.8 0.7 %unpack.1 = (f32[2,32,1,512]{3,2,1,0:T(1,128)}, f32[2,32,1,512]{3,2,1,0:T(1,128)}) custom-call(f32[2,2,16,512]{3,2,1,0:T(8,128)S(1)} %get-tuple-element.48.mine, f32[2,2,16,512]{3,2,1,0:T(8,128)S(1)} %collective-permute-done.15.theirs), custom_call_target="tpu_custom_call" | custom-call | tf_op jit(solution)/shard_map/unpack/pallas_call | solution.py:664
  (3 shorter events, 0.0 us)
Async XLA Ops:
  1.7 3.2 %collective-permute-start.2 = (f32[40,512]{1,0:T(8,128)S(1)}, f32[40,512]{1,0:T(8,128)S(1)}, u32[]{:S(2)}, u32[]{:S(2)}) collective-permute-start(f32[40,512]{1,0:T(8,128)S(1)} %get-tuple-element.27), channel_id=1, source_target_pairs={{0,1},{1,0},{2,3},{3,2},{4,5},{5,4},{6,7},{7,6},{8,9},{9,8},{10,11... | collective-permute-start | bytes 245768 | tf_op jit(solution)/shard_map/ppermute | solution.py:583
  2.2 7.4 %collective-permute-start.1 = (f32[40,512]{1,0:T(8,128)S(1)}, f32[40,512]{1,0:T(8,128)S(1)}, u32[]{:S(2)}, u32[]{:S(2)}) collective-permute-start(f32[40,512]{1,0:T(8,128)S(1)} %get-tuple-element.27), channel_id=1, source_target_pairs={{0,3},{1,2},{2,1},{3,0},{4,7},{5,6},{6,5},{7,4},{8,11},{9,10},{10,... | collective-permute-start | bytes 245768 | tf_op jit(solution)/shard_map/ppermute | solution.py:586
  4.9 4.7 %collective-permute-start = (f32[40,512]{1,0:T(8,128)S(1)}, f32[40,512]{1,0:T(8,128)S(1)}, u32[]{:S(2)}, u32[]{:S(2)}) collective-permute-start(f32[40,512]{1,0:T(8,128)S(1)} %get-tuple-element.26.refs_0_), channel_id=1, source_target_pairs={{0,2},{2,0},{1,3},{3,1},{4,6},{6,4},{5,7},{7,5},{8,10},{10,8},{9,1... | collective-permute-start | bytes 245768 | tf_op jit(solution)/shard_map/ppermute | solution.py:586
  4.9 0.7 %copy-start = (f32[512]{0:T(512)S(1)}, f32[512]{0:T(512)}, u32[]{:S(2)}) copy-start(f32[512]{0:T(512)} %param.11) | copy-start | bytes 6148
  12.4 1.2 %collective-permute-start.3 = (f32[8,128]{1,0:T(8,128)S(1)}, f32[8,128]{1,0:T(8,128)S(1)}, u32[]{:S(2)}, u32[]{:S(2)}) collective-permute-start(f32[8,128]{1,0:T(8,128)S(1)} %get-tuple-element.29), channel_id=1, source_target_pairs={{0,1},{1,0},{2,3},{3,2},{4,5},{5,4},{6,7},{7,6},{8,9},{9,8},{10,11... | collective-permute-start | bytes 12296 | tf_op jit(solution)/shard_map/ppermute | solution.py:535
  13.7 4.9 %collective-permute-start.6 = (f32[8,128]{1,0:T(8,128)S(1)}, f32[8,128]{1,0:T(8,128)S(1)}, u32[]{:S(2)}, u32[]{:S(2)}) collective-permute-start(f32[8,128]{1,0:T(8,128)S(1)} %add.9.refs_0_), channel_id=1, source_target_pairs={{0,13},{1,12},{4,9},{5,8},{8,5},{9,4},{12,1},{13,0},{2,15},{3,14},... | collective-permute-start | bytes 12296 | tf_op jit(solution)/shard_map/ppermute | solution.py:545
  17.2 3.9 %collective-permute-start.5 = (f32[8,128]{1,0:T(8,128)S(1)}, f32[8,128]{1,0:T(8,128)S(1)}, u32[]{:S(2)}, u32[]{:S(2)}) collective-permute-start(f32[8,128]{1,0:T(8,128)S(1)} %add.9.refs_0_), channel_id=1, source_target_pairs={{0,9},{1,8},{4,13},{5,12},{8,1},{9,0},{12,5},{13,4},{2,11},{3,10},... | collective-permute-start | bytes 12296 | tf_op jit(solution)/shard_map/ppermute | solution.py:545
  17.3 3.9 %collective-permute-start.4 = (f32[8,128]{1,0:T(8,128)S(1)}, f32[8,128]{1,0:T(8,128)S(1)}, u32[]{:S(2)}, u32[]{:S(2)}) collective-permute-start(f32[8,128]{1,0:T(8,128)S(1)} %add.9.refs_0_), channel_id=1, source_target_pairs={{0,5},{1,4},{4,1},{5,0},{8,13},{9,12},{12,9},{13,8},{2,7},{3,6},{6... | collective-permute-start | bytes 12296 | tf_op jit(solution)/shard_map/ppermute | solution.py:545
  24.4 1.2 %collective-permute-start.7 = (f32[8,128]{1,0:T(8,128)S(1)}, f32[8,128]{1,0:T(8,128)S(1)}, u32[]{:S(2)}, u32[]{:S(2)}) collective-permute-start(f32[8,128]{1,0:T(8,128)S(1)} %get-tuple-element.41), channel_id=1, source_target_pairs={{0,1},{1,0},{2,3},{3,2},{4,5},{5,4},{6,7},{7,6},{8,9},{9,8},{10,11... | collective-permute-start | bytes 12296 | tf_op jit(solution)/shard_map/ppermute | solution.py:535
  25.7 4.8 %collective-permute-start.10 = (f32[8,128]{1,0:T(8,128)S(1)}, f32[8,128]{1,0:T(8,128)S(1)}, u32[]{:S(2)}, u32[]{:S(2)}) collective-permute-start(f32[8,128]{1,0:T(8,128)S(1)} %add.10.refs_0_), channel_id=1, source_target_pairs={{0,13},{1,12},{4,9},{5,8},{8,5},{9,4},{12,1},{13,0},{2,15},{3,14},... | collective-permute-start | bytes 12296 | tf_op jit(solution)/shard_map/ppermute | solution.py:545
  27.1 3.9 %collective-permute-start.9 = (f32[8,128]{1,0:T(8,128)S(1)}, f32[8,128]{1,0:T(8,128)S(1)}, u32[]{:S(2)}, u32[]{:S(2)}) collective-permute-start(f32[8,128]{1,0:T(8,128)S(1)} %add.10.refs_0_), channel_id=1, source_target_pairs={{0,9},{1,8},{4,13},{5,12},{8,1},{9,0},{12,5},{13,4},{2,11},{3,10},... | collective-permute-start | bytes 12296 | tf_op jit(solution)/shard_map/ppermute | solution.py:545
  27.4 3.7 %collective-permute-start.8 = (f32[8,128]{1,0:T(8,128)S(1)}, f32[8,128]{1,0:T(8,128)S(1)}, u32[]{:S(2)}, u32[]{:S(2)}) collective-permute-start(f32[8,128]{1,0:T(8,128)S(1)} %add.10.refs_0_), channel_id=1, source_target_pairs={{0,5},{1,4},{4,1},{5,0},{8,13},{9,12},{12,9},{13,8},{2,7},{3,6},{6... | collective-permute-start | bytes 12296 | tf_op jit(solution)/shard_map/ppermute | solution.py:545
  34.4 1.2 %collective-permute-start.11 = (f32[8,128]{1,0:T(8,128)S(1)}, f32[8,128]{1,0:T(8,128)S(1)}, u32[]{:S(2)}, u32[]{:S(2)}) collective-permute-start(f32[8,128]{1,0:T(8,128)S(1)} %get-tuple-element.44), channel_id=1, source_target_pairs={{0,1},{1,0},{2,3},{3,2},{4,5},{5,4},{6,7},{7,6},{8,9},{9,8},{10,11... | collective-permute-start | bytes 12296 | tf_op jit(solution)/shard_map/ppermute | solution.py:535
  35.6 4.8 %collective-permute-start.14 = (f32[8,128]{1,0:T(8,128)S(1)}, f32[8,128]{1,0:T(8,128)S(1)}, u32[]{:S(2)}, u32[]{:S(2)}) collective-permute-start(f32[8,128]{1,0:T(8,128)S(1)} %add.11.refs_0_), channel_id=1, source_target_pairs={{0,13},{1,12},{4,9},{5,8},{8,5},{9,4},{12,1},{13,0},{2,15},{3,14},... | collective-permute-start | bytes 12296 | tf_op jit(solution)/shard_map/ppermute | solution.py:545
  37.7 4.0 %collective-permute-start.13 = (f32[8,128]{1,0:T(8,128)S(1)}, f32[8,128]{1,0:T(8,128)S(1)}, u32[]{:S(2)}, u32[]{:S(2)}) collective-permute-start(f32[8,128]{1,0:T(8,128)S(1)} %add.11.refs_0_), channel_id=1, source_target_pairs={{0,9},{1,8},{4,13},{5,12},{8,1},{9,0},{12,5},{13,4},{2,11},{3,10},... | collective-permute-start | bytes 12296 | tf_op jit(solution)/shard_map/ppermute | solution.py:545
  38.5 3.1 %collective-permute-start.12 = (f32[8,128]{1,0:T(8,128)S(1)}, f32[8,128]{1,0:T(8,128)S(1)}, u32[]{:S(2)}, u32[]{:S(2)}) collective-permute-start(f32[8,128]{1,0:T(8,128)S(1)} %add.11.refs_0_), channel_id=1, source_target_pairs={{0,5},{1,4},{4,1},{5,0},{8,13},{9,12},{12,9},{13,8},{2,7},{3,6},{6... | collective-permute-start | bytes 12296 | tf_op jit(solution)/shard_map/ppermute | solution.py:545
  43.5 1.4 %collective-permute-start.15 = (f32[2,2,16,512]{3,2,1,0:T(8,128)S(1)}, f32[2,2,16,512]{3,2,1,0:T(8,128)S(1)}, u32[]{:S(2)}, u32[]{:S(2)}) collective-permute-start(f32[2,2,16,512]{3,2,1,0:T(8,128)S(1)} %get-tuple-element.49), channel_id=1, source_target_pairs={{0,1},{1,0},{2,3},{3,2},{4,5},{5,4},{6,7},{7,6},{8,9},{9,8},{10,11... | collective-permute-start | bytes 393224 | tf_op jit(solution)/shard_map/ppermute | solution.py:662

commit v5 on v4

--- a/solution.py
+++ b/solution.py
@@ -62,7 +62,7 @@
 
 
 def pack_kernel(
-    recorded, geometry, present, intersection, pattern, keep, send, *scratch
+    recorded, geometry, present, intersection, pattern, keep, send, keep_coded, send_coded, *scratch
 ):
     sources = (recorded, geometry, present, intersection, pattern)
     local, sems, turned = scratch[:5], scratch[5], scratch[6]
@@ -81,7 +81,7 @@
     for i in range(blocks):
         turned[span * i : span * (i + 1), :] = pattern[i].astype(jnp.float32)
     base = 2 * half
-    for out, part in ((keep, rep), (send, 1 - rep)):
+    for out, coded, part in ((keep, keep_coded, rep), (send, send_coded, 1 - rep)):
         for c in range(2):
             out[c * half : (c + 1) * half, :] = recorded[c, pl.ds(part * half, half), 0, :]
         out[base : base + 8, :] = jnp.zeros((8, out.shape[1]), jnp.float32)
@@ -100,6 +100,13 @@
             out[base + 4 + t : base + 5 + t, 256:384] = geometry[1, :, sl]
             out[base + t : base + t + 1, 384:512] = present[:, sl].astype(jnp.float32)
         out[base + 4 : base + 5, 384:512] = intersection[0].astype(jnp.float32)
+        coded[0:base, :] = out[0:base, :].astype(jnp.bfloat16)
+        small = out[base : base + 8, :]
+        rest = small[:, 256:384] - rounded(small[:, 256:384])
+        parts = [rounded(rest), rounded(rest - rounded(rest)), jnp.zeros((8, 256), jnp.float32)]
+        coded[base : base + 16, :] = jnp.concatenate(
+            [small, jnp.concatenate(parts, axis=1)], axis=0
+        ).astype(jnp.bfloat16)
 
 
 def unpack_kernel(mine, theirs, coefficients, reconstruction):
@@ -179,14 +186,9 @@
     extra, refs = refs[0], refs[1:]
     cross, inline, observed, mask, updated, energy, *refs = refs
     if own:
-        matching, threshold, pay, hb, acc = refs
-        lane = iota((LANES, LANES), 1)
-        at = lane % SPAN
-        source = jnp.where(at < FOLD, lane, lane + PY - 1 + FOLD - 2 * at)
-        order = (iota((LANES, LANES), 0) == source).astype(jnp.float32)
-        threshold[...] = jnp.dot(
-            extra[...], order, precision=HIGHEST, preferred_element_type=jnp.float32
-        )
+        matching, threshold, pay, hb, acc, scale_local, sem = refs
+        scale_copy = pltpu.make_async_copy(extra, scale_local, sem)
+        scale_copy.start()
     else:
         pay, hb, acc = refs
         energy[0:4, :] = extra[...]
@@ -203,7 +205,16 @@
 
     for n in range(many):
         for s in range(2):
-            pay[n, s] = pays[s][...] if pays[s].shape == pay.shape[2:] else pays[s][window(n)]
+            source = pays[s] if len(pays[s].shape) == 2 else pays[s].at[window(n)]
+            if own:
+                pay[n, s] = source[...]
+                continue
+            pay[n, s, 0:base, :] = source[0:base, :].astype(jnp.float32)
+            small = source[base : base + 16, :].astype(jnp.float32)
+            pay[n, s, base : base + 8, :] = small[:8]
+            pay[n, s, base : base + 8, 256:384] = (
+                small[:8, 256:384] + small[8:, :LANES] + small[8:, LANES:256]
+            )
 
     def pairing(n, s):
         index = pay[n, s, base + 4 : base + 5, 384:512].astype(jnp.int32)
@@ -319,6 +330,15 @@
     lax.fori_loop(0, many * groups, first_group, 0, unroll=True)
     for n in range(many):
         pack_energy(acc[n], energy, 4 * (n + (not own)))
+    if own:
+        scale_copy.wait()
+        lane = iota((LANES, LANES), 1)
+        at = lane % SPAN
+        source = jnp.where(at < FOLD, lane, lane + PY - 1 + FOLD - 2 * at)
+        order = (iota((LANES, LANES), 0) == source).astype(jnp.float32)
+        threshold[...] = jnp.dot(
+            scale_local[...], order, precision=HIGHEST, preferred_element_type=jnp.float32
+        )
 
 
 def spread_factor(energies, threshold, factor, windows, nfreq):
@@ -567,11 +587,12 @@
         pltpu.with_memory_space_constraint(x, pltpu.HBM)
         for x in (recorded, geometry, present, intersection_index, turned)
     )
-    keep, send = pl.pallas_call(
+    coded = shape(2 * half + 16, traces, dtype=jnp.bfloat16)
+    keep, send, keep_coded, send_coded = pl.pallas_call(
         pack_kernel,
-        out_shape=(payload, payload),
+        out_shape=(payload, payload, coded, coded),
         in_specs=[HB] * 5,
-        out_specs=(VM, VM),
+        out_specs=(VM,) * 4,
         scratch_shapes=[pltpu.VMEM(x.shape, x.dtype) for x in sources]
         + [
             pltpu.SemaphoreType.DMA((5,)),
@@ -583,9 +604,13 @@
     received = lax.ppermute(send, "rep", swap)
     if windows == 2:
         diagonal = [(2 * i + r, 2 * (1 - i) + 1 - r) for i in range(2) for r in range(2)]
-        others = [lax.ppermute(keep, "win", swap), lax.ppermute(send, ("win", "rep"), diagonal)]
+        others = [
+            lax.ppermute(keep_coded, "win", swap),
+            lax.ppermute(send_coded, ("win", "rep"), diagonal),
+        ]
     else:
-        others = [lax.all_gather(keep, "win"), lax.all_gather(received, "win")]
+        received_coded = lax.ppermute(send_coded, "rep", swap)
+        others = [lax.all_gather(x, "win") for x in (keep_coded, received_coded)]
 
     rows = 2 * HALF
     energy_shape = shape(4 * windows, LANES)
@@ -612,17 +637,23 @@
         return pl.pallas_call(
             functools.partial(table_kernel, windows, nfreq, amplitude, own),
             out_shape=out_shape,
-            in_specs=[VM] * len(inputs),
+            in_specs=[VM] * (len(inputs) - 1) + [HB if own else VM],
             out_specs=(VM,) * len(out_shape),
             scratch_shapes=[pltpu.VMEM((many, 2, 2 * half + 8, traces), jnp.float32)]
-            + scratch(many),
+            + scratch(many)
+            + ([pltpu.VMEM((4, LANES), jnp.float32), pltpu.SemaphoreType.DMA] if own else []),
             compiler_params=params(windows),
             cost_estimate=pl.CostEstimate(flops=4 * 10**9, bytes_accessed=0, transcendentals=0),
             name="tables",
         )(*inputs)
 
     *tables, updated, energy, matching, threshold = build(
-        True, [keep, received, group_scale.reshape(4, LANES)]
+        True,
+        [
+            keep,
+            received,
+            pltpu.with_memory_space_constraint(group_scale.reshape(4, LANES), pltpu.HBM),
+        ],
     )
     tables, states = [tables], [updated]
     if windows > 1:

time: 45.8 us -> 44.5 us (0.972)
  waiting for transfers between devices: 12 us -> 11.3 us
  local copies, waits for them, and re-layouts: 0.68 us -> 0 us
    unnamed x2 -> x0, local copies, waits for them, and re-layouts: 0.68 us -> none
    ppermute x2, waiting for transfers between devices: 1.05 us -> 0.51 us  [the longest x1 0.51 us: per_device(): lax.ppermute(send_coded, ('win', 'rep'), diagonal)]
  transfers between devices with their start and end apart: 16 -> 16, of which waited for: 12 -> 12; matrix products, arithmetic and copies ran while one was open for 0% -> 0% of each run, Pallas kernels for 6% -> 7%
where the time goes in v5:
time: 44.5 us; the launch traced here: 44.3 us
  Pallas kernels  16.1 us (36%)
  starting transfers between devices  16.1 us (36%)
  waiting for transfers between devices  11.3 us (25%)
  between operations  0.69 us (2%)
    ppermute x9, starting transfers between devices, sum_parts(): lax.ppermute(energy, axes, crossed(k))  11.8 us
    ppermute x9, waiting for transfers between devices, sum_parts(): lax.ppermute(energy, axes, crossed(k))  6.93 us
    pallas_call x2, Pallas kernels, per_device(): pl.pallas_call(functools.partial(step_kernel, windows, nfreq, len(energie...  6.51 us
    pallas_call x2, Pallas kernels, build(): pl.pallas_call(functools.partial(table_kernel, windows, nfreq, amplitude,...  5.91 us
    ppermute x3, waiting for transfers between devices, sum_parts(): energy = energy + lax.ppermute(energy, 'rep', swap)  2.85 us
    ppermute x1, starting transfers between devices, per_device(): lax.ppermute(keep_coded, 'win', swap)  2.56 us
    pallas_call x1, Pallas kernels, per_device(): pl.pallas_call(functools.partial(final_kernel, windows, nfreq, len(energi...  1.83 us
    pallas_call x1, Pallas kernels, per_device(): pl.pallas_call(pack_kernel, out_shape=(payload, payload, coded, coded), i...  1.1 us
  transfers between devices with their start and end apart: 16, of which 12 were waited for; matrix products, arithmetic and copies ran while one was open for 0% of the time, Pallas kernels for 7%

profile of v5, /device:TPU:0, one launch (start us, length us, event | category | flops | bytes accessed | tf_op | source)
XLA Modules:
  0.0 44.3 jit_solution(955937137314041757)
XLA Ops:
  0.6 1.1 %pack.1 = (f32[40,512]{1,0:T(8,128)S(1)}, f32[40,512]{1,0:T(8,128)S(1)}, bf16[48,512]{1,0:T(8,128)(2,1)S(1)}, bf16[48,512]{1,0:T(8,128)(2,1)S(1)}) custom-call(f32[2,32,1,512]{3,2,1,0:T(1,128)} %recorded.1, f32[2,1,512]{2,1,0:T(1,128)} %geometry.1, s32[1,512]{1,0:T(1,128)} %present.1, s32[1,1,128]{2,1,0:T(1,128)} %intersection.1, s32[8,4,32]{2,1,0:T(4,128)} %bitcast.2), custom_call_target="tpu_custom_call" | custom-call | tf_op jit(solution)/shard_map/pack/pallas_call | solution.py:591
  1.7 0.5 %collective-permute-start.2 = (f32[40,512]{1,0:T(8,128)S(1)}, f32[40,512]{1,0:T(8,128)S(1)}, u32[]{:S(2)}, u32[]{:S(2)}) collective-permute-start(f32[40,512]{1,0:T(8,128)S(1)} %get-tuple-element.31), channel_id=1, source_target_pairs={{0,1},{1,0},{2,3},{3,2},{4,5},{5,4},{6,7},{7,6},{8,9},{9,8},{10,11... | collective-permute-start | bytes 245768 | tf_op jit(solution)/shard_map/ppermute | solution.py:604
  2.3 2.6 %collective-permute-start = (bf16[48,512]{1,0:T(8,128)(2,1)S(1)}, bf16[48,512]{1,0:T(8,128)(2,1)S(1)}, u32[]{:S(2)}, u32[]{:S(2)}) collective-permute-start(bf16[48,512]{1,0:T(8,128)(2,1)S(1)} %get-tuple-element.28), channel_id=1, source_target_pairs={{0,2},{2,0},{1,3},{3,1},{4,6},{6,4},{5,7},{7,5},{8,10},{10,8},{9,1... | collective-permute-start | bytes 147464 | tf_op jit(solution)/shard_map/ppermute | solution.py:608
  4.8 0.1 collective-permute-start.1
  4.9 0.0 collective-permute-done.2.refs_1_
  4.9 3.1 %tables.2 = (bf16[1,2,8,256,128]{4,3,2,1,0:T(8,128)(2,1)S(1)}, f32[1,2,256,1024]{3,2,1,0:T(8,128)S(1)}, f32[1,2,2,8,1024]{4,3,2,1,0:T(8,128)S(1)}, f32[1,8,1024]...) custom-call(f32[40,512]{1,0:T(8,128)S(1)} %get-tuple-element.30.refs, ...), custom_call_target="tpu_custom_call" | custom-call | flops 4000000000 | tf_op jit(solution)/shard_map/tables/pallas_call | solution.py:637
  8.0 0.0 collective-permute-done.refs_0_
  8.0 0.5 %collective-permute-done.1.refs_1_ = bf16[48,512]{1,0:T(8,128)(2,1)S(1)} collective-permute-done((bf16[48,512]{1,0:T(8,128)(2,1)S(1)}, bf16[48,512]{1,0:T(8,128)(2,1)S(1)}, u32[]{:S(2)}, u32[]{:S(2)}) %collective-permute-start.1) | collective-permute-done | bytes 49184 | tf_op jit(solution)/shard_map/ppermute | solution.py:609
  8.5 2.8 %tables.3 = (bf16[1,2,8,256,128]{4,3,2,1,0:T(8,128)(2,1)S(1)}, f32[1,2,256,1024]{3,2,1,0:T(8,128)S(1)}, f32[1,2,2,8,1024]{4,3,2,1,0:T(8,128)S(1)}, f32[1,8,1024]...) custom-call(bf16[48,512]{1,0:T(8,128)(2,1)S(1)} %collective-permute-done.refs_0_, ...), custom_call_target="tpu_custom_call" | custom-call | flops 4000000000 | tf_op jit(solution)/shard_map/tables/pallas_call | solution.py:637
  11.3 0.2 collective-permute-start.3
  11.6 1.0 %collective-permute-done.3 = f32[8,128]{1,0:T(8,128)S(1)} collective-permute-done((f32[8,128]{1,0:T(8,128)S(1)}, f32[8,128]{1,0:T(8,128)S(1)}, u32[]{:S(2)}, u32[]{:S(2)}) %collective-permute-start.3) | collective-permute-done | bytes 4128 | tf_op jit(solution)/shard_map/ppermute | solution.py:555
  12.6 3.4 %collective-permute-start.6 = (f32[8,128]{1,0:T(8,128)S(1)}, f32[8,128]{1,0:T(8,128)S(1)}, u32[]{:S(2)}, u32[]{:S(2)}) collective-permute-start(f32[8,128]{1,0:T(8,128)S(1)} %add.9.refs_0_), channel_id=1, source_target_pairs={{0,13},{1,12},{4,9},{5,8},{8,5},{9,4},{12,1},{13,0},{2,15},{3,14},... | collective-permute-start | bytes 12296 | tf_op jit(solution)/shard_map/ppermute | solution.py:565
  15.9 0.0 collective-permute-start.5
  15.9 0.5 %collective-permute-start.4 = (f32[8,128]{1,0:T(8,128)S(1)}, f32[8,128]{1,0:T(8,128)S(1)}, u32[]{:S(2)}, u32[]{:S(2)}) collective-permute-start(f32[8,128]{1,0:T(8,128)S(1)} %add.9.refs_0_), channel_id=1, source_target_pairs={{0,5},{1,4},{4,1},{5,0},{8,13},{9,12},{12,9},{13,8},{2,7},{3,6},{6... | collective-permute-start | bytes 12296 | tf_op jit(solution)/shard_map/ppermute | solution.py:565
  16.5 0.9 %collective-permute-done.6.refs_3_ = f32[8,128]{1,0:T(8,128)S(1)} collective-permute-done((f32[8,128]{1,0:T(8,128)S(1)}, f32[8,128]{1,0:T(8,128)S(1)}, u32[]{:S(2)}, u32[]{:S(2)}) %collective-permute-start.6) | collective-permute-done | bytes 4128 | tf_op jit(solution)/shard_map/ppermute | solution.py:565
  17.4 2.5 %collective-permute-done.5.refs_2_ = f32[8,128]{1,0:T(8,128)S(1)} collective-permute-done((f32[8,128]{1,0:T(8,128)S(1)}, f32[8,128]{1,0:T(8,128)S(1)}, u32[]{:S(2)}, u32[]{:S(2)}) %collective-permute-start.5) | collective-permute-done | bytes 4128 | tf_op jit(solution)/shard_map/ppermute | solution.py:565
  19.9 0.0 collective-permute-done.4.refs_1_
  19.9 3.3 %step.2 = (f32[1,2,256,128]{3,2,1,0:T(8,128)S(1)}, f32[1,2,256,128]{3,2,1,0:T(8,128)S(1)}, f32[8,128]{1,0:T(8,128)S(1)}) custom-call(f32[8,128]{1,0:T(8,128)S(1)} %add.9.refs_0_, f32[8,128]{1,0:T(8,128)S(1)} %collective-permute-done.4.refs_1_, f32[8,128]{1,0:T(8,128)S(1)} %collective-permute-done.5.refs_2_, f32[8,128]{1,0:T(8,128)S(1)} %collective-permute-done.6.refs_3_, ...), custom_call_target="tpu_custom_call" | custom-call | tf_op jit(solution)/shard_map/step/pallas_call | solution.py:670
  23.1 0.4 collective-permute-start.7
  23.5 0.8 %collective-permute-done.7 = f32[8,128]{1,0:T(8,128)S(1)} collective-permute-done((f32[8,128]{1,0:T(8,128)S(1)}, f32[8,128]{1,0:T(8,128)S(1)}, u32[]{:S(2)}, u32[]{:S(2)}) %collective-permute-start.7) | collective-permute-done | bytes 4128 | tf_op jit(solution)/shard_map/ppermute | solution.py:555
  24.4 1.4 %collective-permute-start.10 = (f32[8,128]{1,0:T(8,128)S(1)}, f32[8,128]{1,0:T(8,128)S(1)}, u32[]{:S(2)}, u32[]{:S(2)}) collective-permute-start(f32[8,128]{1,0:T(8,128)S(1)} %add.10.refs_0_), channel_id=1, source_target_pairs={{0,13},{1,12},{4,9},{5,8},{8,5},{9,4},{12,1},{13,0},{2,15},{3,14},... | collective-permute-start | bytes 12296 | tf_op jit(solution)/shard_map/ppermute | solution.py:565
  25.8 0.3 collective-permute-start.9
  26.1 2.3 %collective-permute-start.8 = (f32[8,128]{1,0:T(8,128)S(1)}, f32[8,128]{1,0:T(8,128)S(1)}, u32[]{:S(2)}, u32[]{:S(2)}) collective-permute-start(f32[8,128]{1,0:T(8,128)S(1)} %add.10.refs_0_), channel_id=1, source_target_pairs={{0,5},{1,4},{4,1},{5,0},{8,13},{9,12},{12,9},{13,8},{2,7},{3,6},{6... | collective-permute-start | bytes 12296 | tf_op jit(solution)/shard_map/ppermute | solution.py:565
  28.4 0.8 %collective-permute-done.10.refs_3_ = f32[8,128]{1,0:T(8,128)S(1)} collective-permute-done((f32[8,128]{1,0:T(8,128)S(1)}, f32[8,128]{1,0:T(8,128)S(1)}, u32[]{:S(2)}, u32[]{:S(2)}) %collective-permute-start.10) | collective-permute-done | bytes 4128 | tf_op jit(solution)/shard_map/ppermute | solution.py:565
  29.2 0.5 %collective-permute-done.9.refs_2_ = f32[8,128]{1,0:T(8,128)S(1)} collective-permute-done((f32[8,128]{1,0:T(8,128)S(1)}, f32[8,128]{1,0:T(8,128)S(1)}, u32[]{:S(2)}, u32[]{:S(2)}) %collective-permute-start.9) | collective-permute-done | bytes 4128 | tf_op jit(solution)/shard_map/ppermute | solution.py:565
  29.7 0.1 collective-permute-done.8.refs_1_
  29.8 3.3 %step.3 = (f32[1,2,256,128]{3,2,1,0:T(8,128)S(1)}, f32[1,2,256,128]{3,2,1,0:T(8,128)S(1)}, f32[8,128]{1,0:T(8,128)S(1)}) custom-call(f32[8,128]{1,0:T(8,128)S(1)} %add.10.refs_0_, f32[8,128]{1,0:T(8,128)S(1)} %collective-permute-done.8.refs_1_, f32[8,128]{1,0:T(8,128)S(1)} %collective-permute-done.9.refs_2_, f32[8,128]{1,0:T(8,128)S(1)} %collective-permute-done.10.refs_3_, ...), custom_call_target="tpu_custom_call" | custom-call | tf_op jit(solution)/shard_map/step/pallas_call | solution.py:670
  33.1 0.2 collective-permute-start.11
  33.3 1.0 %collective-permute-done.11 = f32[8,128]{1,0:T(8,128)S(1)} collective-permute-done((f32[8,128]{1,0:T(8,128)S(1)}, f32[8,128]{1,0:T(8,128)S(1)}, u32[]{:S(2)}, u32[]{:S(2)}) %collective-permute-start.11) | collective-permute-done | bytes 4128 | tf_op jit(solution)/shard_map/ppermute | solution.py:555
  34.3 2.1 %collective-permute-start.14 = (f32[8,128]{1,0:T(8,128)S(1)}, f32[8,128]{1,0:T(8,128)S(1)}, u32[]{:S(2)}, u32[]{:S(2)}) collective-permute-start(f32[8,128]{1,0:T(8,128)S(1)} %add.11.refs_0_), channel_id=1, source_target_pairs={{0,13},{1,12},{4,9},{5,8},{8,5},{9,4},{12,1},{13,0},{2,15},{3,14},... | collective-permute-start | bytes 12296 | tf_op jit(solution)/shard_map/ppermute | solution.py:565
  36.4 0.8 %collective-permute-start.13 = (f32[8,128]{1,0:T(8,128)S(1)}, f32[8,128]{1,0:T(8,128)S(1)}, u32[]{:S(2)}, u32[]{:S(2)}) collective-permute-start(f32[8,128]{1,0:T(8,128)S(1)} %add.11.refs_0_), channel_id=1, source_target_pairs={{0,9},{1,8},{4,13},{5,12},{8,1},{9,0},{12,5},{13,4},{2,11},{3,10},... | collective-permute-start | bytes 12296 | tf_op jit(solution)/shard_map/ppermute | solution.py:565
  37.2 1.0 %collective-permute-start.12 = (f32[8,128]{1,0:T(8,128)S(1)}, f32[8,128]{1,0:T(8,128)S(1)}, u32[]{:S(2)}, u32[]{:S(2)}) collective-permute-start(f32[8,128]{1,0:T(8,128)S(1)} %add.11.refs_0_), channel_id=1, source_target_pairs={{0,5},{1,4},{4,1},{5,0},{8,13},{9,12},{12,9},{13,8},{2,7},{3,6},{6... | collective-permute-start | bytes 12296 | tf_op jit(solution)/shard_map/ppermute | solution.py:565
  38.2 0.9 %collective-permute-done.14.refs_3_ = f32[8,128]{1,0:T(8,128)S(1)} collective-permute-done((f32[8,128]{1,0:T(8,128)S(1)}, f32[8,128]{1,0:T(8,128)S(1)}, u32[]{:S(2)}, u32[]{:S(2)}) %collective-permute-start.14) | collective-permute-done | bytes 4128 | tf_op jit(solution)/shard_map/ppermute | solution.py:565
  39.1 1.2 %collective-permute-done.13.refs_2_ = f32[8,128]{1,0:T(8,128)S(1)} collective-permute-done((f32[8,128]{1,0:T(8,128)S(1)}, f32[8,128]{1,0:T(8,128)S(1)}, u32[]{:S(2)}, u32[]{:S(2)}) %collective-permute-start.13) | collective-permute-done | bytes 4128 | tf_op jit(solution)/shard_map/ppermute | solution.py:565
  40.3 0.0 collective-permute-done.12.refs_1_
  40.3 1.8 %final.1 = (f32[2,2,16,512]{3,2,1,0:T(8,128)S(1)}, f32[2,2,16,512]{3,2,1,0:T(8,128)S(1)}) custom-call(f32[8,128]{1,0:T(8,128)S(1)} %add.11.refs_0_, f32[8,128]{1,0:T(8,128)S(1)} %collective-permute-done.12.refs_1_, f32[8,128]{1,0:T(8,128)S(1)} %collective-permute-done.13.refs_2_, f32[8,128]{1,0:T(8,128)S(1)} %collective-permute-done.14.refs_3_, ...), custom_call_target="tpu_custom_call" | custom-call | tf_op jit(solution)/shard_map/final/pallas_call | solution.py:684
  42.2 0.3 collective-permute-start.15
  42.5 1.0 %collective-permute-done.15.theirs = f32[2,2,16,512]{3,2,1,0:T(8,128)S(1)} collective-permute-done((f32[2,2,16,512]{3,2,1,0:T(8,128)S(1)}, f32[2,2,16,512]{3,2,1,0:T(8,128)S(1)}, u32[]{:S(2)}, u32[]{:S(2)}) %collective-permute-start.15) | collective-permute-done | bytes 131104 | tf_op jit(solution)/shard_map/ppermute | solution.py:693
  43.5 0.7 %unpack.1 = (f32[2,32,1,512]{3,2,1,0:T(1,128)}, f32[2,32,1,512]{3,2,1,0:T(1,128)}) custom-call(f32[2,2,16,512]{3,2,1,0:T(8,128)S(1)} %get-tuple-element.52.mine, f32[2,2,16,512]{3,2,1,0:T(8,128)S(1)} %collective-permute-done.15.theirs), custom_call_target="tpu_custom_call" | custom-call | tf_op jit(solution)/shard_map/unpack/pallas_call | solution.py:695
  (3 shorter events, 0.0 us)
Async XLA Ops:
  1.7 3.2 %collective-permute-start.2 = (f32[40,512]{1,0:T(8,128)S(1)}, f32[40,512]{1,0:T(8,128)S(1)}, u32[]{:S(2)}, u32[]{:S(2)}) collective-permute-start(f32[40,512]{1,0:T(8,128)S(1)} %get-tuple-element.31), channel_id=1, source_target_pairs={{0,1},{1,0},{2,3},{3,2},{4,5},{5,4},{6,7},{7,6},{8,9},{9,8},{10,11... | collective-permute-start | bytes 245768 | tf_op jit(solution)/shard_map/ppermute | solution.py:604
  2.3 5.7 %collective-permute-start = (bf16[48,512]{1,0:T(8,128)(2,1)S(1)}, bf16[48,512]{1,0:T(8,128)(2,1)S(1)}, u32[]{:S(2)}, u32[]{:S(2)}) collective-permute-start(bf16[48,512]{1,0:T(8,128)(2,1)S(1)} %get-tuple-element.28), channel_id=1, source_target_pairs={{0,2},{2,0},{1,3},{3,1},{4,6},{6,4},{5,7},{7,5},{8,10},{10,8},{9,1... | collective-permute-start | bytes 147464 | tf_op jit(solution)/shard_map/ppermute | solution.py:608
  4.8 3.7 %collective-permute-start.1 = (bf16[48,512]{1,0:T(8,128)(2,1)S(1)}, bf16[48,512]{1,0:T(8,128)(2,1)S(1)}, u32[]{:S(2)}, u32[]{:S(2)}) collective-permute-start(bf16[48,512]{1,0:T(8,128)(2,1)S(1)} %get-tuple-element.29), channel_id=1, source_target_pairs={{0,3},{1,2},{2,1},{3,0},{4,7},{5,6},{6,5},{7,4},{8,11},{9,10},{10,... | collective-permute-start | bytes 147464 | tf_op jit(solution)/shard_map/ppermute | solution.py:609
  11.3 1.2 %collective-permute-start.3 = (f32[8,128]{1,0:T(8,128)S(1)}, f32[8,128]{1,0:T(8,128)S(1)}, u32[]{:S(2)}, u32[]{:S(2)}) collective-permute-start(f32[8,128]{1,0:T(8,128)S(1)} %get-tuple-element.33), channel_id=1, source_target_pairs={{0,1},{1,0},{2,3},{3,2},{4,5},{5,4},{6,7},{7,6},{8,9},{9,8},{10,11... | collective-permute-start | bytes 12296 | tf_op jit(solution)/shard_map/ppermute | solution.py:555
  12.6 4.8 %collective-permute-start.6 = (f32[8,128]{1,0:T(8,128)S(1)}, f32[8,128]{1,0:T(8,128)S(1)}, u32[]{:S(2)}, u32[]{:S(2)}) collective-permute-start(f32[8,128]{1,0:T(8,128)S(1)} %add.9.refs_0_), channel_id=1, source_target_pairs={{0,13},{1,12},{4,9},{5,8},{8,5},{9,4},{12,1},{13,0},{2,15},{3,14},... | collective-permute-start | bytes 12296 | tf_op jit(solution)/shard_map/ppermute | solution.py:565
  15.9 3.9 %collective-permute-start.5 = (f32[8,128]{1,0:T(8,128)S(1)}, f32[8,128]{1,0:T(8,128)S(1)}, u32[]{:S(2)}, u32[]{:S(2)}) collective-permute-start(f32[8,128]{1,0:T(8,128)S(1)} %add.9.refs_0_), channel_id=1, source_target_pairs={{0,9},{1,8},{4,13},{5,12},{8,1},{9,0},{12,5},{13,4},{2,11},{3,10},... | collective-permute-start | bytes 12296 | tf_op jit(solution)/shard_map/ppermute | solution.py:565
  15.9 3.9 %collective-permute-start.4 = (f32[8,128]{1,0:T(8,128)S(1)}, f32[8,128]{1,0:T(8,128)S(1)}, u32[]{:S(2)}, u32[]{:S(2)}) collective-permute-start(f32[8,128]{1,0:T(8,128)S(1)} %add.9.refs_0_), channel_id=1, source_target_pairs={{0,5},{1,4},{4,1},{5,0},{8,13},{9,12},{12,9},{13,8},{2,7},{3,6},{6... | collective-permute-start | bytes 12296 | tf_op jit(solution)/shard_map/ppermute | solution.py:565
  23.1 1.2 %collective-permute-start.7 = (f32[8,128]{1,0:T(8,128)S(1)}, f32[8,128]{1,0:T(8,128)S(1)}, u32[]{:S(2)}, u32[]{:S(2)}) collective-permute-start(f32[8,128]{1,0:T(8,128)S(1)} %get-tuple-element.45), channel_id=1, source_target_pairs={{0,1},{1,0},{2,3},{3,2},{4,5},{5,4},{6,7},{7,6},{8,9},{9,8},{10,11... | collective-permute-start | bytes 12296 | tf_op jit(solution)/shard_map/ppermute | solution.py:555
  24.4 4.8 %collective-permute-start.10 = (f32[8,128]{1,0:T(8,128)S(1)}, f32[8,128]{1,0:T(8,128)S(1)}, u32[]{:S(2)}, u32[]{:S(2)}) collective-permute-start(f32[8,128]{1,0:T(8,128)S(1)} %add.10.refs_0_), channel_id=1, source_target_pairs={{0,13},{1,12},{4,9},{5,8},{8,5},{9,4},{12,1},{13,0},{2,15},{3,14},... | collective-permute-start | bytes 12296 | tf_op jit(solution)/shard_map/ppermute | solution.py:565
  25.8 3.9 %collective-permute-start.9 = (f32[8,128]{1,0:T(8,128)S(1)}, f32[8,128]{1,0:T(8,128)S(1)}, u32[]{:S(2)}, u32[]{:S(2)}) collective-permute-start(f32[8,128]{1,0:T(8,128)S(1)} %add.10.refs_0_), channel_id=1, source_target_pairs={{0,9},{1,8},{4,13},{5,12},{8,1},{9,0},{12,5},{13,4},{2,11},{3,10},... | collective-permute-start | bytes 12296 | tf_op jit(solution)/shard_map/ppermute | solution.py:565
  26.1 3.7 %collective-permute-start.8 = (f32[8,128]{1,0:T(8,128)S(1)}, f32[8,128]{1,0:T(8,128)S(1)}, u32[]{:S(2)}, u32[]{:S(2)}) collective-permute-start(f32[8,128]{1,0:T(8,128)S(1)} %add.10.refs_0_), channel_id=1, source_target_pairs={{0,5},{1,4},{4,1},{5,0},{8,13},{9,12},{12,9},{13,8},{2,7},{3,6},{6... | collective-permute-start | bytes 12296 | tf_op jit(solution)/shard_map/ppermute | solution.py:565
  33.1 1.2 %collective-permute-start.11 = (f32[8,128]{1,0:T(8,128)S(1)}, f32[8,128]{1,0:T(8,128)S(1)}, u32[]{:S(2)}, u32[]{:S(2)}) collective-permute-start(f32[8,128]{1,0:T(8,128)S(1)} %get-tuple-element.48), channel_id=1, source_target_pairs={{0,1},{1,0},{2,3},{3,2},{4,5},{5,4},{6,7},{7,6},{8,9},{9,8},{10,11... | collective-permute-start | bytes 12296 | tf_op jit(solution)/shard_map/ppermute | solution.py:555
  34.3 4.8 %collective-permute-start.14 = (f32[8,128]{1,0:T(8,128)S(1)}, f32[8,128]{1,0:T(8,128)S(1)}, u32[]{:S(2)}, u32[]{:S(2)}) collective-permute-start(f32[8,128]{1,0:T(8,128)S(1)} %add.11.refs_0_), channel_id=1, source_target_pairs={{0,13},{1,12},{4,9},{5,8},{8,5},{9,4},{12,1},{13,0},{2,15},{3,14},... | collective-permute-start | bytes 12296 | tf_op jit(solution)/shard_map/ppermute | solution.py:565
  36.4 4.0 %collective-permute-start.13 = (f32[8,128]{1,0:T(8,128)S(1)}, f32[8,128]{1,0:T(8,128)S(1)}, u32[]{:S(2)}, u32[]{:S(2)}) collective-permute-start(f32[8,128]{1,0:T(8,128)S(1)} %add.11.refs_0_), channel_id=1, source_target_pairs={{0,9},{1,8},{4,13},{5,12},{8,1},{9,0},{12,5},{13,4},{2,11},{3,10},... | collective-permute-start | bytes 12296 | tf_op jit(solution)/shard_map/ppermute | solution.py:565
  37.2 3.1 %collective-permute-start.12 = (f32[8,128]{1,0:T(8,128)S(1)}, f32[8,128]{1,0:T(8,128)S(1)}, u32[]{:S(2)}, u32[]{:S(2)}) collective-permute-start(f32[8,128]{1,0:T(8,128)S(1)} %add.11.refs_0_), channel_id=1, source_target_pairs={{0,5},{1,4},{4,1},{5,0},{8,13},{9,12},{12,9},{13,8},{2,7},{3,6},{6... | collective-permute-start | bytes 12296 | tf_op jit(solution)/shard_map/ppermute | solution.py:565
  42.2 1.4 %collective-permute-start.15 = (f32[2,2,16,512]{3,2,1,0:T(8,128)S(1)}, f32[2,2,16,512]{3,2,1,0:T(8,128)S(1)}, u32[]{:S(2)}, u32[]{:S(2)}) collective-permute-start(f32[2,2,16,512]{3,2,1,0:T(8,128)S(1)} %get-tuple-element.53), channel_id=1, source_target_pairs={{0,1},{1,0},{2,3},{3,2},{4,5},{5,4},{6,7},{7,6},{8,9},{9,8},{10,11... | collective-permute-start | bytes 393224 | tf_op jit(solution)/shard_map/ppermute | solution.py:693

commit v6 on v5

--- a/solution.py
+++ b/solution.py
@@ -55,6 +55,20 @@
 
 def rounded(x):
     return x.astype(jnp.bfloat16).astype(jnp.float32)
+
+
+def choose(values, hot, transposed=False):
+    rest = values - rounded(values)
+    last = rest - rounded(rest)
+    parts = jnp.concatenate([values, rest, last], axis=0).astype(jnp.bfloat16)
+    out = lax.dot_general(
+        parts,
+        hot.astype(jnp.bfloat16),
+        (((1,), (1 if transposed else 0,)), ((), ())),
+        preferred_element_type=jnp.float32,
+    )
+    n = values.shape[0]
+    return out[:n] + (out[n : 2 * n] + out[2 * n :])
 
 
 def times(p, q):
@@ -227,22 +241,19 @@
 
     def align(n, _):
         n, s = n // 2, n % 2
-        hot = pairing(n, s)
-        dot = functools.partial(
-            lax.dot_general,
-            dimension_numbers=(((1,), (1,)), ((), ())),
-            precision=HIGHEST,
-            preferred_element_type=jnp.float32,
-        )
-        pay[n, s, 0:half, 0:LANES] = dot(pay[n, s, 0:half, 0:LANES], hot)
-        geo = dot(pay[n, s, base : base + 8, 256:384], hot)
-        pay[n, s, base : base + 1, 256:384] = geo[0:1]
-        pay[n, s, base + 4 : base + 5, 256:384] = geo[4:5]
-        here = dot(pay[n, s, base : base + 8, 384:512], hot)
-        pay[n, s, base : base + 1, 384:512] = here[0:1]
+        lead = [
+            pay[n, s, 0:half, 0:LANES],
+            pay[n, s, base : base + 8, 256:384],
+            pay[n, s, base : base + 8, 384:512],
+        ]
+        lead = choose(jnp.concatenate(lead, axis=0), pairing(n, s), transposed=True)
+        pay[n, s, 0:half, 0:LANES] = lead[:half]
+        pay[n, s, base : base + 1, 256:384] = lead[half : half + 1]
+        pay[n, s, base + 4 : base + 5, 256:384] = lead[half + 4 : half + 5]
+        pay[n, s, base : base + 1, 384:512] = lead[half + 8 : half + 9]
         return 0
 
-    lax.fori_loop(0, 2 * many, align, 0)
+    lax.fori_loop(0, 2 * many, align, 0, unroll=many == 1)
 
     sub = iota((8, LANES), 0)
     delta = 0.75 / nfreq
@@ -511,7 +522,7 @@
                     jnp.where(win < windows - 1, high[c], trail[c]) for c in range(2)
                 )
         spans = jnp.where(wide == 0, current[:HALF], jnp.where(wide == 1, current[HALF:], 0.0))
-        spans = jnp.dot(spans, order, precision=HIGHEST, preferred_element_type=jnp.float32)
+        spans = choose(spans, order)
         sl = slice(GROUP * g, GROUP * (g + 1))
         for c in range(2):
             for j in range(4):
@@ -529,13 +540,11 @@
                 out = keep if t < 4 else swap
                 out[1, c, sl, lanes] = traces[t][c]
     for s, out in enumerate((keep, swap)):
+        lead = choose(
+            jnp.concatenate([out[1, c, :, :LANES] for c in range(2)], axis=0), matching[s]
+        )
         for c in range(2):
-            out[1, c, :, :LANES] = jnp.dot(
-                out[1, c, :, :LANES],
-                matching[s],
-                precision=HIGHEST,
-                preferred_element_type=jnp.float32,
-            )
+            out[1, c, :, :LANES] = lead[c * out.shape[2] : (c + 1) * out.shape[2]]
 
 
 VM = pl.BlockSpec(memory_space=pltpu.VMEM)

time: 44.5 us -> 43.6 us (0.980)
  Pallas kernels: 16.1 us -> 14.5 us
  waiting for transfers between devices: 11.3 us -> 12 us
    pallas_call x2, Pallas kernels: 5.91 us -> 4.55 us  [build(): pl.pallas_call(functools.partial(table_kernel, windows, nfreq, amplitude,...]
    ppermute x1, waiting for transfers between devices: 0.51 us -> 1.21 us  [per_device(): lax.ppermute(send_coded, ('win', 'rep'), diagonal)]
  transfers between devices with their start and end apart: 16 -> 16, of which waited for: 12 -> 12; matrix products, arithmetic and copies ran while one was open for 0% -> 0% of each run, Pallas kernels for 7% -> 6%
where the time goes in v6:
time: 43.6 us; the launch traced here: 43.4 us
  starting transfers between devices  16.1 us (37%)
  Pallas kernels  14.5 us (33%)
  waiting for transfers between devices  12 us (28%)
  between operations  0.69 us (2%)
    ppermute x9, starting transfers between devices, sum_parts(): lax.ppermute(energy, axes, crossed(k))  11.8 us
    ppermute x9, waiting for transfers between devices, sum_parts(): lax.ppermute(energy, axes, crossed(k))  6.93 us
    pallas_call x2, Pallas kernels, per_device(): pl.pallas_call(functools.partial(step_kernel, windows, nfreq, len(energie...  6.52 us
    pallas_call x2, Pallas kernels, build(): pl.pallas_call(functools.partial(table_kernel, windows, nfreq, amplitude,...  4.55 us
    ppermute x3, waiting for transfers between devices, sum_parts(): energy = energy + lax.ppermute(energy, 'rep', swap)  2.86 us
    ppermute x1, starting transfers between devices, per_device(): lax.ppermute(keep_coded, 'win', swap)  2.56 us
    pallas_call x1, Pallas kernels, per_device(): pl.pallas_call(functools.partial(final_kernel, windows, nfreq, len(energi...  1.62 us
    ppermute x1, waiting for transfers between devices, per_device(): lax.ppermute(send_coded, ('win', 'rep'), diagonal)  1.21 us
  transfers between devices with their start and end apart: 16, of which 12 were waited for; matrix products, arithmetic and copies ran while one was open for 0% of the time, Pallas kernels for 6%

profile of v6, /device:TPU:0, one launch (start us, length us, event | category | flops | bytes accessed | tf_op | source)
XLA Modules:
  0.0 43.4 jit_solution(8084368142374366924)
XLA Ops:
  0.6 1.1 %pack.1 = (f32[40,512]{1,0:T(8,128)S(1)}, f32[40,512]{1,0:T(8,128)S(1)}, bf16[48,512]{1,0:T(8,128)(2,1)S(1)}, bf16[48,512]{1,0:T(8,128)(2,1)S(1)}) custom-call(f32[2,32,1,512]{3,2,1,0:T(1,128)} %recorded.1, f32[2,1,512]{2,1,0:T(1,128)} %geometry.1, s32[1,512]{1,0:T(1,128)} %present.1, s32[1,1,128]{2,1,0:T(1,128)} %intersection.1, s32[8,4,32]{2,1,0:T(4,128)} %bitcast.2), custom_call_target="tpu_custom_call" | custom-call | tf_op jit(solution)/shard_map/pack/pallas_call | solution.py:600
  1.7 0.5 %collective-permute-start.2 = (f32[40,512]{1,0:T(8,128)S(1)}, f32[40,512]{1,0:T(8,128)S(1)}, u32[]{:S(2)}, u32[]{:S(2)}) collective-permute-start(f32[40,512]{1,0:T(8,128)S(1)} %get-tuple-element.31), channel_id=1, source_target_pairs={{0,1},{1,0},{2,3},{3,2},{4,5},{5,4},{6,7},{7,6},{8,9},{9,8},{10,11... | collective-permute-start | bytes 245768 | tf_op jit(solution)/shard_map/ppermute | solution.py:613
  2.3 2.6 %collective-permute-start = (bf16[48,512]{1,0:T(8,128)(2,1)S(1)}, bf16[48,512]{1,0:T(8,128)(2,1)S(1)}, u32[]{:S(2)}, u32[]{:S(2)}) collective-permute-start(bf16[48,512]{1,0:T(8,128)(2,1)S(1)} %get-tuple-element.28), channel_id=1, source_target_pairs={{0,2},{2,0},{1,3},{3,1},{4,6},{6,4},{5,7},{7,5},{8,10},{10,8},{9,1... | collective-permute-start | bytes 147464 | tf_op jit(solution)/shard_map/ppermute | solution.py:617
  4.8 0.1 collective-permute-start.1
  4.9 0.0 collective-permute-done.2.refs_1_
  4.9 2.4 %tables.2 = (bf16[1,2,8,256,128]{4,3,2,1,0:T(8,128)(2,1)S(1)}, f32[1,2,256,1024]{3,2,1,0:T(8,128)S(1)}, f32[1,2,2,8,1024]{4,3,2,1,0:T(8,128)S(1)}, f32[1,8,1024]...) custom-call(f32[40,512]{1,0:T(8,128)S(1)} %get-tuple-element.30.refs, ...), custom_call_target="tpu_custom_call" | custom-call | flops 4000000000 | tf_op jit(solution)/shard_map/tables/pallas_call | solution.py:646
  7.3 0.0 collective-permute-done.refs_0_
  7.3 1.2 %collective-permute-done.1.refs_1_ = bf16[48,512]{1,0:T(8,128)(2,1)S(1)} collective-permute-done((bf16[48,512]{1,0:T(8,128)(2,1)S(1)}, bf16[48,512]{1,0:T(8,128)(2,1)S(1)}, u32[]{:S(2)}, u32[]{:S(2)}) %collective-permute-start.1) | collective-permute-done | bytes 49184 | tf_op jit(solution)/shard_map/ppermute | solution.py:618
  8.5 2.2 %tables.3 = (bf16[1,2,8,256,128]{4,3,2,1,0:T(8,128)(2,1)S(1)}, f32[1,2,256,1024]{3,2,1,0:T(8,128)S(1)}, f32[1,2,2,8,1024]{4,3,2,1,0:T(8,128)S(1)}, f32[1,8,1024]...) custom-call(bf16[48,512]{1,0:T(8,128)(2,1)S(1)} %collective-permute-done.refs_0_, ...), custom_call_target="tpu_custom_call" | custom-call | flops 4000000000 | tf_op jit(solution)/shard_map/tables/pallas_call | solution.py:646
  10.7 0.2 collective-permute-start.3
  10.9 1.0 %collective-permute-done.3 = f32[8,128]{1,0:T(8,128)S(1)} collective-permute-done((f32[8,128]{1,0:T(8,128)S(1)}, f32[8,128]{1,0:T(8,128)S(1)}, u32[]{:S(2)}, u32[]{:S(2)}) %collective-permute-start.3) | collective-permute-done | bytes 4128 | tf_op jit(solution)/shard_map/ppermute | solution.py:564
  11.9 3.4 %collective-permute-start.6 = (f32[8,128]{1,0:T(8,128)S(1)}, f32[8,128]{1,0:T(8,128)S(1)}, u32[]{:S(2)}, u32[]{:S(2)}) collective-permute-start(f32[8,128]{1,0:T(8,128)S(1)} %add.9.refs_0_), channel_id=1, source_target_pairs={{0,13},{1,12},{4,9},{5,8},{8,5},{9,4},{12,1},{13,0},{2,15},{3,14},... | collective-permute-start | bytes 12296 | tf_op jit(solution)/shard_map/ppermute | solution.py:574
  15.3 0.0 collective-permute-start.5
  15.3 0.5 %collective-permute-start.4 = (f32[8,128]{1,0:T(8,128)S(1)}, f32[8,128]{1,0:T(8,128)S(1)}, u32[]{:S(2)}, u32[]{:S(2)}) collective-permute-start(f32[8,128]{1,0:T(8,128)S(1)} %add.9.refs_0_), channel_id=1, source_target_pairs={{0,5},{1,4},{4,1},{5,0},{8,13},{9,12},{12,9},{13,8},{2,7},{3,6},{6... | collective-permute-start | bytes 12296 | tf_op jit(solution)/shard_map/ppermute | solution.py:574
  15.8 0.9 %collective-permute-done.6.refs_3_ = f32[8,128]{1,0:T(8,128)S(1)} collective-permute-done((f32[8,128]{1,0:T(8,128)S(1)}, f32[8,128]{1,0:T(8,128)S(1)}, u32[]{:S(2)}, u32[]{:S(2)}) %collective-permute-start.6) | collective-permute-done | bytes 4128 | tf_op jit(solution)/shard_map/ppermute | solution.py:574
  16.7 2.5 %collective-permute-done.5.refs_2_ = f32[8,128]{1,0:T(8,128)S(1)} collective-permute-done((f32[8,128]{1,0:T(8,128)S(1)}, f32[8,128]{1,0:T(8,128)S(1)}, u32[]{:S(2)}, u32[]{:S(2)}) %collective-permute-start.5) | collective-permute-done | bytes 4128 | tf_op jit(solution)/shard_map/ppermute | solution.py:574
  19.2 0.0 collective-permute-done.4.refs_1_
  19.2 3.3 %step.2 = (f32[1,2,256,128]{3,2,1,0:T(8,128)S(1)}, f32[1,2,256,128]{3,2,1,0:T(8,128)S(1)}, f32[8,128]{1,0:T(8,128)S(1)}) custom-call(f32[8,128]{1,0:T(8,128)S(1)} %add.9.refs_0_, f32[8,128]{1,0:T(8,128)S(1)} %collective-permute-done.4.refs_1_, f32[8,128]{1,0:T(8,128)S(1)} %collective-permute-done.5.refs_2_, f32[8,128]{1,0:T(8,128)S(1)} %collective-permute-done.6.refs_3_, ...), custom_call_target="tpu_custom_call" | custom-call | tf_op jit(solution)/shard_map/step/pallas_call | solution.py:679
  22.5 0.4 collective-permute-start.7
  22.9 0.8 %collective-permute-done.7 = f32[8,128]{1,0:T(8,128)S(1)} collective-permute-done((f32[8,128]{1,0:T(8,128)S(1)}, f32[8,128]{1,0:T(8,128)S(1)}, u32[]{:S(2)}, u32[]{:S(2)}) %collective-permute-start.7) | collective-permute-done | bytes 4128 | tf_op jit(solution)/shard_map/ppermute | solution.py:564
  23.7 1.4 %collective-permute-start.10 = (f32[8,128]{1,0:T(8,128)S(1)}, f32[8,128]{1,0:T(8,128)S(1)}, u32[]{:S(2)}, u32[]{:S(2)}) collective-permute-start(f32[8,128]{1,0:T(8,128)S(1)} %add.10.refs_0_), channel_id=1, source_target_pairs={{0,13},{1,12},{4,9},{5,8},{8,5},{9,4},{12,1},{13,0},{2,15},{3,14},... | collective-permute-start | bytes 12296 | tf_op jit(solution)/shard_map/ppermute | solution.py:574
  25.1 0.3 collective-permute-start.9
  25.5 2.3 %collective-permute-start.8 = (f32[8,128]{1,0:T(8,128)S(1)}, f32[8,128]{1,0:T(8,128)S(1)}, u32[]{:S(2)}, u32[]{:S(2)}) collective-permute-start(f32[8,128]{1,0:T(8,128)S(1)} %add.10.refs_0_), channel_id=1, source_target_pairs={{0,5},{1,4},{4,1},{5,0},{8,13},{9,12},{12,9},{13,8},{2,7},{3,6},{6... | collective-permute-start | bytes 12296 | tf_op jit(solution)/shard_map/ppermute | solution.py:574
  27.8 0.8 %collective-permute-done.10.refs_3_ = f32[8,128]{1,0:T(8,128)S(1)} collective-permute-done((f32[8,128]{1,0:T(8,128)S(1)}, f32[8,128]{1,0:T(8,128)S(1)}, u32[]{:S(2)}, u32[]{:S(2)}) %collective-permute-start.10) | collective-permute-done | bytes 4128 | tf_op jit(solution)/shard_map/ppermute | solution.py:574
  28.5 0.5 %collective-permute-done.9.refs_2_ = f32[8,128]{1,0:T(8,128)S(1)} collective-permute-done((f32[8,128]{1,0:T(8,128)S(1)}, f32[8,128]{1,0:T(8,128)S(1)}, u32[]{:S(2)}, u32[]{:S(2)}) %collective-permute-start.9) | collective-permute-done | bytes 4128 | tf_op jit(solution)/shard_map/ppermute | solution.py:574
  29.1 0.1 collective-permute-done.8.refs_1_
  29.1 3.3 %step.3 = (f32[1,2,256,128]{3,2,1,0:T(8,128)S(1)}, f32[1,2,256,128]{3,2,1,0:T(8,128)S(1)}, f32[8,128]{1,0:T(8,128)S(1)}) custom-call(f32[8,128]{1,0:T(8,128)S(1)} %add.10.refs_0_, f32[8,128]{1,0:T(8,128)S(1)} %collective-permute-done.8.refs_1_, f32[8,128]{1,0:T(8,128)S(1)} %collective-permute-done.9.refs_2_, f32[8,128]{1,0:T(8,128)S(1)} %collective-permute-done.10.refs_3_, ...), custom_call_target="tpu_custom_call" | custom-call | tf_op jit(solution)/shard_map/step/pallas_call | solution.py:679
  32.4 0.2 collective-permute-start.11
  32.6 1.0 %collective-permute-done.11 = f32[8,128]{1,0:T(8,128)S(1)} collective-permute-done((f32[8,128]{1,0:T(8,128)S(1)}, f32[8,128]{1,0:T(8,128)S(1)}, u32[]{:S(2)}, u32[]{:S(2)}) %collective-permute-start.11) | collective-permute-done | bytes 4128 | tf_op jit(solution)/shard_map/ppermute | solution.py:564
  33.6 2.0 %collective-permute-start.14 = (f32[8,128]{1,0:T(8,128)S(1)}, f32[8,128]{1,0:T(8,128)S(1)}, u32[]{:S(2)}, u32[]{:S(2)}) collective-permute-start(f32[8,128]{1,0:T(8,128)S(1)} %add.11.refs_0_), channel_id=1, source_target_pairs={{0,13},{1,12},{4,9},{5,8},{8,5},{9,4},{12,1},{13,0},{2,15},{3,14},... | collective-permute-start | bytes 12296 | tf_op jit(solution)/shard_map/ppermute | solution.py:574
  35.7 0.8 %collective-permute-start.13 = (f32[8,128]{1,0:T(8,128)S(1)}, f32[8,128]{1,0:T(8,128)S(1)}, u32[]{:S(2)}, u32[]{:S(2)}) collective-permute-start(f32[8,128]{1,0:T(8,128)S(1)} %add.11.refs_0_), channel_id=1, source_target_pairs={{0,9},{1,8},{4,13},{5,12},{8,1},{9,0},{12,5},{13,4},{2,11},{3,10},... | collective-permute-start | bytes 12296 | tf_op jit(solution)/shard_map/ppermute | solution.py:574
  36.5 1.0 %collective-permute-start.12 = (f32[8,128]{1,0:T(8,128)S(1)}, f32[8,128]{1,0:T(8,128)S(1)}, u32[]{:S(2)}, u32[]{:S(2)}) collective-permute-start(f32[8,128]{1,0:T(8,128)S(1)} %add.11.refs_0_), channel_id=1, source_target_pairs={{0,5},{1,4},{4,1},{5,0},{8,13},{9,12},{12,9},{13,8},{2,7},{3,6},{6... | collective-permute-start | bytes 12296 | tf_op jit(solution)/shard_map/ppermute | solution.py:574
  37.5 0.9 %collective-permute-done.14.refs_3_ = f32[8,128]{1,0:T(8,128)S(1)} collective-permute-done((f32[8,128]{1,0:T(8,128)S(1)}, f32[8,128]{1,0:T(8,128)S(1)}, u32[]{:S(2)}, u32[]{:S(2)}) %collective-permute-start.14) | collective-permute-done | bytes 4128 | tf_op jit(solution)/shard_map/ppermute | solution.py:574
  38.5 1.2 %collective-permute-done.13.refs_2_ = f32[8,128]{1,0:T(8,128)S(1)} collective-permute-done((f32[8,128]{1,0:T(8,128)S(1)}, f32[8,128]{1,0:T(8,128)S(1)}, u32[]{:S(2)}, u32[]{:S(2)}) %collective-permute-start.13) | collective-permute-done | bytes 4128 | tf_op jit(solution)/shard_map/ppermute | solution.py:574
  39.7 0.0 collective-permute-done.12.refs_1_
  39.7 1.6 %final.1 = (f32[2,2,16,512]{3,2,1,0:T(8,128)S(1)}, f32[2,2,16,512]{3,2,1,0:T(8,128)S(1)}) custom-call(f32[8,128]{1,0:T(8,128)S(1)} %add.11.refs_0_, f32[8,128]{1,0:T(8,128)S(1)} %collective-permute-done.12.refs_1_, f32[8,128]{1,0:T(8,128)S(1)} %collective-permute-done.13.refs_2_, f32[8,128]{1,0:T(8,128)S(1)} %collective-permute-done.14.refs_3_, ...), custom_call_target="tpu_custom_call" | custom-call | tf_op jit(solution)/shard_map/final/pallas_call | solution.py:693
  41.3 0.3 collective-permute-start.15
  41.6 1.0 %collective-permute-done.15.theirs = f32[2,2,16,512]{3,2,1,0:T(8,128)S(1)} collective-permute-done((f32[2,2,16,512]{3,2,1,0:T(8,128)S(1)}, f32[2,2,16,512]{3,2,1,0:T(8,128)S(1)}, u32[]{:S(2)}, u32[]{:S(2)}) %collective-permute-start.15) | collective-permute-done | bytes 131104 | tf_op jit(solution)/shard_map/ppermute | solution.py:702
  42.6 0.7 %unpack.1 = (f32[2,32,1,512]{3,2,1,0:T(1,128)}, f32[2,32,1,512]{3,2,1,0:T(1,128)}) custom-call(f32[2,2,16,512]{3,2,1,0:T(8,128)S(1)} %get-tuple-element.52.mine, f32[2,2,16,512]{3,2,1,0:T(8,128)S(1)} %collective-permute-done.15.theirs), custom_call_target="tpu_custom_call" | custom-call | tf_op jit(solution)/shard_map/unpack/pallas_call | solution.py:704
  (3 shorter events, 0.0 us)
Async XLA Ops:
  1.7 3.2 %collective-permute-start.2 = (f32[40,512]{1,0:T(8,128)S(1)}, f32[40,512]{1,0:T(8,128)S(1)}, u32[]{:S(2)}, u32[]{:S(2)}) collective-permute-start(f32[40,512]{1,0:T(8,128)S(1)} %get-tuple-element.31), channel_id=1, source_target_pairs={{0,1},{1,0},{2,3},{3,2},{4,5},{5,4},{6,7},{7,6},{8,9},{9,8},{10,11... | collective-permute-start | bytes 245768 | tf_op jit(solution)/shard_map/ppermute | solution.py:613
  2.3 5.0 %collective-permute-start = (bf16[48,512]{1,0:T(8,128)(2,1)S(1)}, bf16[48,512]{1,0:T(8,128)(2,1)S(1)}, u32[]{:S(2)}, u32[]{:S(2)}) collective-permute-start(bf16[48,512]{1,0:T(8,128)(2,1)S(1)} %get-tuple-element.28), channel_id=1, source_target_pairs={{0,2},{2,0},{1,3},{3,1},{4,6},{6,4},{5,7},{7,5},{8,10},{10,8},{9,1... | collective-permute-start | bytes 147464 | tf_op jit(solution)/shard_map/ppermute | solution.py:617
  4.8 3.7 %collective-permute-start.1 = (bf16[48,512]{1,0:T(8,128)(2,1)S(1)}, bf16[48,512]{1,0:T(8,128)(2,1)S(1)}, u32[]{:S(2)}, u32[]{:S(2)}) collective-permute-start(bf16[48,512]{1,0:T(8,128)(2,1)S(1)} %get-tuple-element.29), channel_id=1, source_target_pairs={{0,3},{1,2},{2,1},{3,0},{4,7},{5,6},{6,5},{7,4},{8,11},{9,10},{10,... | collective-permute-start | bytes 147464 | tf_op jit(solution)/shard_map/ppermute | solution.py:618
  10.7 1.2 %collective-permute-start.3 = (f32[8,128]{1,0:T(8,128)S(1)}, f32[8,128]{1,0:T(8,128)S(1)}, u32[]{:S(2)}, u32[]{:S(2)}) collective-permute-start(f32[8,128]{1,0:T(8,128)S(1)} %get-tuple-element.33), channel_id=1, source_target_pairs={{0,1},{1,0},{2,3},{3,2},{4,5},{5,4},{6,7},{7,6},{8,9},{9,8},{10,11... | collective-permute-start | bytes 12296 | tf_op jit(solution)/shard_map/ppermute | solution.py:564
  11.9 4.8 %collective-permute-start.6 = (f32[8,128]{1,0:T(8,128)S(1)}, f32[8,128]{1,0:T(8,128)S(1)}, u32[]{:S(2)}, u32[]{:S(2)}) collective-permute-start(f32[8,128]{1,0:T(8,128)S(1)} %add.9.refs_0_), channel_id=1, source_target_pairs={{0,13},{1,12},{4,9},{5,8},{8,5},{9,4},{12,1},{13,0},{2,15},{3,14},... | collective-permute-start | bytes 12296 | tf_op jit(solution)/shard_map/ppermute | solution.py:574
  15.3 3.9 %collective-permute-start.5 = (f32[8,128]{1,0:T(8,128)S(1)}, f32[8,128]{1,0:T(8,128)S(1)}, u32[]{:S(2)}, u32[]{:S(2)}) collective-permute-start(f32[8,128]{1,0:T(8,128)S(1)} %add.9.refs_0_), channel_id=1, source_target_pairs={{0,9},{1,8},{4,13},{5,12},{8,1},{9,0},{12,5},{13,4},{2,11},{3,10},... | collective-permute-start | bytes 12296 | tf_op jit(solution)/shard_map/ppermute | solution.py:574
  15.3 3.9 %collective-permute-start.4 = (f32[8,128]{1,0:T(8,128)S(1)}, f32[8,128]{1,0:T(8,128)S(1)}, u32[]{:S(2)}, u32[]{:S(2)}) collective-permute-start(f32[8,128]{1,0:T(8,128)S(1)} %add.9.refs_0_), channel_id=1, source_target_pairs={{0,5},{1,4},{4,1},{5,0},{8,13},{9,12},{12,9},{13,8},{2,7},{3,6},{6... | collective-permute-start | bytes 12296 | tf_op jit(solution)/shard_map/ppermute | solution.py:574
  22.5 1.2 %collective-permute-start.7 = (f32[8,128]{1,0:T(8,128)S(1)}, f32[8,128]{1,0:T(8,128)S(1)}, u32[]{:S(2)}, u32[]{:S(2)}) collective-permute-start(f32[8,128]{1,0:T(8,128)S(1)} %get-tuple-element.45), channel_id=1, source_target_pairs={{0,1},{1,0},{2,3},{3,2},{4,5},{5,4},{6,7},{7,6},{8,9},{9,8},{10,11... | collective-permute-start | bytes 12296 | tf_op jit(solution)/shard_map/ppermute | solution.py:564
  23.7 4.8 %collective-permute-start.10 = (f32[8,128]{1,0:T(8,128)S(1)}, f32[8,128]{1,0:T(8,128)S(1)}, u32[]{:S(2)}, u32[]{:S(2)}) collective-permute-start(f32[8,128]{1,0:T(8,128)S(1)} %add.10.refs_0_), channel_id=1, source_target_pairs={{0,13},{1,12},{4,9},{5,8},{8,5},{9,4},{12,1},{13,0},{2,15},{3,14},... | collective-permute-start | bytes 12296 | tf_op jit(solution)/shard_map/ppermute | solution.py:574
  25.1 3.9 %collective-permute-start.9 = (f32[8,128]{1,0:T(8,128)S(1)}, f32[8,128]{1,0:T(8,128)S(1)}, u32[]{:S(2)}, u32[]{:S(2)}) collective-permute-start(f32[8,128]{1,0:T(8,128)S(1)} %add.10.refs_0_), channel_id=1, source_target_pairs={{0,9},{1,8},{4,13},{5,12},{8,1},{9,0},{12,5},{13,4},{2,11},{3,10},... | collective-permute-start | bytes 12296 | tf_op jit(solution)/shard_map/ppermute | solution.py:574
  25.5 3.7 %collective-permute-start.8 = (f32[8,128]{1,0:T(8,128)S(1)}, f32[8,128]{1,0:T(8,128)S(1)}, u32[]{:S(2)}, u32[]{:S(2)}) collective-permute-start(f32[8,128]{1,0:T(8,128)S(1)} %add.10.refs_0_), channel_id=1, source_target_pairs={{0,5},{1,4},{4,1},{5,0},{8,13},{9,12},{12,9},{13,8},{2,7},{3,6},{6... | collective-permute-start | bytes 12296 | tf_op jit(solution)/shard_map/ppermute | solution.py:574
  32.4 1.2 %collective-permute-start.11 = (f32[8,128]{1,0:T(8,128)S(1)}, f32[8,128]{1,0:T(8,128)S(1)}, u32[]{:S(2)}, u32[]{:S(2)}) collective-permute-start(f32[8,128]{1,0:T(8,128)S(1)} %get-tuple-element.48), channel_id=1, source_target_pairs={{0,1},{1,0},{2,3},{3,2},{4,5},{5,4},{6,7},{7,6},{8,9},{9,8},{10,11... | collective-permute-start | bytes 12296 | tf_op jit(solution)/shard_map/ppermute | solution.py:564
  33.6 4.8 %collective-permute-start.14 = (f32[8,128]{1,0:T(8,128)S(1)}, f32[8,128]{1,0:T(8,128)S(1)}, u32[]{:S(2)}, u32[]{:S(2)}) collective-permute-start(f32[8,128]{1,0:T(8,128)S(1)} %add.11.refs_0_), channel_id=1, source_target_pairs={{0,13},{1,12},{4,9},{5,8},{8,5},{9,4},{12,1},{13,0},{2,15},{3,14},... | collective-permute-start | bytes 12296 | tf_op jit(solution)/shard_map/ppermute | solution.py:574
  35.7 4.0 %collective-permute-start.13 = (f32[8,128]{1,0:T(8,128)S(1)}, f32[8,128]{1,0:T(8,128)S(1)}, u32[]{:S(2)}, u32[]{:S(2)}) collective-permute-start(f32[8,128]{1,0:T(8,128)S(1)} %add.11.refs_0_), channel_id=1, source_target_pairs={{0,9},{1,8},{4,13},{5,12},{8,1},{9,0},{12,5},{13,4},{2,11},{3,10},... | collective-permute-start | bytes 12296 | tf_op jit(solution)/shard_map/ppermute | solution.py:574
  36.5 3.1 %collective-permute-start.12 = (f32[8,128]{1,0:T(8,128)S(1)}, f32[8,128]{1,0:T(8,128)S(1)}, u32[]{:S(2)}, u32[]{:S(2)}) collective-permute-start(f32[8,128]{1,0:T(8,128)S(1)} %add.11.refs_0_), channel_id=1, source_target_pairs={{0,5},{1,4},{4,1},{5,0},{8,13},{9,12},{12,9},{13,8},{2,7},{3,6},{6... | collective-permute-start | bytes 12296 | tf_op jit(solution)/shard_map/ppermute | solution.py:574
  41.3 1.4 %collective-permute-start.15 = (f32[2,2,16,512]{3,2,1,0:T(8,128)S(1)}, f32[2,2,16,512]{3,2,1,0:T(8,128)S(1)}, u32[]{:S(2)}, u32[]{:S(2)}) collective-permute-start(f32[2,2,16,512]{3,2,1,0:T(8,128)S(1)} %get-tuple-element.53), channel_id=1, source_target_pairs={{0,1},{1,0},{2,3},{3,2},{4,5},{5,4},{6,7},{7,6},{8,9},{9,8},{10,11... | collective-permute-start | bytes 393224 | tf_op jit(solution)/shard_map/ppermute | solution.py:702

commit v7 on v6

--- a/solution.py
+++ b/solution.py
@@ -146,12 +146,17 @@
 
 def project_group(hb, cross, w, g, masks, sign):
     tiles = hb.shape[0]
-    g = lax.dot_general(
-        jnp.concatenate([hb[n] for n in range(tiles)], axis=1),
-        side_by_side(cross, w, g, 0, tiles),
-        (((1,), (1,)), ((), ())),
-        preferred_element_type=jnp.float32,
+    half = tiles // 2
+    first, second = (
+        lax.dot_general(
+            jnp.concatenate([hb[n] for n in range(k, k + half)], axis=1),
+            side_by_side(cross, w, g, k, half),
+            (((1,), (1,)), ((), ())),
+            preferred_element_type=jnp.float32,
+        )
+        for k in (0, half)
     )
+    g = first + second
     g = jnp.where(masks[0], g[:, :LANES], jnp.where(masks[1], g[:, LANES:], 0.0))
     g = g + pltpu.roll(g, 32, 1)
     g = g + pltpu.roll(g, 64, 1)

time: 43.6 us -> 43.5 us (level)
  no operation moved by 1% of the time
where the time goes in v7:
time: 43.5 us; the launch traced here: 43.3 us
  starting transfers between devices  16.1 us (37%)
  Pallas kernels  14.4 us (33%)
  waiting for transfers between devices  12 us (28%)
  between operations  0.69 us (2%)
    ppermute x9, starting transfers between devices, sum_parts(): lax.ppermute(energy, axes, crossed(k))  11.8 us
    ppermute x9, waiting for transfers between devices, sum_parts(): lax.ppermute(energy, axes, crossed(k))  6.93 us
    pallas_call x2, Pallas kernels, per_device(): pl.pallas_call(functools.partial(step_kernel, windows, nfreq, len(energie...  6.4 us
    pallas_call x2, Pallas kernels, build(): pl.pallas_call(functools.partial(table_kernel, windows, nfreq, amplitude,...  4.55 us
    ppermute x3, waiting for transfers between devices, sum_parts(): energy = energy + lax.ppermute(energy, 'rep', swap)  2.85 us
    ppermute x1, starting transfers between devices, per_device(): lax.ppermute(keep_coded, 'win', swap)  2.56 us
    pallas_call x1, Pallas kernels, per_device(): pl.pallas_call(functools.partial(final_kernel, windows, nfreq, len(energi...  1.62 us
    ppermute x1, waiting for transfers between devices, per_device(): lax.ppermute(send_coded, ('win', 'rep'), diagonal)  1.21 us
  transfers between devices with their start and end apart: 16, of which 12 were waited for; matrix products, arithmetic and copies ran while one was open for 0% of the time, Pallas kernels for 6%

profile of v7, /device:TPU:0, one launch (start us, length us, event | category | flops | bytes accessed | tf_op | source)
XLA Modules:
  0.0 43.3 jit_solution(2921830893659259728)
XLA Ops:
  0.6 1.1 %pack.1 = (f32[40,512]{1,0:T(8,128)S(1)}, f32[40,512]{1,0:T(8,128)S(1)}, bf16[48,512]{1,0:T(8,128)(2,1)S(1)}, bf16[48,512]{1,0:T(8,128)(2,1)S(1)}) custom-call(f32[2,32,1,512]{3,2,1,0:T(1,128)} %recorded.1, f32[2,1,512]{2,1,0:T(1,128)} %geometry.1, s32[1,512]{1,0:T(1,128)} %present.1, s32[1,1,128]{2,1,0:T(1,128)} %intersection.1, s32[8,4,32]{2,1,0:T(4,128)} %bitcast.2), custom_call_target="tpu_custom_call" | custom-call | tf_op jit(solution)/shard_map/pack/pallas_call | solution.py:605
  1.7 0.5 %collective-permute-start.2 = (f32[40,512]{1,0:T(8,128)S(1)}, f32[40,512]{1,0:T(8,128)S(1)}, u32[]{:S(2)}, u32[]{:S(2)}) collective-permute-start(f32[40,512]{1,0:T(8,128)S(1)} %get-tuple-element.31), channel_id=1, source_target_pairs={{0,1},{1,0},{2,3},{3,2},{4,5},{5,4},{6,7},{7,6},{8,9},{9,8},{10,11... | collective-permute-start | bytes 245768 | tf_op jit(solution)/shard_map/ppermute | solution.py:618
  2.3 2.6 %collective-permute-start = (bf16[48,512]{1,0:T(8,128)(2,1)S(1)}, bf16[48,512]{1,0:T(8,128)(2,1)S(1)}, u32[]{:S(2)}, u32[]{:S(2)}) collective-permute-start(bf16[48,512]{1,0:T(8,128)(2,1)S(1)} %get-tuple-element.28), channel_id=1, source_target_pairs={{0,2},{2,0},{1,3},{3,1},{4,6},{6,4},{5,7},{7,5},{8,10},{10,8},{9,1... | collective-permute-start | bytes 147464 | tf_op jit(solution)/shard_map/ppermute | solution.py:622
  4.8 0.1 collective-permute-start.1
  4.9 0.0 collective-permute-done.2.refs_1_
  4.9 2.4 %tables.2 = (bf16[1,2,8,256,128]{4,3,2,1,0:T(8,128)(2,1)S(1)}, f32[1,2,256,1024]{3,2,1,0:T(8,128)S(1)}, f32[1,2,2,8,1024]{4,3,2,1,0:T(8,128)S(1)}, f32[1,8,1024]...) custom-call(f32[40,512]{1,0:T(8,128)S(1)} %get-tuple-element.30.refs, ...), custom_call_target="tpu_custom_call" | custom-call | flops 4000000000 | tf_op jit(solution)/shard_map/tables/pallas_call | solution.py:651
  7.3 0.0 collective-permute-done.refs_0_
  7.3 1.2 %collective-permute-done.1.refs_1_ = bf16[48,512]{1,0:T(8,128)(2,1)S(1)} collective-permute-done((bf16[48,512]{1,0:T(8,128)(2,1)S(1)}, bf16[48,512]{1,0:T(8,128)(2,1)S(1)}, u32[]{:S(2)}, u32[]{:S(2)}) %collective-permute-start.1) | collective-permute-done | bytes 49184 | tf_op jit(solution)/shard_map/ppermute | solution.py:623
  8.5 2.1 %tables.3 = (bf16[1,2,8,256,128]{4,3,2,1,0:T(8,128)(2,1)S(1)}, f32[1,2,256,1024]{3,2,1,0:T(8,128)S(1)}, f32[1,2,2,8,1024]{4,3,2,1,0:T(8,128)S(1)}, f32[1,8,1024]...) custom-call(bf16[48,512]{1,0:T(8,128)(2,1)S(1)} %collective-permute-done.refs_0_, ...), custom_call_target="tpu_custom_call" | custom-call | flops 4000000000 | tf_op jit(solution)/shard_map/tables/pallas_call | solution.py:651
  10.7 0.2 collective-permute-start.3
  10.9 1.0 %collective-permute-done.3 = f32[8,128]{1,0:T(8,128)S(1)} collective-permute-done((f32[8,128]{1,0:T(8,128)S(1)}, f32[8,128]{1,0:T(8,128)S(1)}, u32[]{:S(2)}, u32[]{:S(2)}) %collective-permute-start.3) | collective-permute-done | bytes 4128 | tf_op jit(solution)/shard_map/ppermute | solution.py:569
  11.9 3.4 %collective-permute-start.6 = (f32[8,128]{1,0:T(8,128)S(1)}, f32[8,128]{1,0:T(8,128)S(1)}, u32[]{:S(2)}, u32[]{:S(2)}) collective-permute-start(f32[8,128]{1,0:T(8,128)S(1)} %add.9.refs_0_), channel_id=1, source_target_pairs={{0,13},{1,12},{4,9},{5,8},{8,5},{9,4},{12,1},{13,0},{2,15},{3,14},... | collective-permute-start | bytes 12296 | tf_op jit(solution)/shard_map/ppermute | solution.py:579
  15.3 0.0 collective-permute-start.5
  15.3 0.5 %collective-permute-start.4 = (f32[8,128]{1,0:T(8,128)S(1)}, f32[8,128]{1,0:T(8,128)S(1)}, u32[]{:S(2)}, u32[]{:S(2)}) collective-permute-start(f32[8,128]{1,0:T(8,128)S(1)} %add.9.refs_0_), channel_id=1, source_target_pairs={{0,5},{1,4},{4,1},{5,0},{8,13},{9,12},{12,9},{13,8},{2,7},{3,6},{6... | collective-permute-start | bytes 12296 | tf_op jit(solution)/shard_map/ppermute | solution.py:579
  15.8 0.9 %collective-permute-done.6.refs_3_ = f32[8,128]{1,0:T(8,128)S(1)} collective-permute-done((f32[8,128]{1,0:T(8,128)S(1)}, f32[8,128]{1,0:T(8,128)S(1)}, u32[]{:S(2)}, u32[]{:S(2)}) %collective-permute-start.6) | collective-permute-done | bytes 4128 | tf_op jit(solution)/shard_map/ppermute | solution.py:579
  16.7 2.5 %collective-permute-done.5.refs_2_ = f32[8,128]{1,0:T(8,128)S(1)} collective-permute-done((f32[8,128]{1,0:T(8,128)S(1)}, f32[8,128]{1,0:T(8,128)S(1)}, u32[]{:S(2)}, u32[]{:S(2)}) %collective-permute-start.5) | collective-permute-done | bytes 4128 | tf_op jit(solution)/shard_map/ppermute | solution.py:579
  19.2 0.0 collective-permute-done.4.refs_1_
  19.2 3.2 %step.2 = (f32[1,2,256,128]{3,2,1,0:T(8,128)S(1)}, f32[1,2,256,128]{3,2,1,0:T(8,128)S(1)}, f32[8,128]{1,0:T(8,128)S(1)}) custom-call(f32[8,128]{1,0:T(8,128)S(1)} %add.9.refs_0_, f32[8,128]{1,0:T(8,128)S(1)} %collective-permute-done.4.refs_1_, f32[8,128]{1,0:T(8,128)S(1)} %collective-permute-done.5.refs_2_, f32[8,128]{1,0:T(8,128)S(1)} %collective-permute-done.6.refs_3_, ...), custom_call_target="tpu_custom_call" | custom-call | tf_op jit(solution)/shard_map/step/pallas_call | solution.py:684
  22.4 0.4 collective-permute-start.7
  22.8 0.8 %collective-permute-done.7 = f32[8,128]{1,0:T(8,128)S(1)} collective-permute-done((f32[8,128]{1,0:T(8,128)S(1)}, f32[8,128]{1,0:T(8,128)S(1)}, u32[]{:S(2)}, u32[]{:S(2)}) %collective-permute-start.7) | collective-permute-done | bytes 4128 | tf_op jit(solution)/shard_map/ppermute | solution.py:569
  23.7 1.4 %collective-permute-start.10 = (f32[8,128]{1,0:T(8,128)S(1)}, f32[8,128]{1,0:T(8,128)S(1)}, u32[]{:S(2)}, u32[]{:S(2)}) collective-permute-start(f32[8,128]{1,0:T(8,128)S(1)} %add.10.refs_0_), channel_id=1, source_target_pairs={{0,13},{1,12},{4,9},{5,8},{8,5},{9,4},{12,1},{13,0},{2,15},{3,14},... | collective-permute-start | bytes 12296 | tf_op jit(solution)/shard_map/ppermute | solution.py:579
  25.1 0.3 collective-permute-start.9
  25.4 2.3 %collective-permute-start.8 = (f32[8,128]{1,0:T(8,128)S(1)}, f32[8,128]{1,0:T(8,128)S(1)}, u32[]{:S(2)}, u32[]{:S(2)}) collective-permute-start(f32[8,128]{1,0:T(8,128)S(1)} %add.10.refs_0_), channel_id=1, source_target_pairs={{0,5},{1,4},{4,1},{5,0},{8,13},{9,12},{12,9},{13,8},{2,7},{3,6},{6... | collective-permute-start | bytes 12296 | tf_op jit(solution)/shard_map/ppermute | solution.py:579
  27.7 0.8 %collective-permute-done.10.refs_3_ = f32[8,128]{1,0:T(8,128)S(1)} collective-permute-done((f32[8,128]{1,0:T(8,128)S(1)}, f32[8,128]{1,0:T(8,128)S(1)}, u32[]{:S(2)}, u32[]{:S(2)}) %collective-permute-start.10) | collective-permute-done | bytes 4128 | tf_op jit(solution)/shard_map/ppermute | solution.py:579
  28.5 0.5 %collective-permute-done.9.refs_2_ = f32[8,128]{1,0:T(8,128)S(1)} collective-permute-done((f32[8,128]{1,0:T(8,128)S(1)}, f32[8,128]{1,0:T(8,128)S(1)}, u32[]{:S(2)}, u32[]{:S(2)}) %collective-permute-start.9) | collective-permute-done | bytes 4128 | tf_op jit(solution)/shard_map/ppermute | solution.py:579
  29.0 0.1 collective-permute-done.8.refs_1_
  29.1 3.2 %step.3 = (f32[1,2,256,128]{3,2,1,0:T(8,128)S(1)}, f32[1,2,256,128]{3,2,1,0:T(8,128)S(1)}, f32[8,128]{1,0:T(8,128)S(1)}) custom-call(f32[8,128]{1,0:T(8,128)S(1)} %add.10.refs_0_, f32[8,128]{1,0:T(8,128)S(1)} %collective-permute-done.8.refs_1_, f32[8,128]{1,0:T(8,128)S(1)} %collective-permute-done.9.refs_2_, f32[8,128]{1,0:T(8,128)S(1)} %collective-permute-done.10.refs_3_, ...), custom_call_target="tpu_custom_call" | custom-call | tf_op jit(solution)/shard_map/step/pallas_call | solution.py:684
  32.3 0.2 collective-permute-start.11
  32.5 1.0 %collective-permute-done.11 = f32[8,128]{1,0:T(8,128)S(1)} collective-permute-done((f32[8,128]{1,0:T(8,128)S(1)}, f32[8,128]{1,0:T(8,128)S(1)}, u32[]{:S(2)}, u32[]{:S(2)}) %collective-permute-start.11) | collective-permute-done | bytes 4128 | tf_op jit(solution)/shard_map/ppermute | solution.py:569
  33.5 2.1 %collective-permute-start.14 = (f32[8,128]{1,0:T(8,128)S(1)}, f32[8,128]{1,0:T(8,128)S(1)}, u32[]{:S(2)}, u32[]{:S(2)}) collective-permute-start(f32[8,128]{1,0:T(8,128)S(1)} %add.11.refs_0_), channel_id=1, source_target_pairs={{0,13},{1,12},{4,9},{5,8},{8,5},{9,4},{12,1},{13,0},{2,15},{3,14},... | collective-permute-start | bytes 12296 | tf_op jit(solution)/shard_map/ppermute | solution.py:579
  35.6 0.8 %collective-permute-start.13 = (f32[8,128]{1,0:T(8,128)S(1)}, f32[8,128]{1,0:T(8,128)S(1)}, u32[]{:S(2)}, u32[]{:S(2)}) collective-permute-start(f32[8,128]{1,0:T(8,128)S(1)} %add.11.refs_0_), channel_id=1, source_target_pairs={{0,9},{1,8},{4,13},{5,12},{8,1},{9,0},{12,5},{13,4},{2,11},{3,10},... | collective-permute-start | bytes 12296 | tf_op jit(solution)/shard_map/ppermute | solution.py:579
  36.4 1.0 %collective-permute-start.12 = (f32[8,128]{1,0:T(8,128)S(1)}, f32[8,128]{1,0:T(8,128)S(1)}, u32[]{:S(2)}, u32[]{:S(2)}) collective-permute-start(f32[8,128]{1,0:T(8,128)S(1)} %add.11.refs_0_), channel_id=1, source_target_pairs={{0,5},{1,4},{4,1},{5,0},{8,13},{9,12},{12,9},{13,8},{2,7},{3,6},{6... | collective-permute-start | bytes 12296 | tf_op jit(solution)/shard_map/ppermute | solution.py:579
  37.4 0.9 %collective-permute-done.14.refs_3_ = f32[8,128]{1,0:T(8,128)S(1)} collective-permute-done((f32[8,128]{1,0:T(8,128)S(1)}, f32[8,128]{1,0:T(8,128)S(1)}, u32[]{:S(2)}, u32[]{:S(2)}) %collective-permute-start.14) | collective-permute-done | bytes 4128 | tf_op jit(solution)/shard_map/ppermute | solution.py:579
  38.4 1.2 %collective-permute-done.13.refs_2_ = f32[8,128]{1,0:T(8,128)S(1)} collective-permute-done((f32[8,128]{1,0:T(8,128)S(1)}, f32[8,128]{1,0:T(8,128)S(1)}, u32[]{:S(2)}, u32[]{:S(2)}) %collective-permute-start.13) | collective-permute-done | bytes 4128 | tf_op jit(solution)/shard_map/ppermute | solution.py:579
  39.6 0.0 collective-permute-done.12.refs_1_
  39.6 1.6 %final.1 = (f32[2,2,16,512]{3,2,1,0:T(8,128)S(1)}, f32[2,2,16,512]{3,2,1,0:T(8,128)S(1)}) custom-call(f32[8,128]{1,0:T(8,128)S(1)} %add.11.refs_0_, f32[8,128]{1,0:T(8,128)S(1)} %collective-permute-done.12.refs_1_, f32[8,128]{1,0:T(8,128)S(1)} %collective-permute-done.13.refs_2_, f32[8,128]{1,0:T(8,128)S(1)} %collective-permute-done.14.refs_3_, ...), custom_call_target="tpu_custom_call" | custom-call | tf_op jit(solution)/shard_map/final/pallas_call | solution.py:698
  41.2 0.3 collective-permute-start.15
  41.5 1.0 %collective-permute-done.15.theirs = f32[2,2,16,512]{3,2,1,0:T(8,128)S(1)} collective-permute-done((f32[2,2,16,512]{3,2,1,0:T(8,128)S(1)}, f32[2,2,16,512]{3,2,1,0:T(8,128)S(1)}, u32[]{:S(2)}, u32[]{:S(2)}) %collective-permute-start.15) | collective-permute-done | bytes 131104 | tf_op jit(solution)/shard_map/ppermute | solution.py:707
  42.5 0.7 %unpack.1 = (f32[2,32,1,512]{3,2,1,0:T(1,128)}, f32[2,32,1,512]{3,2,1,0:T(1,128)}) custom-call(f32[2,2,16,512]{3,2,1,0:T(8,128)S(1)} %get-tuple-element.52.mine, f32[2,2,16,512]{3,2,1,0:T(8,128)S(1)} %collective-permute-done.15.theirs), custom_call_target="tpu_custom_call" | custom-call | tf_op jit(solution)/shard_map/unpack/pallas_call | solution.py:709
  (3 shorter events, 0.0 us)
Async XLA Ops:
  1.7 3.2 %collective-permute-start.2 = (f32[40,512]{1,0:T(8,128)S(1)}, f32[40,512]{1,0:T(8,128)S(1)}, u32[]{:S(2)}, u32[]{:S(2)}) collective-permute-start(f32[40,512]{1,0:T(8,128)S(1)} %get-tuple-element.31), channel_id=1, source_target_pairs={{0,1},{1,0},{2,3},{3,2},{4,5},{5,4},{6,7},{7,6},{8,9},{9,8},{10,11... | collective-permute-start | bytes 245768 | tf_op jit(solution)/shard_map/ppermute | solution.py:618
  2.3 5.0 %collective-permute-start = (bf16[48,512]{1,0:T(8,128)(2,1)S(1)}, bf16[48,512]{1,0:T(8,128)(2,1)S(1)}, u32[]{:S(2)}, u32[]{:S(2)}) collective-permute-start(bf16[48,512]{1,0:T(8,128)(2,1)S(1)} %get-tuple-element.28), channel_id=1, source_target_pairs={{0,2},{2,0},{1,3},{3,1},{4,6},{6,4},{5,7},{7,5},{8,10},{10,8},{9,1... | collective-permute-start | bytes 147464 | tf_op jit(solution)/shard_map/ppermute | solution.py:622
  4.8 3.7 %collective-permute-start.1 = (bf16[48,512]{1,0:T(8,128)(2,1)S(1)}, bf16[48,512]{1,0:T(8,128)(2,1)S(1)}, u32[]{:S(2)}, u32[]{:S(2)}) collective-permute-start(bf16[48,512]{1,0:T(8,128)(2,1)S(1)} %get-tuple-element.29), channel_id=1, source_target_pairs={{0,3},{1,2},{2,1},{3,0},{4,7},{5,6},{6,5},{7,4},{8,11},{9,10},{10,... | collective-permute-start | bytes 147464 | tf_op jit(solution)/shard_map/ppermute | solution.py:623
  10.7 1.2 %collective-permute-start.3 = (f32[8,128]{1,0:T(8,128)S(1)}, f32[8,128]{1,0:T(8,128)S(1)}, u32[]{:S(2)}, u32[]{:S(2)}) collective-permute-start(f32[8,128]{1,0:T(8,128)S(1)} %get-tuple-element.33), channel_id=1, source_target_pairs={{0,1},{1,0},{2,3},{3,2},{4,5},{5,4},{6,7},{7,6},{8,9},{9,8},{10,11... | collective-permute-start | bytes 12296 | tf_op jit(solution)/shard_map/ppermute | solution.py:569
  11.9 4.8 %collective-permute-start.6 = (f32[8,128]{1,0:T(8,128)S(1)}, f32[8,128]{1,0:T(8,128)S(1)}, u32[]{:S(2)}, u32[]{:S(2)}) collective-permute-start(f32[8,128]{1,0:T(8,128)S(1)} %add.9.refs_0_), channel_id=1, source_target_pairs={{0,13},{1,12},{4,9},{5,8},{8,5},{9,4},{12,1},{13,0},{2,15},{3,14},... | collective-permute-start | bytes 12296 | tf_op jit(solution)/shard_map/ppermute | solution.py:579
  15.3 3.9 %collective-permute-start.5 = (f32[8,128]{1,0:T(8,128)S(1)}, f32[8,128]{1,0:T(8,128)S(1)}, u32[]{:S(2)}, u32[]{:S(2)}) collective-permute-start(f32[8,128]{1,0:T(8,128)S(1)} %add.9.refs_0_), channel_id=1, source_target_pairs={{0,9},{1,8},{4,13},{5,12},{8,1},{9,0},{12,5},{13,4},{2,11},{3,10},... | collective-permute-start | bytes 12296 | tf_op jit(solution)/shard_map/ppermute | solution.py:579
  15.3 3.9 %collective-permute-start.4 = (f32[8,128]{1,0:T(8,128)S(1)}, f32[8,128]{1,0:T(8,128)S(1)}, u32[]{:S(2)}, u32[]{:S(2)}) collective-permute-start(f32[8,128]{1,0:T(8,128)S(1)} %add.9.refs_0_), channel_id=1, source_target_pairs={{0,5},{1,4},{4,1},{5,0},{8,13},{9,12},{12,9},{13,8},{2,7},{3,6},{6... | collective-permute-start | bytes 12296 | tf_op jit(solution)/shard_map/ppermute | solution.py:579
  22.4 1.2 %collective-permute-start.7 = (f32[8,128]{1,0:T(8,128)S(1)}, f32[8,128]{1,0:T(8,128)S(1)}, u32[]{:S(2)}, u32[]{:S(2)}) collective-permute-start(f32[8,128]{1,0:T(8,128)S(1)} %get-tuple-element.45), channel_id=1, source_target_pairs={{0,1},{1,0},{2,3},{3,2},{4,5},{5,4},{6,7},{7,6},{8,9},{9,8},{10,11... | collective-permute-start | bytes 12296 | tf_op jit(solution)/shard_map/ppermute | solution.py:569
  23.7 4.8 %collective-permute-start.10 = (f32[8,128]{1,0:T(8,128)S(1)}, f32[8,128]{1,0:T(8,128)S(1)}, u32[]{:S(2)}, u32[]{:S(2)}) collective-permute-start(f32[8,128]{1,0:T(8,128)S(1)} %add.10.refs_0_), channel_id=1, source_target_pairs={{0,13},{1,12},{4,9},{5,8},{8,5},{9,4},{12,1},{13,0},{2,15},{3,14},... | collective-permute-start | bytes 12296 | tf_op jit(solution)/shard_map/ppermute | solution.py:579
  25.1 3.9 %collective-permute-start.9 = (f32[8,128]{1,0:T(8,128)S(1)}, f32[8,128]{1,0:T(8,128)S(1)}, u32[]{:S(2)}, u32[]{:S(2)}) collective-permute-start(f32[8,128]{1,0:T(8,128)S(1)} %add.10.refs_0_), channel_id=1, source_target_pairs={{0,9},{1,8},{4,13},{5,12},{8,1},{9,0},{12,5},{13,4},{2,11},{3,10},... | collective-permute-start | bytes 12296 | tf_op jit(solution)/shard_map/ppermute | solution.py:579
  25.4 3.7 %collective-permute-start.8 = (f32[8,128]{1,0:T(8,128)S(1)}, f32[8,128]{1,0:T(8,128)S(1)}, u32[]{:S(2)}, u32[]{:S(2)}) collective-permute-start(f32[8,128]{1,0:T(8,128)S(1)} %add.10.refs_0_), channel_id=1, source_target_pairs={{0,5},{1,4},{4,1},{5,0},{8,13},{9,12},{12,9},{13,8},{2,7},{3,6},{6... | collective-permute-start | bytes 12296 | tf_op jit(solution)/shard_map/ppermute | solution.py:579
  32.3 1.2 %collective-permute-start.11 = (f32[8,128]{1,0:T(8,128)S(1)}, f32[8,128]{1,0:T(8,128)S(1)}, u32[]{:S(2)}, u32[]{:S(2)}) collective-permute-start(f32[8,128]{1,0:T(8,128)S(1)} %get-tuple-element.48), channel_id=1, source_target_pairs={{0,1},{1,0},{2,3},{3,2},{4,5},{5,4},{6,7},{7,6},{8,9},{9,8},{10,11... | collective-permute-start | bytes 12296 | tf_op jit(solution)/shard_map/ppermute | solution.py:569
  33.5 4.8 %collective-permute-start.14 = (f32[8,128]{1,0:T(8,128)S(1)}, f32[8,128]{1,0:T(8,128)S(1)}, u32[]{:S(2)}, u32[]{:S(2)}) collective-permute-start(f32[8,128]{1,0:T(8,128)S(1)} %add.11.refs_0_), channel_id=1, source_target_pairs={{0,13},{1,12},{4,9},{5,8},{8,5},{9,4},{12,1},{13,0},{2,15},{3,14},... | collective-permute-start | bytes 12296 | tf_op jit(solution)/shard_map/ppermute | solution.py:579
  35.6 4.0 %collective-permute-start.13 = (f32[8,128]{1,0:T(8,128)S(1)}, f32[8,128]{1,0:T(8,128)S(1)}, u32[]{:S(2)}, u32[]{:S(2)}) collective-permute-start(f32[8,128]{1,0:T(8,128)S(1)} %add.11.refs_0_), channel_id=1, source_target_pairs={{0,9},{1,8},{4,13},{5,12},{8,1},{9,0},{12,5},{13,4},{2,11},{3,10},... | collective-permute-start | bytes 12296 | tf_op jit(solution)/shard_map/ppermute | solution.py:579
  36.4 3.1 %collective-permute-start.12 = (f32[8,128]{1,0:T(8,128)S(1)}, f32[8,128]{1,0:T(8,128)S(1)}, u32[]{:S(2)}, u32[]{:S(2)}) collective-permute-start(f32[8,128]{1,0:T(8,128)S(1)} %add.11.refs_0_), channel_id=1, source_target_pairs={{0,5},{1,4},{4,1},{5,0},{8,13},{9,12},{12,9},{13,8},{2,7},{3,6},{6... | collective-permute-start | bytes 12296 | tf_op jit(solution)/shard_map/ppermute | solution.py:579
  41.2 1.4 %collective-permute-start.15 = (f32[2,2,16,512]{3,2,1,0:T(8,128)S(1)}, f32[2,2,16,512]{3,2,1,0:T(8,128)S(1)}, u32[]{:S(2)}, u32[]{:S(2)}) collective-permute-start(f32[2,2,16,512]{3,2,1,0:T(8,128)S(1)} %get-tuple-element.53), channel_id=1, source_target_pairs={{0,1},{1,0},{2,3},{3,2},{4,5},{5,4},{6,7},{7,6},{8,9},{9,8},{10,11... | collective-permute-start | bytes 393224 | tf_op jit(solution)/shard_map/ppermute | solution.py:707
